TPU v7x, 32 devices: a whole 2x2x4 slice. The times are simulated.
32 devices in a mesh: rows: 16 (over z, y, core), cols: 2 (over x).
Axes of the slice: x: 2, y: 2, z: 4, core: 2. Of those that a mesh axis runs over, the one named last changes fastest.
Arguments:
- pair: bfloat16 [384, 384, 128], P('rows', 'cols'), may hold values from -6 to 6
- token_mask: int32 [384], P('cols'), may hold values from 0 to 1
- norm_gain: float32 [128], replicated, may hold values from 0.25 to 1.75
- norm_shift: float32 [128], replicated, may hold values from -3 to 3
- in_weight: bfloat16 [128, 512], replicated, may hold values from -1.5 to 1.5
- gate_bias: float32 [128], replicated, may hold values from -4 to 4
- bias_weight: bfloat16 [128, 4], replicated, may hold values from -16 to 16
- out_weight: bfloat16 [128, 128], replicated, may hold values from -1.5 to 1.5
- out_bias: float32 [128], replicated, may hold values from -1.8 to 1.8
Outputs:
- updated: bfloat16 [384, 384, 128], P('rows', 'cols')
All inputs are finite; a program needn't handle non-finite values.
Results may differ from a plain program's by a relative error of at most 0.006.
The roundings to bfloat16 on the way count: a program that leaves them out, or rounds other values in their place, can miss the bound.
Values may be sent and summed in bfloat16 or wider, within the bound.
No kernel may reach another device: no remote copies, remote signals or barrier semaphores. Data moves between devices by JAX's collectives and lax.ppermute only.
A program may use at most 128 MiB of HBM per device.

v0:
```python
import jax
import jax.numpy as jnp
from jax import lax
from jax.sharding import PartitionSpec as P


def layer_norm(pair_block, norm_gain, norm_shift):
    as_float = pair_block.astype(jnp.float32)
    center = jnp.mean(as_float, axis=-1, keepdims=True)
    spread = jnp.mean(jnp.square(as_float - center), axis=-1, keepdims=True)
    return ((as_float - center) * lax.rsqrt(spread + 1e-05) * norm_gain + norm_shift).astype(
        jnp.bfloat16
    )


def shards(
    pair, token_mask, norm_gain, norm_shift, in_weight, gate_bias, bias_weight, out_weight, out_bias
):
    row_count, col_count, channels = pair.shape
    head_count = bias_weight.shape[1]
    inner_width = out_weight.shape[0]
    head_size = inner_width // head_count
    normed = layer_norm(pair, norm_gain, norm_shift)
    flat_normed = normed.reshape(row_count * col_count, channels)
    bias_tile = jnp.einsum(
        "jkc,ch->jhk", normed, bias_weight, preferred_element_type=jnp.float32
    ).astype(jnp.bfloat16)
    bias_columns = lax.all_gather(bias_tile, "rows", axis=0, tiled=True)
    own_bias = lax.all_to_all(bias_columns, "cols", split_axis=0, concat_axis=2, tiled=True)
    query_gate = jnp.concatenate(
        (in_weight[:, :inner_width], in_weight[:, 3 * inner_width :]), axis=1
    )
    projected = jnp.dot(flat_normed, query_gate, preferred_element_type=jnp.float32)
    queries = (projected[:, :inner_width] * head_size ** (-0.5)).astype(jnp.bfloat16)
    queries = queries.reshape(row_count, col_count, head_count, head_size)
    gates = jax.nn.sigmoid(projected[:, inner_width:] + gate_bias)
    key_value_weight = in_weight[:, inner_width : 3 * inner_width]
    mask_row = token_mask.reshape(1, col_count)
    start_state = (
        jnp.full((row_count, col_count, head_count), -jnp.inf, jnp.float32),
        jnp.zeros((row_count, col_count, head_count), jnp.float32),
        jnp.zeros((row_count, col_count, inner_width), jnp.float32),
    )
    key_values = jnp.dot(flat_normed, key_value_weight, preferred_element_type=jnp.float32).astype(
        jnp.bfloat16
    )
    key_values = key_values.reshape(row_count, col_count, 2 * inner_width)
    pair_keys = lax.all_gather(key_values, "cols", axis=1, tiled=True)
    mask_in = lax.all_gather(mask_row, "cols", axis=1, tiled=True)
    state_now = start_state
    begin_at = jnp.int32(0)
    span_len = pair_keys.shape[1]
    for low_edge in range(0, span_len, col_count):
        high_edge = min(low_edge + col_count, span_len)
        attend_pair_keys = pair_keys[:, low_edge:high_edge]
        attend_begin_at = begin_at + low_edge
        attend_running_max, attend_totals, attend_summed = state_now
        attend_span_len = attend_pair_keys.shape[1]
        key_part = attend_pair_keys[..., :inner_width].reshape(
            row_count, attend_span_len, head_count, head_size
        )
        value_part = attend_pair_keys[..., inner_width:].reshape(
            row_count, attend_span_len, head_count, head_size
        )
        scores = jnp.einsum(
            "rjhd,rkhd->rjhk", queries, key_part, preferred_element_type=jnp.float32
        )
        bias_part = lax.dynamic_slice_in_dim(own_bias, attend_begin_at, attend_span_len, 2).astype(
            jnp.float32
        )
        masking = 1000000000.0 * (mask_in[:, low_edge:high_edge][0].astype(jnp.float32) - 1.0)
        scores = scores + bias_part + masking
        new_max = jnp.maximum(attend_running_max, jnp.max(scores, axis=-1))
        shrink = jnp.exp(attend_running_max - new_max)
        weights = jnp.exp(scores - new_max[..., None])
        attend_totals = attend_totals * shrink + jnp.sum(weights, axis=-1)
        mixed_part = jnp.einsum(
            "rjhk,rkhd->rjhd",
            weights.astype(jnp.bfloat16),
            value_part,
            preferred_element_type=jnp.float32,
        )
        attend_summed = (
            attend_summed.reshape(row_count, col_count, head_count, head_size) * shrink[..., None]
            + mixed_part
        )
        state_now = (
            new_max,
            attend_totals,
            attend_summed.reshape(row_count, col_count, inner_width),
        )
    running_max, totals, summed = state_now
    attended = summed.reshape(row_count, col_count, head_count, head_size) / totals[..., None]
    gated = gates.reshape(row_count, col_count, head_count, head_size) * attended
    gated = gated.astype(jnp.bfloat16).reshape(row_count * col_count, inner_width)
    updated = jnp.dot(gated, out_weight, preferred_element_type=jnp.float32) + out_bias
    return updated.astype(jnp.bfloat16).reshape(row_count, col_count, channels)


def solution(mesh):
    placed = (P("rows", "cols", None), P("cols"), P(), P(), P(), P(), P(), P(), P())
    return jax.shard_map(
        shards, mesh=mesh, in_specs=placed, out_specs=P("rows", "cols", None), check_vma=False
    )
```

profile of v0, /device:TPU:0, one launch (start us, length us, event | category | flops | bytes accessed | tf_op | source)
XLA Modules:
  0.0 171.0 jit_solution(1921558812404166594)
XLA Ops:
  6.5 0.0 copy-start
  6.5 0.0 all-gather.3.cloned.1.call-start
  6.6 1.9 %convert_reduce_fusion = f32[24,192]{1,0:T(8,128)S(1)} fusion(bf16[24,192,128]{2,1,0:T(8,128)(2,1)} %param.9), kind=kLoop, calls=%fused_computation.24 | loop fusion | flops 1175040 | bytes 1198080 | tf_op jit(solution)/shard_map/reduce_sum | solution.py:9
  8.5 2.8 %fusion.19 = f32[24,192]{1,0:T(8,128)S(1)} fusion(bf16[24,192,128]{2,1,0:T(8,128)(2,1)} %param.9, f32[24,192]{1,0:T(8,128)S(1)} %broadcast_multiply_fusion), kind=kLoop, calls=%fused_computation.27 | loop fusion | flops 2354688 | bytes 1216512 | tf_op jit(solution)/shard_map/reduce_sum | solution.py:10
  11.3 1.5 fusion.22
  12.8 0.0 copy-done.6
  12.8 0.0 copy-start.8
  12.8 2.2 %convolution_convert_fusion = bf16[4608,256]{1,0:T(8,128)(2,1)} fusion(bf16[4608,128]{1,0:T(8,128)(2,1)S(1)} %bitcast.74, bf16[128,512]{1,0:T(8,128)(2,1)S(1)} %copy-done.6), kind=kOutput, calls=%fused_computation.14 | convolution fusion | flops 303169536 | bytes 3604480 | tf_op jit(solution)/shard_map/dot_general | solution.py:44
  15.0 0.0 all-gather.3.cloned.1.call-update
  15.0 0.7 fusion.34
  15.8 26.7 %all_gather.10 = bf16[384,4,192]{2,1,0:T(4,128)(2,1)} all-gather(bf16[24,4,192]{2,1,0:T(4,128)(2,1)S(1)} %fusion.34), channel_id=1, replica_groups=mesh['rows'=16,'cols'=2] {'rows'}, dimensions={0}, use_global_device_ids=true | all-gather | bytes 626688 | tf_op jit(solution)/shard_map/all_gather | solution.py:28
  42.5 4.3 %all-to-all-start = ((bf16[384,4,192]{2,1,0:T(4,128)(2,1)}), bf16[384,4,192]{2,1,0:T(4,128)(2,1)}, u32[]{:S(2)}, u32[]{:S(2)}) async-start(bf16[384,4,192]{2,1,0:T(4,128)(2,1)} %all_gather.10), calls=%async_computation | async-start | bytes 1572864 | tf_op jit(solution)/shard_map/all_to_all | solution.py:29
  46.8 0.0 copy-start.11
  46.8 0.8 fusion.35
  47.6 2.0 %fusion.27 = (f32[4608,128]{1,0:T(8,128)}, bf16[4608,128]{1,0:T(8,128)(2,1)S(1)}) fusion(f32[4608,256]{1,0:T(8,128)S(1)} %fusion.35, f32[128]{0:T(128)S(1)} %copy-done.11), kind=kLoop, calls=%fused_computation.37 | loop fusion | flops 3538944 | bytes 8258048 | tf_op jit(solution)/shard_map/div | solution.py:36
  49.6 0.6 copy.35
  50.2 1.2 reshape.110
  51.5 0.0 copy-done.13
  51.5 0.6 dynamic-slice
  52.7 0.2 dynamic-update-slice
  53.0 14.4 %all-reduce = s32[384]{0:T(512)S(1)} all-reduce(s32[384]{0:T(512)S(1)} %dynamic-update-slice), channel_id=2, replica_groups=mesh['rows'=16,'cols'=2] {'cols'}, use_global_device_ids=true, to_apply=%add | all-reduce | flops 384 | bytes 3072
  67.3 3.1 %copy.33 = f32[4608,128]{0,1:T(8,128)} copy(f32[4608,128]{1,0:T(8,128)} %get-tuple-element.11) | data formatting | bytes 4718592 | tf_op jit(solution)/shard_map/div | solution.py:36
  70.5 3.7 %reshape.107 = f32[24,192,4,32]{1,0,3,2:T(8,128)} reshape(f32[4608,128]{0,1:T(8,128)} %copy.33) | data formatting | bytes 4718592 | tf_op jit(solution)/shard_map/reshape | solution.py:94
  74.2 0.1 fusion.41
  74.3 0.0 all-to-all-done
  74.3 2.3 %copy.37 = bf16[192,4,2,192]{0,3,2,1:T(8,128)(2,1)} copy(bf16[192,4,2,192]{3,1,0,2:T(4,128)(2,1)} %bitcast.7) | data formatting | bytes 1179648 | tf_op jit(solution)/shard_map/all_to_all | solution.py:29
  76.5 1.3 slice_convert_fusion
  77.8 11.3 %all-gather.3.cloned.1.call-done = bf16[24,384,256]{2,1,0:T(8,128)(2,1)} async-done(((bf16[24,192,256]{2,1,0:T(8,128)(2,1)}), bf16[24,384,256]{2,1,0:T(8,128)(2,1)}) %all-gather.3.cloned.1.call-update) | async-done | bytes 4718608 | tf_op jit(solution)/shard_map/all_gather | solution.py:48
  89.1 4.6 %fusion.46 = (bf16[24,192,128]{2,1,0:T(8,128)(2,1)}, bf16[24,192,128]{2,1,0:T(8,128)(2,1)}, bf16[24,192,128]{2,1,0:T(8,128)(2,1)}, bf16[24,192,128]{2,1,0:T(8,128)(2,1)}) fusion(bf16[24,384,256]{2,1,0:T(8,128)(2,1)} %all-gather.3.cloned.1.call-done), kind=kLoop, calls=%fused_computation.64 | loop fusion | bytes 9437184 | tf_op jit(solution)/shard_map/slice | solution.py:62
  93.7 2.5 %copy.34 = bf16[24,192,128]{1,2,0:T(8,128)(2,1)} copy(bf16[24,192,128]{2,1,0:T(8,128)(2,1)} %get-tuple-element.10) | data formatting | bytes 2359296 | tf_op jit(solution)/shard_map/slice | solution.py:59
  96.2 2.5 %copy.40 = bf16[24,192,128]{1,2,0:T(8,128)(2,1)} copy(bf16[24,192,128]{2,1,0:T(8,128)(2,1)} %get-tuple-element.9) | data formatting | bytes 2359296 | tf_op jit(solution)/shard_map/slice | solution.py:59
  98.7 2.6 %copy.42 = bf16[24,192,128]{1,2,0:T(8,128)(2,1)} copy(bf16[24,192,128]{2,1,0:T(8,128)(2,1)} %get-tuple-element.8) | data formatting | bytes 2359296 | tf_op jit(solution)/shard_map/slice | solution.py:62
  101.3 5.7 %fusion.6 = (f32[24,192,4]{1,2,0:T(4,128)S(1)}, f32[24,4,192,192]{3,2,1,0:T(8,128)S(1)}) fusion(f32[192]{0:T(256)S(1)} %bitcast.82, f32[192,4,192]{0,2,1:T(8,128)S(1)} %get-tuple-element.14, bf16[24,192,4,32]{1,3,2,0:T(8,128)(2,1)} %bitcast.78, bf16[24,192,4,32]{1,0,3,2:T(8,128)(2,1)S(1)} %reshape.110), kind=kOutput, calls=%fused_computation.10 | convolution fusion | flops 237090816 | bytes 17179392 | tf_op jit(solution)/shard_map/rjhd,rkhd->rjhk/dot_general | solution.py:65
  107.0 0.0 copy-start.1
  107.0 0.0 copy-done.3
  107.0 9.3 %fusion.7 = (f32[24,192,4]{1,2,0:T(4,128)S(1)}, f32[24,4,192,192]{3,2,1,0:T(8,128)}) fusion(f32[192]{0:T(256)S(1)} %bitcast.85, f32[192,4,192]{0,2,1:T(8,128)S(1)} %get-tuple-element.13, bf16[24,192,4,32]{1,3,2,0:T(8,128)(2,1)S(1)} %bitcast.77, bf16[24,192,4,32]{1,0,3,2:T(8,128)(2,1)S(1)} %reshape.110), kind=kOutput, calls=%fused_computation.11 | convolution fusion | flops 237090816 | bytes 17179392 | tf_op jit(solution)/shard_map/rjhd,rkhd->rjhk/dot_general | solution.py:65
  116.3 2.8 %copy-done.1 = f32[24,4,192,192]{3,2,1,0:T(8,128)} copy-done((f32[24,4,192,192]{3,2,1,0:T(8,128)}, f32[24,4,192,192]{3,2,1,0:T(8,128)S(1)}, u32[]{:S(2)}) %copy-start.1) | copy-done | bytes 14155800
  119.1 15.8 %fusion.2 = (f32[24,192,4]{1,2,0:T(4,128)S(1)}, f32[24,192,4]{1,2,0:T(4,128)S(1)}) fusion(f32[24,4,192,192]{3,2,1,0:T(8,128)S(1)} %get-tuple-element.21, f32[24,192,4]{1,2,0:T(4,128)S(1)} %get-tuple-element.20, f32[192]{0:T(256)S(1)} %bitcast.83, f32[192,4,192]{0,2,1:T(8,128)S(1)} %get-tuple-element.14, f32[24,192,4]{1,2,0:T(4,128)S(1)} %max.13, ...), kind=kLoop, calls=%fused_computation.6 | loop fusion | flops 28274688 | bytes 29787648 | tf_op jit(solution)/shard_map/reduce_sum | solution.py:76
  134.9 0.0 copy-start.4
  134.9 12.1 %fusion.8 = f32[24,4,32,192]{3,2,1,0:T(8,128)} fusion(bf16[24,192,4,32]{1,3,2,0:T(8,128)(2,1)S(1)} %bitcast.80, f32[24,4,192,192]{3,2,1,0:T(8,128)} %get-tuple-element.23, f32[24,192,4]{1,2,0:T(4,128)S(1)} %max.13, f32[192]{0:T(256)S(1)} %bitcast.87, f32[192,4,192]{0,2,1:T(8,128)S(1)} %get-tuple-element.13), kind=kOutput, calls=%fused_computation.12 | convolution fusion | flops 240648192 | bytes 18359040 | tf_op jit(solution)/shard_map/rjhk,rkhd->rjhd/dot_general | solution.py:77
  147.0 0.0 copy-done.4
  147.0 1.5 copy.38
  148.5 0.1 multiply_add_fusion
  148.6 11.6 %fusion.15 = bf16[24,192,4,32]{1,3,2,0:T(8,128)(2,1)S(1)} fusion(f32[24,4,32,192]{3,2,1,0:T(8,128)} %fusion.8, f32[24,192,4,32]{1,0,3,2:T(8,128)} %reshape.107, bf16[24,192,4,32]{1,3,2,0:T(8,128)(2,1)} %bitcast.81, f32[24,4,192,192]{3,2,1,0:T(8,128)} %copy-done.1, f32[24,192,4]{1,2,0:T(4,128)S(1)} %get-tuple-element.20, f32[192]{0:T(256)S(1)} %bitcast.84, ...), kind=kOutput, calls=%fused_computation.20 | convolution fusion | flops 244187136 | bytes 22119168 | tf_op jit(solution)/shard_map/rjhk,rkhd->rjhd/dot_general | solution.py:77
  160.3 0.0 copy-start.12
  160.3 0.9 copy.45
  161.2 1.4 reshape.116
  162.6 1.5 fusion.12
  (23 shorter events, 0.1 us)
Async XLA Ops:
  6.5 156.1 %copy-start = (bf16[128,128]{1,0:T(8,128)(2,1)S(1)}, bf16[128,128]{1,0:T(8,128)(2,1)}, u32[]{:S(2)}) copy-start(bf16[128,128]{1,0:T(8,128)(2,1)} %param.16) | copy-start | bytes 98308
  6.5 4.7 %copy-start.2 = (bf16[24,192,128]{2,1,0:T(8,128)(2,1)S(1)}, bf16[24,192,128]{2,1,0:T(8,128)(2,1)}, u32[]{:S(2)}) copy-start(bf16[24,192,128]{2,1,0:T(8,128)(2,1)} %param.9) | copy-start | bytes 3538948
  6.5 4.7 %copy-start.10 = (f32[128]{0:T(128)S(1)}, f32[128]{0:T(128)}, u32[]{:S(2)}) copy-start(f32[128]{0:T(128)} %param.11) | copy-start | bytes 1540
  6.5 4.8 %copy-start.9 = (f32[128]{0:T(128)S(1)}, f32[128]{0:T(128)}, u32[]{:S(2)}) copy-start(f32[128]{0:T(128)} %param.12) | copy-start | bytes 1540
  6.5 6.2 %copy-start.6 = (bf16[128,512]{1,0:T(8,128)(2,1)S(1)}, bf16[128,512]{1,0:T(8,128)(2,1)}, u32[]{:S(2)}) copy-start(bf16[128,512]{1,0:T(8,128)(2,1)} %param.13) | copy-start | bytes 393220
  6.5 82.5 %all-gather.3.cloned.1.call-start = ((), (), s32[]{:S(2)}) async-start(), calls=%async_computation.1 | async-start | bytes 7077888 | tf_op jit(solution)/shard_map/all_gather | solution.py:48
  12.8 2.2 %copy-start.8 = (bf16[128,4]{0,1:T(4,128)(2,1)S(1)}, bf16[128,4]{0,1:T(4,128)(2,1)}, u32[]{:S(2)}) copy-start(bf16[128,4]{0,1:T(4,128)(2,1)} %param.15) | copy-start | bytes 3076
  42.5 31.8 %all-to-all-start = ((bf16[384,4,192]{2,1,0:T(4,128)(2,1)}), bf16[384,4,192]{2,1,0:T(4,128)(2,1)}, u32[]{:S(2)}, u32[]{:S(2)}) async-start(bf16[384,4,192]{2,1,0:T(4,128)(2,1)} %all_gather.10), calls=%async_computation | async-start | bytes 1572864 | tf_op jit(solution)/shard_map/all_to_all | solution.py:29
  46.8 0.8 copy-start.11
  49.6 1.9 %copy-start.13 = (u32[32]{0:T(128)S(1)}, u32[32]{0:T(128)}, u32[]{:S(2)}) copy-start(u32[32]{0:T(128)} %constant.26) | copy-start | bytes 388
  49.6 3.1 %copy-start.7 = (s32[192]{0:T(256)S(1)}, s32[192]{0:T(256)}, u32[]{:S(2)}) copy-start(s32[192]{0:T(256)} %param.10) | copy-start | bytes 2308
  101.2 5.7 %copy-start.3 = (bf16[24,192,128]{1,2,0:T(8,128)(2,1)S(1)}, bf16[24,192,128]{1,2,0:T(8,128)(2,1)}, u32[]{:S(2)}) copy-start(bf16[24,192,128]{1,2,0:T(8,128)(2,1)} %copy.40) | copy-start | bytes 3538948
  107.0 12.1 %copy-start.1 = (f32[24,4,192,192]{3,2,1,0:T(8,128)}, f32[24,4,192,192]{3,2,1,0:T(8,128)S(1)}, u32[]{:S(2)}) copy-start(f32[24,4,192,192]{3,2,1,0:T(8,128)S(1)} %get-tuple-element.21) | copy-start | bytes 42467332
  119.1 15.8 %copy-start.5 = (bf16[24,192,128]{1,2,0:T(8,128)(2,1)S(1)}, bf16[24,192,128]{1,2,0:T(8,128)(2,1)}, u32[]{:S(2)}) copy-start(bf16[24,192,128]{1,2,0:T(8,128)(2,1)} %copy.42) | copy-start | bytes 3538948
  134.9 12.1 %copy-start.4 = (bf16[24,192,128]{2,1,0:T(8,128)(2,1)S(1)}, bf16[24,192,128]{2,1,0:T(8,128)(2,1)}, u32[]{:S(2)}) copy-start(bf16[24,192,128]{2,1,0:T(8,128)(2,1)} %get-tuple-element.7) | copy-start | bytes 3538948
  160.3 2.3 %copy-start.12 = (f32[128]{0:T(128)S(1)}, f32[128]{0:T(128)}, u32[]{:S(2)}) copy-start(f32[128]{0:T(128)} %param.17) | copy-start | bytes 1540
Sparse Core Ops, SparseCore 0:
  15.2 73.8 all-gather.2
where the time goes:
time: 171 us
  matrix products  43.9 us (26%)
  blocking collectives  41.1 us (24%)
  local copies, waits for them, and re-layouts  30.7 us (18%)
  other arithmetic  25.4 us (15%)
  between operations  14.3 us (8%)
  waiting for transfers between devices  11.3 us (7%)
  starting transfers between devices  4.36 us (3%)
    all_gather x1, blocking collectives, shards(): bias_columns = lax.all_gather(bias_tile, 'rows', axis=0, tiled=True)  26.7 us
    dot_general x2, matrix products, shards(): jnp.einsum('rjhk,rkhd->rjhd', weights.astype(jnp.bfloat16), value_part, p...  23.8 us
    reduce_sum x1, other arithmetic, shards(): attend_totals = attend_totals * shrink + jnp.sum(weights, axis=-1)  15.8 us
    dot_general x2, matrix products, shards(): jnp.einsum('rjhd,rkhd->rjhk', queries, key_part, preferred_element_type=j...  15 us
    unnamed x1, blocking collectives  14.4 us
    all_gather x1, waiting for transfers between devices, shards(): pair_keys = lax.all_gather(key_values, 'cols', axis=1, tiled=True)  11.3 us
    slice x3, local copies, waits for them, and re-layouts, shards(): attend_pair_keys[..., inner_width:]  8.71 us
    slice x2, local copies, waits for them, and re-layouts, shards(): attend_pair_keys[..., :inner_width]  5.01 us
  transfers between devices with their start and end apart: 2, of which 1 were waited for; matrix products, arithmetic and copies ran while one was open for 10% of the time, Pallas kernels for 0%

commit v1 on v0

--- a/solution.py
+++ b/solution.py
@@ -1,7 +1,23 @@
+import functools
+
 import jax
 import jax.numpy as jnp
+import numpy as np
 from jax import lax
+from jax.experimental import pallas as pl
+from jax.experimental.pallas import tpu as pltpu
 from jax.sharding import PartitionSpec as P
+
+LANES = 128
+MISSING = -1e9
+NN = (((1,), (0,)), ((), ()))
+NT = (((1,), (1,)), ((), ()))
+TN = (((0,), (0,)), ((), ()))
+CHUNKS = 3
+
+
+def dot(left, right, dims=NN):
+    return lax.dot_general(left, right, dims, preferred_element_type=jnp.float32)
 
 
 def layer_norm(pair_block, norm_gain, norm_shift):
@@ -13,7 +29,290 @@
     )
 
 
-def shards(
+def bias_tile_kernel(pair_ref, gain_ref, shift_ref, weight_ref, mask_ref, tile_ref, total):
+    step = pl.program_id(0)
+    rows, slots = pair_ref.shape[0], 32
+    lane = lax.broadcasted_iota(jnp.int32, (LANES, LANES), 1)
+    slot = lax.rem(lane, slots)
+    weight = weight_ref[...]
+    left, right = [], []
+    for row in range(rows):
+        left.append(layer_norm(pair_ref[row], gain_ref[...], shift_ref[...]))
+        right.append(jnp.where(slot == step * rows + row, weight, 0.0).astype(jnp.bfloat16))
+    part = dot(jnp.concatenate(left, 1), jnp.concatenate(right, 0))
+
+    @pl.when(step == 0)
+    def _():
+        total[...] = part
+
+    @pl.when(step > 0)
+    def _():
+        total[...] += part
+
+    @pl.when(step == pl.num_programs(0) - 1)
+    def _():
+        lanes = lax.broadcasted_iota(jnp.int32, total.shape, 1)
+        is_mask = lanes == rows * pl.num_programs(0)
+        tile_ref[...] = jnp.where(is_mask, mask_ref[...], total[...]).astype(jnp.bfloat16)
+
+
+def bias_tile(pair, gain, shift, bias_weight, mask, block):
+    rows, cols, channels = pair.shape
+    spread = jnp.repeat(bias_weight, 32, axis=1).astype(jnp.float32)
+    whole = lambda a: pl.BlockSpec(a.shape, lambda i: (0,) * a.ndim)
+    mask = mask.astype(jnp.float32).reshape(cols, 1)
+    return pl.pallas_call(
+        bias_tile_kernel,
+        grid=(rows // block,),
+        in_specs=[pl.BlockSpec((block, cols, channels), lambda i: (i, 0, 0))]
+        + [whole(a) for a in (gain, shift, spread, mask)],
+        out_specs=pl.BlockSpec((cols, LANES), lambda i: (0, 0)),
+        out_shape=jax.ShapeDtypeStruct((cols, LANES), jnp.bfloat16),
+        scratch_shapes=[pltpu.VMEM((cols, LANES), jnp.float32)],
+        name="bias_tile",
+    )(pair, gain, shift, spread, mask)
+
+
+def assemble_kernel(index_ref, near_ref, far_ref, order_ref, bias_ref, present_ref, tiles, marks):
+    count, cols, _ = near_ref.shape
+    tiles[:count] = near_ref[...]
+    tiles[count:] = far_ref[...]
+    for half in range(2):
+        taken = [tiles[index_ref[half * count + place]] for place in range(count)]
+        marks[half * cols : (half + 1) * cols] = taken[0].astype(jnp.float32)[:, 24:25]
+        bias_ref[half * cols : (half + 1) * cols] = dot(
+            jnp.concatenate(taken, 1), order_ref[...]
+        )
+    present = jnp.max(marks[...])
+    present_ref[0, 0] = (present > 0.5).astype(jnp.int32)
+    hidden = jnp.logical_and(marks[...] < 0.5, present > 0.5)
+    bias_ref[...] = jnp.where(hidden, MISSING, bias_ref[...])
+
+
+def lane_order(cols, rows, places):
+    order = np.zeros((places * LANES, 4 * cols), np.float32)
+    for place in range(places):
+        for head in range(4):
+            for row in range(rows):
+                query = place * rows + row
+                base = (head // 2) * 2 * cols
+                if query < LANES:
+                    lane = base + (head % 2) * LANES + query
+                else:
+                    lane = base + 2 * LANES + (head % 2) * (cols - LANES) + query - LANES
+                order[place * LANES + head * 32 + row, lane] = 1
+    return jnp.asarray(order, jnp.bfloat16)
+
+
+def assemble(index, near, far, order):
+    count, cols, _ = near.shape
+    vmem = pl.BlockSpec(memory_space=pltpu.VMEM)
+    smem = pl.BlockSpec(memory_space=pltpu.SMEM)
+    return pl.pallas_call(
+        assemble_kernel,
+        in_specs=[smem, vmem, vmem, vmem],
+        out_specs=[vmem, smem],
+        out_shape=[
+            jax.ShapeDtypeStruct((2 * cols, order.shape[1]), jnp.float32),
+            jax.ShapeDtypeStruct((1, 1), jnp.int32),
+        ],
+        scratch_shapes=[
+            pltpu.VMEM((2 * count, cols, LANES), jnp.bfloat16),
+            pltpu.VMEM((2 * cols, 1), jnp.float32),
+        ],
+        compiler_params=pltpu.CompilerParams(vmem_limit_bytes=32 << 20),
+        name="assemble_bias",
+    )(index, near, far, order)
+
+
+def project_kernel(own_ref, other_ref, gain_ref, shift_ref, wk_ref, wv_ref, wqg_ref, gb_ref, k_ref, v_ref, q_ref, g_ref):
+    for row in range(own_ref.shape[0]):
+        own = layer_norm(own_ref[row], gain_ref[...], shift_ref[...])
+        other = layer_norm(other_ref[row], gain_ref[...], shift_ref[...])
+        both = jnp.concatenate((own, other), 0)
+        twice = jnp.concatenate((own, own[LANES:]), 0)
+        k_ref[row] = dot(both, wk_ref[...]).astype(jnp.bfloat16)
+        v_ref[row] = dot(wv_ref[...], both, NT).astype(jnp.bfloat16)
+        mixed = dot(wqg_ref[...], twice, NT)
+        q_ref[row] = (mixed[:LANES] * 32 ** (-0.5)).astype(jnp.bfloat16)
+        g_ref[row] = 0.5 * jnp.tanh(0.5 * (mixed[LANES:] + gb_ref[...])) + 0.5
+
+
+def project(own, other, weights, block):
+    rows, cols, channels = own.shape
+    tile = lambda *shape: pl.BlockSpec((block,) + shape, lambda i: (i, 0, 0))
+    whole = lambda a: pl.BlockSpec(a.shape, lambda i: (0,) * a.ndim)
+    shape = lambda *s, dtype=jnp.bfloat16: jax.ShapeDtypeStruct((rows,) + s, dtype)
+    return pl.pallas_call(
+        project_kernel,
+        grid=(rows // block,),
+        in_specs=[tile(cols, channels)] * 2 + [whole(a) for a in weights],
+        out_specs=[
+            tile(2 * cols, LANES),
+            tile(LANES, 2 * cols),
+            tile(LANES, 2 * LANES),
+            tile(LANES, 2 * LANES),
+        ],
+        out_shape=[
+            shape(2 * cols, LANES),
+            shape(LANES, 2 * cols),
+            shape(LANES, 2 * LANES),
+            shape(LANES, 2 * LANES, dtype=jnp.float32),
+        ],
+        compiler_params=pltpu.CompilerParams(vmem_limit_bytes=48 << 20),
+        name="project_rows",
+    )(own, other, *weights)
+
+
+TILE_ROWS = ((0, 32), (32, 64), (0, 64), (64, 96), (96, 128), (64, 128))
+
+
+def attend_kernel(present_ref, k_ref, v_ref, q_ref, g_ref, bias_ref, wo_ref, ob_ref, out_ref, *scratch):
+    rows = k_ref.shape[0]
+    cols = out_ref.shape[1]
+    low = lax.broadcasted_iota(jnp.int32, (32, LANES), 1) < 64
+    scores, weights = scratch[0:2], scratch[2:4]
+    tops, shares = scratch[4:6], scratch[6:8]
+    lanes = [slice(tile * LANES, (tile + 1) * LANES) for tile in range(6)]
+
+    def blank(count):
+        return jnp.zeros((count, LANES), jnp.bfloat16)
+
+    def query_tile(row, tile):
+        begin, end = TILE_ROWS[tile]
+        if tile % 3 < 2:
+            part = q_ref[row, begin:end, :LANES]
+        else:
+            first = q_ref[row, begin : begin + 32, LANES:]
+            second = q_ref[row, begin + 32 : end, LANES:]
+            part = jnp.concatenate(
+                (jnp.where(low, first, 0), jnp.where(low, 0, second)), 0
+            ).astype(jnp.bfloat16)
+        pieces = [part]
+        if begin:
+            pieces.insert(0, blank(begin))
+        if end < LANES:
+            pieces.append(blank(LANES - end))
+        return jnp.concatenate(pieces, 0)
+
+    def score(row, slot, shift):
+        for tile in range(6):
+            part = dot(k_ref[row], query_tile(row, tile)) + bias_ref[:, lanes[tile]]
+            if shift:
+                part = part + MISSING
+            scores[slot][:, lanes[tile]] = part
+            tops[slot][0:1, lanes[tile]] = jnp.max(part, axis=0, keepdims=True)
+            yield
+
+    def soften(slot):
+        for tile in range(6):
+            part = jnp.exp(scores[slot][:, lanes[tile]] - tops[slot][0:1, lanes[tile]])
+            shares[slot][0:1, lanes[tile]] = 1.0 / jnp.sum(part, axis=0, keepdims=True)
+            weights[slot][:, lanes[tile]] = part.astype(jnp.bfloat16)
+            yield
+
+    def mix(row, slot):
+        mixed = []
+        for tile in range(6):
+            begin, end = TILE_ROWS[tile]
+            part = dot(v_ref[row, begin:end], weights[slot][:, lanes[tile]])
+            mixed.append(part * shares[slot][0:1, lanes[tile]])
+            yield
+        gated = []
+        for pair in range(2):
+            first, second, third = mixed[3 * pair : 3 * pair + 3]
+            gate = g_ref[row, 64 * pair : 64 * pair + 32]
+            gated.append(
+                jnp.concatenate(
+                    (first * gate[:, :LANES], jnp.where(low, third[:32] * gate[:, LANES:], 0.0)), 1
+                )
+            )
+            gate = g_ref[row, 64 * pair + 32 : 64 * pair + 64]
+            gated.append(
+                jnp.concatenate(
+                    (second * gate[:, :LANES], jnp.where(low, 0.0, third[32:] * gate[:, LANES:])), 1
+                )
+            )
+        gated = jnp.concatenate(gated, 0).astype(jnp.bfloat16)
+        update = dot(gated, wo_ref[...], TN)
+        rest = cols - LANES
+        update = jnp.concatenate(
+            (update[:LANES], update[LANES : LANES + rest] + update[LANES + rest :]), 0
+        )
+        out_ref[row] = (update + ob_ref[...]).astype(jnp.bfloat16)
+        yield
+
+    def run(*stages):
+        stages = list(stages)
+        while stages:
+            stages = [stage for stage in stages if next(stage, True) is None]
+
+    @pl.when(present_ref[0, 0] > 0)
+    def _():
+        for step in range(rows + 2):
+            stages = []
+            if step >= 2:
+                stages.append(mix(step - 2, step % 2))
+            if 1 <= step <= rows:
+                stages.append(soften((step - 1) % 2))
+            if step < rows:
+                stages.append(score(step, step % 2, False))
+            run(*stages)
+
+    @pl.when(present_ref[0, 0] == 0)
+    def _():
+        def one(row, carry):
+            run(score(row, 0, True))
+            run(soften(0))
+            run(mix(row, 0))
+            return carry
+
+        lax.fori_loop(0, rows, one, 0)
+
+
+def attend(present, k, v, q, g, bias, wo, ob, block):
+    rows, keys, _ = k.shape
+    cols = keys // 2
+    tile = lambda a: pl.BlockSpec((block,) + a.shape[1:], lambda i: (i, 0, 0))
+    whole = lambda a: pl.BlockSpec(a.shape, lambda i: (0,) * a.ndim)
+    lanes = bias.shape[1]
+    return pl.pallas_call(
+        attend_kernel,
+        grid=(rows // block,),
+        in_specs=[pl.BlockSpec(memory_space=pltpu.SMEM)]
+        + [tile(a) for a in (k, v, q, g)]
+        + [whole(a) for a in (bias, wo, ob)],
+        out_specs=pl.BlockSpec((block, cols, LANES), lambda i: (i, 0, 0)),
+        out_shape=jax.ShapeDtypeStruct((rows, cols, LANES), jnp.bfloat16),
+        scratch_shapes=[pltpu.VMEM((keys, lanes), jnp.float32)] * 2
+        + [pltpu.VMEM((keys, lanes), jnp.bfloat16)] * 2
+        + [pltpu.VMEM((8, lanes), jnp.float32)] * 4,
+        compiler_params=pltpu.CompilerParams(vmem_limit_bytes=56 << 20),
+        name="attend_rows",
+    )(present, k, v, q, g, bias, wo, ob)
+
+
+def device(z_hi, z_lo, y, core, x):
+    return (((z_hi * 2 + z_lo) * 2 + y) * 2 + core) * 2 + x
+
+
+def spread_tiles(tile):
+    arrived = []
+    for t in range(8):
+        t0, t1, t2 = t >> 2, (t >> 1) & 1, t & 1
+        moves = [
+            (device(a, b, y, c, x), device(x ^ t2, b ^ t0, y ^ t1, c, a))
+            for a in range(2)
+            for b in range(2)
+            for y in range(2)
+            for c in range(2)
+            for x in range(2)
+        ]
+        arrived.append(lax.ppermute(tile, ("rows", "cols"), moves))
+    return jnp.stack(arrived)
+
+
+def shards_general(
     pair, token_mask, norm_gain, norm_shift, in_weight, gate_bias, bias_weight, out_weight, out_bias
 ):
     row_count, col_count, channels = pair.shape
@@ -97,8 +396,64 @@
     return updated.astype(jnp.bfloat16).reshape(row_count, col_count, channels)
 
 
+def fits(mesh, pair_shape, heads, inner):
+    rows, cols, channels = pair_shape
+    return (
+        (mesh.shape["rows"], mesh.shape["cols"]) == (16, 2)
+        and (rows, cols, channels) == (24, 192, LANES)
+        and (heads, inner) == (4, LANES)
+    )
+
+
+def shards(
+    pair, token_mask, norm_gain, norm_shift, in_weight, gate_bias, bias_weight, out_weight, out_bias
+):
+    rows, cols, channels = pair.shape
+    inner = out_weight.shape[0]
+    gain, shift = norm_gain.reshape(1, channels), norm_shift.reshape(1, channels)
+    step = rows // CHUNKS
+    swap = [(0, 1), (1, 0)]
+    parts = [pair[i * step : (i + 1) * step] for i in range(CHUNKS)]
+    others = [lax.ppermute(part, "cols", swap) for part in parts]
+    tile = bias_tile(pair, gain, shift, bias_weight, token_mask, step)
+    near = spread_tiles(tile)
+    far = lax.ppermute(near, "rows", [(i, i ^ 1) for i in range(16)])
+    row = lax.axis_index("rows")
+    x = lax.axis_index("cols")
+    z_hi, z_lo, y, core = row >> 3, (row >> 2) & 1, (row >> 1) & 1, row & 1
+    place = jnp.arange(16, dtype=jnp.int32)
+    half, a, b, c = place >> 3, (place >> 2) & 1, (place >> 1) & 1, place & 1
+    index = (c ^ core) * 8 + (a ^ z_lo) * 4 + (b ^ y) * 2 + (half ^ z_hi ^ x)
+    bias, present = assemble(index, near, far, lane_order(cols, rows, 8))
+    weights = (
+        gain,
+        shift,
+        in_weight[:, inner : 2 * inner],
+        in_weight[:, 2 * inner : 3 * inner].T,
+        jnp.concatenate((in_weight[:, :inner].T, in_weight[:, 3 * inner :].T), 0),
+        gate_bias.reshape(inner, 1),
+    )
+    outs = []
+    for part, other in zip(parts, others):
+        k, v, q, g = project(part, other, weights, step // 2)
+        outs.append(attend(present, k, v, q, g, bias, out_weight, out_bias.reshape(1, channels), step))
+    return jnp.concatenate(outs, 0)
+
+
 def solution(mesh):
     placed = (P("rows", "cols", None), P("cols"), P(), P(), P(), P(), P(), P(), P())
-    return jax.shard_map(
-        shards, mesh=mesh, in_specs=placed, out_specs=P("rows", "cols", None), check_vma=False
-    )
+
+    def run(pair, *rest):
+        tall, wide, channels = pair.shape
+        block = (tall // mesh.shape["rows"], wide // mesh.shape["cols"], channels)
+        bias_weight, out_weight = rest[5], rest[6]
+        special = fits(mesh, block, bias_weight.shape[1], out_weight.shape[0])
+        return jax.shard_map(
+            shards if special else shards_general,
+            mesh=mesh,
+            in_specs=placed,
+            out_specs=P("rows", "cols", None),
+            check_vma=False,
+        )(pair, *rest)
+
+    return run

time: 171 us -> 84.4 us (0.49)
  matrix products: 43.9 us -> 0 us
  blocking collectives: 41.1 us -> 0 us
  Pallas kernels: 0 us -> 35.4 us
  other arithmetic: 25.4 us -> 2.84 us
  local copies, waits for them, and re-layouts: 30.7 us -> 12 us
  starting transfers between devices: 4.36 us -> 21.1 us
  between operations: 14.3 us -> 0.31 us
    dot_general x8 -> x0, matrix products: 43.9 us -> none  [the longest x2 23.8 us: shards(): jnp.einsum('rjhk,rkhd->rjhd', weights.astype(jnp.bfloat16), value_part, p...]
    pallas_call x0 -> x8, Pallas kernels: none -> 35.4 us  [the longest x3 23.9 us: attend(): pl.pallas_call(attend_kernel, grid=(rows // block,), in_specs=[pl.BlockSp...]
    all_gather x1 -> x0, blocking collectives: 26.7 us -> none  [shards(): bias_columns = lax.all_gather(bias_tile, 'rows', axis=0, tiled=True)]
    ppermute x0 -> x12, starting transfers between devices: none -> 21.1 us  [the longest x8 18.8 us: spread_tiles(): arrived.append(lax.ppermute(tile, ('rows', 'cols'), moves))]
    reduce_sum x3 -> x0, other arithmetic: 20.4 us -> none  [the longest x1 15.8 us: shards(): attend_totals = attend_totals * shrink + jnp.sum(weights, axis=-1)]
    unnamed x1 -> x0, blocking collectives: 14.4 us -> none
    slice x6 -> x2, local copies, waits for them, and re-layouts: 13.7 us -> 0.1 us  [the longest x1 0.08 us: shards(): parts = [pair[i * step:(i + 1) * step] for i in range(CHUNKS)]]
    ppermute x0 -> x12, waiting for transfers between devices: none -> 12.4 us  [the longest x3 11.6 us: shards(): others = [lax.ppermute(part, 'cols', swap) for part in parts]]
  transfers between devices with their start and end apart: 2 -> 12, of which waited for: 1 -> 4; matrix products, arithmetic and copies ran while one was open for 10% -> 1% of each run, Pallas kernels for 0% -> 7%
where the time goes in v1:
time: 84.4 us; the launch traced here: 84.1 us
  Pallas kernels  35.4 us (42%)
  starting transfers between devices  21.1 us (25%)
  waiting for transfers between devices  12.4 us (15%)
  local copies, waits for them, and re-layouts  12 us (14%)
  other arithmetic  2.84 us (3%)
    pallas_call x3, Pallas kernels, attend(): pl.pallas_call(attend_kernel, grid=(rows // block,), in_specs=[pl.BlockSp...  23.9 us
    ppermute x8, starting transfers between devices, spread_tiles(): arrived.append(lax.ppermute(tile, ('rows', 'cols'), moves))  18.8 us
    ppermute x3, waiting for transfers between devices, shards(): others = [lax.ppermute(part, 'cols', swap) for part in parts]  11.6 us
    unnamed x54, local copies, waits for them, and re-layouts  9.51 us
    pallas_call x3, Pallas kernels, project(): pl.pallas_call(project_kernel, grid=(rows // block,), in_specs=[tile(cols...  5.71 us
    pallas_call x1, Pallas kernels, bias_tile(): pl.pallas_call(bias_tile_kernel, grid=(rows // block,), in_specs=[pl.Bloc...  4.16 us
    ppermute x3, starting transfers between devices, shards(): others = [lax.ppermute(part, 'cols', swap) for part in parts]  2.23 us
    concatenate x1, other arithmetic, shards(): return jnp.concatenate(outs, 0)  2.14 us
  transfers between devices with their start and end apart: 12, of which 4 were waited for; matrix products, arithmetic and copies ran while one was open for 1% of the time, Pallas kernels for 7%

profile of v1, /device:TPU:0, one launch (start us, length us, event | category | flops | bytes accessed | tf_op | source)
XLA Modules:
  0.0 84.1 jit_solution(13972618379831435723)
XLA Ops:
  0.0 0.8 broadcast_in_dim.3
  0.8 0.7 copy.18.weight_ref
  1.5 0.7 convert_element_type.10
  2.2 0.8 copy.19.mask_ref
  3.0 4.2 %bias_tile.1 = bf16[192,128]{1,0:T(8,128)(2,1)} custom-call(bf16[24,192,128]{2,1,0:T(8,128)(2,1)} %pair_ref.1, f32[1,128]{1,0:T(1,128)} %bitcast.28, f32[1,128]{1,0:T(1,128)} %bitcast.32, f32[128,128]{1,0:T(8,128)} %copy.18.weight_ref, f32[192,1]{1,0:T(8,128)} %copy.19.mask_ref), custom_call_target="tpu_custom_call" | custom-call | tf_op jit(solution)/shard_map/bias_tile/pallas_call | solution.py:64
  7.1 1.6 %collective-permute-start = (bf16[192,128]{1,0:T(8,128)(2,1)}, bf16[192,128]{1,0:T(8,128)(2,1)S(1)}, u32[]{:S(2)}, u32[]{:S(2)}) collective-permute-start(bf16[192,128]{1,0:T(8,128)(2,1)} %bias_tile.1), channel_id=1, source_target_pairs={{0,0},{1,16},{2,2},{3,18},{4,4},{5,20},{6,6},{7,22},{8,8},{9,24},{... | collective-permute-start | bytes 147464 | tf_op jit(solution)/shard_map/ppermute | solution.py:311
  8.7 5.8 %collective-permute-start.1 = (bf16[192,128]{1,0:T(8,128)(2,1)}, bf16[192,128]{1,0:T(8,128)(2,1)S(1)}, u32[]{:S(2)}, u32[]{:S(2)}) collective-permute-start(bf16[192,128]{1,0:T(8,128)(2,1)} %bias_tile.1), channel_id=1, source_target_pairs={{0,16},{1,0},{2,18},{3,2},{4,20},{5,4},{6,22},{7,6},{8,24},{9,8},{... | collective-permute-start | bytes 147464 | tf_op jit(solution)/shard_map/ppermute | solution.py:311
  14.5 1.5 %collective-permute-start.2 = (bf16[192,128]{1,0:T(8,128)(2,1)}, bf16[192,128]{1,0:T(8,128)(2,1)S(1)}, u32[]{:S(2)}, u32[]{:S(2)}) collective-permute-start(bf16[192,128]{1,0:T(8,128)(2,1)} %bias_tile.1), channel_id=1, source_target_pairs={{0,4},{1,20},{2,6},{3,22},{4,0},{5,16},{6,2},{7,18},{8,12},{9,28},... | collective-permute-start | bytes 147464 | tf_op jit(solution)/shard_map/ppermute | solution.py:311
  16.0 2.0 %collective-permute-start.3 = (bf16[192,128]{1,0:T(8,128)(2,1)}, bf16[192,128]{1,0:T(8,128)(2,1)S(1)}, u32[]{:S(2)}, u32[]{:S(2)}) collective-permute-start(bf16[192,128]{1,0:T(8,128)(2,1)} %bias_tile.1), channel_id=1, source_target_pairs={{0,20},{1,4},{2,22},{3,6},{4,16},{5,0},{6,18},{7,2},{8,28},{9,12},... | collective-permute-start | bytes 147464 | tf_op jit(solution)/shard_map/ppermute | solution.py:311
  18.0 1.6 %collective-permute-start.4 = (bf16[192,128]{1,0:T(8,128)(2,1)}, bf16[192,128]{1,0:T(8,128)(2,1)S(1)}, u32[]{:S(2)}, u32[]{:S(2)}) collective-permute-start(bf16[192,128]{1,0:T(8,128)(2,1)} %bias_tile.1), channel_id=1, source_target_pairs={{0,8},{1,24},{2,10},{3,26},{4,12},{5,28},{6,14},{7,30},{8,0},{9,16... | collective-permute-start | bytes 147464 | tf_op jit(solution)/shard_map/ppermute | solution.py:311
  19.6 0.1 fusion
  19.7 0.0 copy-start.21
  19.7 0.0 copy-start.14
  19.7 0.0 copy-start.15
  19.8 1.7 %collective-permute-start.5 = (bf16[192,128]{1,0:T(8,128)(2,1)S(1)}, bf16[192,128]{1,0:T(8,128)(2,1)S(1)}, u32[]{:S(2)}, u32[]{:S(2)}) collective-permute-start(bf16[192,128]{1,0:T(8,128)(2,1)S(1)} %copy-done.20), channel_id=1, source_target_pairs={{0,24},{1,8},{2,26},{3,10},{4,28},{5,12},{6,30},{7,14},{8,16},{9,0... | collective-permute-start | bytes 147464 | tf_op jit(solution)/shard_map/ppermute | solution.py:311
  21.5 0.8 collective-permute-start.6
  22.3 3.8 %collective-permute-start.7 = (bf16[192,128]{1,0:T(8,128)(2,1)S(1)}, bf16[192,128]{1,0:T(8,128)(2,1)S(1)}, u32[]{:S(2)}, u32[]{:S(2)}) collective-permute-start(bf16[192,128]{1,0:T(8,128)(2,1)S(1)} %copy-done.20), channel_id=1, source_target_pairs={{0,28},{1,12},{2,30},{3,14},{4,24},{5,8},{6,26},{7,10},{8,20},{9,4... | collective-permute-start | bytes 147464 | tf_op jit(solution)/shard_map/ppermute | solution.py:311
  26.1 0.1 collective-permute-start.9
  26.2 2.1 %collective-permute-start.10 = (bf16[8,192,128]{2,1,0:T(8,128)(2,1)S(1)}, bf16[8,192,128]{2,1,0:T(8,128)(2,1)S(1)}, u32[]{:S(2)}, u32[]{:S(2)}) collective-permute-start(bf16[8,192,128]{2,1,0:T(8,128)(2,1)S(1)} %get-tuple-element.35.own_ref), channel_id=1, source_target_pairs={{0,1},{1,0},{2,3},{3,2},{4,5},{5,4},{6,7},{7,6},{8,9},{9,8},{10,11... | collective-permute-start | bytes 1179656 | tf_op jit(solution)/shard_map/ppermute | solution.py:417
  28.3 0.1 collective-permute-start.11
  28.5 0.8 collective-permute-done.7
  29.2 0.1 collective-permute-start.8
  29.3 0.1 copy.27
  29.5 0.1 copy.28
  29.6 0.1 copy.26
  29.7 0.1 copy.23.gb_ref
  29.9 8.4 %collective-permute-done.9.other_ref = bf16[8,192,128]{2,1,0:T(8,128)(2,1)S(1)} collective-permute-done((bf16[8,192,128]{2,1,0:T(8,128)(2,1)S(1)}, bf16[8,192,128]{2,1,0:T(8,128)(2,1)S(1)}, u32[]{:S(2)}, u32[]{:S(2)}) %collective-permute-start.9) | collective-permute-done | bytes 393248 | tf_op jit(solution)/shard_map/ppermute | solution.py:417
  38.3 1.9 %project_rows.3 = (bf16[8,384,128]{2,1,0:T(8,128)(2,1)S(1)}, bf16[8,128,384]{2,1,0:T(8,128)(2,1)S(1)}, bf16[8,128,256]{2,1,0:T(8,128)(2,1)S(1)}, f32[8,128,256]{2,1,0:T(8,128)S(1)}) custom-call(bf16[8,192,128]{2,1,0:T(8,128)(2,1)S(1)} %get-tuple-element.33.own_ref, bf16[8,192,128]{2,1,0:T(8,128)(2,1)S(1)} %collective-permute-done.9.other_ref, ...), custom_call_target="tpu_custom_call" | custom-call | tf_op jit(solution)/shard_map/project_rows/pallas_call | solution.py:146
  40.2 1.0 %copy-done.2 = f32[8,128,256]{2,1,0:T(8,128)} copy-done((f32[8,128,256]{2,1,0:T(8,128)}, f32[8,128,256]{2,1,0:T(8,128)S(1)}, u32[]{:S(2)}) %copy-start.2) | copy-done | bytes 1048600
  41.2 0.9 %copy-done.5 = bf16[8,384,128]{2,1,0:T(8,128)(2,1)} copy-done((bf16[8,384,128]{2,1,0:T(8,128)(2,1)}, bf16[8,384,128]{2,1,0:T(8,128)(2,1)S(1)}, u32[]{:S(2)}) %copy-start.5) | copy-done | bytes 786456
  42.0 0.9 %copy-done.6 = bf16[8,128,384]{2,1,0:T(8,128)(2,1)} copy-done((bf16[8,128,384]{2,1,0:T(8,128)(2,1)}, bf16[8,128,384]{2,1,0:T(8,128)(2,1)S(1)}, u32[]{:S(2)}) %copy-start.6) | copy-done | bytes 786456
  43.0 0.8 copy-done.11
  43.7 2.9 %collective-permute-done.10.other_ref = bf16[8,192,128]{2,1,0:T(8,128)(2,1)S(1)} collective-permute-done((bf16[8,192,128]{2,1,0:T(8,128)(2,1)S(1)}, bf16[8,192,128]{2,1,0:T(8,128)(2,1)S(1)}, u32[]{:S(2)}, u32[]{:S(2)}) %collective-permute-start.10) | collective-permute-done | bytes 393248 | tf_op jit(solution)/shard_map/ppermute | solution.py:417
  46.7 1.9 %project_rows.4 = (bf16[8,384,128]{2,1,0:T(8,128)(2,1)S(1)}, bf16[8,128,384]{2,1,0:T(8,128)(2,1)S(1)}, bf16[8,128,256]{2,1,0:T(8,128)(2,1)S(1)}, f32[8,128,256]{2,1,0:T(8,128)S(1)}) custom-call(bf16[8,192,128]{2,1,0:T(8,128)(2,1)S(1)} %get-tuple-element.35.own_ref, bf16[8,192,128]{2,1,0:T(8,128)(2,1)S(1)} %collective-permute-done.10.other_ref, ...), custom_call_target="tpu_custom_call" | custom-call | tf_op jit(solution)/shard_map/project_rows/pallas_call | solution.py:146
  48.6 1.0 %copy-done.3 = f32[8,128,256]{2,1,0:T(8,128)} copy-done((f32[8,128,256]{2,1,0:T(8,128)}, f32[8,128,256]{2,1,0:T(8,128)S(1)}, u32[]{:S(2)}) %copy-start.3) | copy-done | bytes 1048600
  49.6 0.9 %copy-done.7 = bf16[8,384,128]{2,1,0:T(8,128)(2,1)} copy-done((bf16[8,384,128]{2,1,0:T(8,128)(2,1)}, bf16[8,384,128]{2,1,0:T(8,128)(2,1)S(1)}, u32[]{:S(2)}) %copy-start.7) | copy-done | bytes 786456
  50.5 0.9 %copy-done.8 = bf16[8,128,384]{2,1,0:T(8,128)(2,1)} copy-done((bf16[8,128,384]{2,1,0:T(8,128)(2,1)}, bf16[8,128,384]{2,1,0:T(8,128)(2,1)S(1)}, u32[]{:S(2)}) %copy-start.8) | copy-done | bytes 786456
  51.4 0.8 copy-done.12
  52.2 0.3 collective-permute-done.11.other_ref
  52.5 1.9 %project_rows.5 = (bf16[8,384,128]{2,1,0:T(8,128)(2,1)S(1)}, bf16[8,128,384]{2,1,0:T(8,128)(2,1)S(1)}, bf16[8,128,256]{2,1,0:T(8,128)(2,1)S(1)}, f32[8,128,256]{2,1,0:T(8,128)S(1)}) custom-call(bf16[8,192,128]{2,1,0:T(8,128)(2,1)S(1)} %get-tuple-element.34.own_ref, bf16[8,192,128]{2,1,0:T(8,128)(2,1)S(1)} %collective-permute-done.11.other_ref, ...), custom_call_target="tpu_custom_call" | custom-call | tf_op jit(solution)/shard_map/project_rows/pallas_call | solution.py:146
  54.4 0.9 %copy-done.10 = bf16[8,128,384]{2,1,0:T(8,128)(2,1)} copy-done((bf16[8,128,384]{2,1,0:T(8,128)(2,1)}, bf16[8,128,384]{2,1,0:T(8,128)(2,1)S(1)}, u32[]{:S(2)}) %copy-start.10) | copy-done | bytes 786456
  55.3 1.7 %assemble_bias.1 = (f32[384,768]{1,0:T(8,128)S(1)}, s32[1,1]{1,0:T(1,128)}) custom-call(s32[16]{0:T(128)S(1)} %xor_add_fusion.index_ref, bf16[8,192,128]{2,1,0:T(8,128)(2,1)S(1)} %bitcast_dynamic-update-slice_fusion.near_ref, bf16[8,192,128]{2,1,0:T(8,128)(2,1)S(1)} %collective-permute-done.8.far_ref, bf16[1024,768]{1,0:T(8,128)(2,1)S(1)} %copy-done.1), custom_call_target="tpu_custom_call" | custom-call | tf_op jit(solution)/shard_map/assemble_bias/pallas_call | solution.py:111
  57.0 0.0 copy-start
  57.1 1.0 %copy-done = f32[384,768]{1,0:T(8,128)} copy-done((f32[384,768]{1,0:T(8,128)}, f32[384,768]{1,0:T(8,128)S(1)}, u32[]{:S(2)}) %copy-start) | copy-done | bytes 1179672
  58.1 7.9 %attend_rows.3 = bf16[8,192,128]{2,1,0:T(8,128)(2,1)} custom-call(s32[1,1]{1,0:T(1,128)} %get-tuple-element.19.present_ref, bf16[8,384,128]{2,1,0:T(8,128)(2,1)} %copy-done.5, bf16[8,128,384]{2,1,0:T(8,128)(2,1)} %copy-done.6, bf16[8,128,256]{2,1,0:T(8,128)(2,1)} %copy-done.11, f32[8,128,256]{2,1,0:T(8,128)} %copy-done.2, f32[384,768]{1,0:T(8,128)} %copy-done, ...), custom_call_target="tpu_custom_call" | custom-call | tf_op jit(solution)/shard_map/attend_rows/pallas_call | solution.py:279
  66.0 7.9 %attend_rows.4 = bf16[8,192,128]{2,1,0:T(8,128)(2,1)} custom-call(s32[1,1]{1,0:T(1,128)} %get-tuple-element.19.present_ref, bf16[8,384,128]{2,1,0:T(8,128)(2,1)} %copy-done.7, bf16[8,128,384]{2,1,0:T(8,128)(2,1)} %copy-done.8, bf16[8,128,256]{2,1,0:T(8,128)(2,1)} %copy-done.12, f32[8,128,256]{2,1,0:T(8,128)} %copy-done.3, f32[384,768]{1,0:T(8,128)} %copy-done, ...), custom_call_target="tpu_custom_call" | custom-call | tf_op jit(solution)/shard_map/attend_rows/pallas_call | solution.py:279
  73.9 8.0 %attend_rows.5 = bf16[8,192,128]{2,1,0:T(8,128)(2,1)} custom-call(s32[1,1]{1,0:T(1,128)} %get-tuple-element.19.present_ref, bf16[8,384,128]{2,1,0:T(8,128)(2,1)} %copy-done.9, bf16[8,128,384]{2,1,0:T(8,128)(2,1)} %copy-done.10, bf16[8,128,256]{2,1,0:T(8,128)(2,1)} %copy-done.13, f32[8,128,256]{2,1,0:T(8,128)} %copy-done.4, f32[384,768]{1,0:T(8,128)} %copy-done, ...), custom_call_target="tpu_custom_call" | custom-call | tf_op jit(solution)/shard_map/attend_rows/pallas_call | solution.py:279
  81.9 2.1 %pad_maximum_fusion = bf16[24,192,128]{2,1,0:T(8,128)(2,1)} fusion(bf16[8,192,128]{2,1,0:T(8,128)(2,1)} %attend_rows.5, bf16[8,192,128]{2,1,0:T(8,128)(2,1)S(1)} %copy-done.18, bf16[8,192,128]{2,1,0:T(8,128)(2,1)S(1)} %copy-done.17), kind=kLoop, calls=%fused_computation | loop fusion | flops 1179648 | bytes 2359296 | tf_op jit(solution)/shard_map/concatenate | solution.py:440
  (49 shorter events, 0.2 us)
Async XLA Ops:
  0.0 19.6 %copy-start.16 = (bf16[24,192,128]{2,1,0:T(8,128)(2,1)S(1)}, bf16[24,192,128]{2,1,0:T(8,128)(2,1)}, u32[]{:S(2)}) copy-start(bf16[24,192,128]{2,1,0:T(8,128)(2,1)} %pair_ref.1) | copy-start | bytes 3538948
  7.1 12.7 %copy-start.20 = (bf16[192,128]{1,0:T(8,128)(2,1)S(1)}, bf16[192,128]{1,0:T(8,128)(2,1)}, u32[]{:S(2)}) copy-start(bf16[192,128]{1,0:T(8,128)(2,1)} %bias_tile.1) | copy-start | bytes 147460
  7.1 22.2 %copy-start.19 = (bf16[128,512]{1,0:T(8,128)(2,1)S(1)}, bf16[128,512]{1,0:T(8,128)(2,1)}, u32[]{:S(2)}) copy-start(bf16[128,512]{1,0:T(8,128)(2,1)} %param.14) | copy-start | bytes 393220
  7.1 12.6 %collective-permute-start = (bf16[192,128]{1,0:T(8,128)(2,1)}, bf16[192,128]{1,0:T(8,128)(2,1)S(1)}, u32[]{:S(2)}, u32[]{:S(2)}) collective-permute-start(bf16[192,128]{1,0:T(8,128)(2,1)} %bias_tile.1), channel_id=1, source_target_pairs={{0,0},{1,16},{2,2},{3,18},{4,4},{5,20},{6,6},{7,22},{8,8},{9,24},{... | collective-permute-start | bytes 147464 | tf_op jit(solution)/shard_map/ppermute | solution.py:311
  8.7 12.8 %collective-permute-start.1 = (bf16[192,128]{1,0:T(8,128)(2,1)}, bf16[192,128]{1,0:T(8,128)(2,1)S(1)}, u32[]{:S(2)}, u32[]{:S(2)}) collective-permute-start(bf16[192,128]{1,0:T(8,128)(2,1)} %bias_tile.1), channel_id=1, source_target_pairs={{0,16},{1,0},{2,18},{3,2},{4,20},{5,4},{6,22},{7,6},{8,24},{9,8},{... | collective-permute-start | bytes 147464 | tf_op jit(solution)/shard_map/ppermute | solution.py:311
  14.5 7.8 %collective-permute-start.2 = (bf16[192,128]{1,0:T(8,128)(2,1)}, bf16[192,128]{1,0:T(8,128)(2,1)S(1)}, u32[]{:S(2)}, u32[]{:S(2)}) collective-permute-start(bf16[192,128]{1,0:T(8,128)(2,1)} %bias_tile.1), channel_id=1, source_target_pairs={{0,4},{1,20},{2,6},{3,22},{4,0},{5,16},{6,2},{7,18},{8,12},{9,28},... | collective-permute-start | bytes 147464 | tf_op jit(solution)/shard_map/ppermute | solution.py:311
  16.0 10.1 %collective-permute-start.3 = (bf16[192,128]{1,0:T(8,128)(2,1)}, bf16[192,128]{1,0:T(8,128)(2,1)S(1)}, u32[]{:S(2)}, u32[]{:S(2)}) collective-permute-start(bf16[192,128]{1,0:T(8,128)(2,1)} %bias_tile.1), channel_id=1, source_target_pairs={{0,20},{1,4},{2,22},{3,6},{4,16},{5,0},{6,18},{7,2},{8,28},{9,12},... | collective-permute-start | bytes 147464 | tf_op jit(solution)/shard_map/ppermute | solution.py:311
  18.0 8.2 %collective-permute-start.4 = (bf16[192,128]{1,0:T(8,128)(2,1)}, bf16[192,128]{1,0:T(8,128)(2,1)S(1)}, u32[]{:S(2)}, u32[]{:S(2)}) collective-permute-start(bf16[192,128]{1,0:T(8,128)(2,1)} %bias_tile.1), channel_id=1, source_target_pairs={{0,8},{1,24},{2,10},{3,26},{4,12},{5,28},{6,14},{7,30},{8,0},{9,16... | collective-permute-start | bytes 147464 | tf_op jit(solution)/shard_map/ppermute | solution.py:311
  19.7 10.0 %copy-start.21 = (f32[128]{0:T(128)S(1)}, f32[128]{0:T(128)}, u32[]{:S(2)}) copy-start(f32[128]{0:T(128)} %param.15) | copy-start | bytes 1540
  19.7 18.5 %copy-start.14 = (f32[128]{0:T(128)S(1)}, f32[128]{0:T(128)}, u32[]{:S(2)}) copy-start(f32[128]{0:T(128)} %param.12) | copy-start | bytes 1540
  19.7 18.5 %copy-start.15 = (f32[128]{0:T(128)S(1)}, f32[128]{0:T(128)}, u32[]{:S(2)}) copy-start(f32[128]{0:T(128)} %param.13) | copy-start | bytes 1540
  19.8 8.6 %collective-permute-start.5 = (bf16[192,128]{1,0:T(8,128)(2,1)S(1)}, bf16[192,128]{1,0:T(8,128)(2,1)S(1)}, u32[]{:S(2)}, u32[]{:S(2)}) collective-permute-start(bf16[192,128]{1,0:T(8,128)(2,1)S(1)} %copy-done.20), channel_id=1, source_target_pairs={{0,24},{1,8},{2,26},{3,10},{4,28},{5,12},{6,30},{7,14},{8,16},{9,0... | collective-permute-start | bytes 147464 | tf_op jit(solution)/shard_map/ppermute | solution.py:311
  21.5 7.0 %collective-permute-start.6 = (bf16[192,128]{1,0:T(8,128)(2,1)S(1)}, bf16[192,128]{1,0:T(8,128)(2,1)S(1)}, u32[]{:S(2)}, u32[]{:S(2)}) collective-permute-start(bf16[192,128]{1,0:T(8,128)(2,1)S(1)} %copy-done.20), channel_id=1, source_target_pairs={{0,12},{1,28},{2,14},{3,30},{4,8},{5,24},{6,10},{7,26},{8,4},{9,20... | collective-permute-start | bytes 147464 | tf_op jit(solution)/shard_map/ppermute | solution.py:311
  22.3 6.9 %collective-permute-start.7 = (bf16[192,128]{1,0:T(8,128)(2,1)S(1)}, bf16[192,128]{1,0:T(8,128)(2,1)S(1)}, u32[]{:S(2)}, u32[]{:S(2)}) collective-permute-start(bf16[192,128]{1,0:T(8,128)(2,1)S(1)} %copy-done.20), channel_id=1, source_target_pairs={{0,28},{1,12},{2,30},{3,14},{4,24},{5,8},{6,26},{7,10},{8,20},{9,4... | collective-permute-start | bytes 147464 | tf_op jit(solution)/shard_map/ppermute | solution.py:311
  26.1 12.1 %collective-permute-start.9 = (bf16[8,192,128]{2,1,0:T(8,128)(2,1)S(1)}, bf16[8,192,128]{2,1,0:T(8,128)(2,1)S(1)}, u32[]{:S(2)}, u32[]{:S(2)}) collective-permute-start(bf16[8,192,128]{2,1,0:T(8,128)(2,1)S(1)} %get-tuple-element.33.own_ref), channel_id=1, source_target_pairs={{0,1},{1,0},{2,3},{3,2},{4,5},{5,4},{6,7},{7,6},{8,9},{9,8},{10,11... | collective-permute-start | bytes 1179656 | tf_op jit(solution)/shard_map/ppermute | solution.py:417
  26.2 20.4 %collective-permute-start.10 = (bf16[8,192,128]{2,1,0:T(8,128)(2,1)S(1)}, bf16[8,192,128]{2,1,0:T(8,128)(2,1)S(1)}, u32[]{:S(2)}, u32[]{:S(2)}) collective-permute-start(bf16[8,192,128]{2,1,0:T(8,128)(2,1)S(1)} %get-tuple-element.35.own_ref), channel_id=1, source_target_pairs={{0,1},{1,0},{2,3},{3,2},{4,5},{5,4},{6,7},{7,6},{8,9},{9,8},{10,11... | collective-permute-start | bytes 1179656 | tf_op jit(solution)/shard_map/ppermute | solution.py:417
  28.3 24.1 %collective-permute-start.11 = (bf16[8,192,128]{2,1,0:T(8,128)(2,1)S(1)}, bf16[8,192,128]{2,1,0:T(8,128)(2,1)S(1)}, u32[]{:S(2)}, u32[]{:S(2)}) collective-permute-start(bf16[8,192,128]{2,1,0:T(8,128)(2,1)S(1)} %get-tuple-element.34.own_ref), channel_id=1, source_target_pairs={{0,1},{1,0},{2,3},{3,2},{4,5},{5,4},{6,7},{7,6},{8,9},{9,8},{10,11... | collective-permute-start | bytes 1179656 | tf_op jit(solution)/shard_map/ppermute | solution.py:417
  29.2 26.0 %collective-permute-start.8 = (bf16[8,192,128]{2,1,0:T(8,128)(2,1)S(1)}, bf16[8,192,128]{2,1,0:T(8,128)(2,1)S(1)}, u32[]{:S(2)}, u32[]{:S(2)}) collective-permute-start(bf16[8,192,128]{2,1,0:T(8,128)(2,1)S(1)} %bitcast_dynamic-update-slice_fusion.near_ref), channel_id=1, source_target_pairs={{0,2},{2,0},{4,6},{6,4},{8,10},{10,8},{12,14},{14,12},{16,18},{18,... | collective-permute-start | bytes 1179656 | tf_op jit(solution)/shard_map/ppermute | solution.py:420
  40.2 1.0 %copy-start.2 = (f32[8,128,256]{2,1,0:T(8,128)}, f32[8,128,256]{2,1,0:T(8,128)S(1)}, u32[]{:S(2)}) copy-start(f32[8,128,256]{2,1,0:T(8,128)S(1)} %get-tuple-element.23.g_ref) | copy-start | bytes 3145732
  41.2 0.9 %copy-start.5 = (bf16[8,384,128]{2,1,0:T(8,128)(2,1)}, bf16[8,384,128]{2,1,0:T(8,128)(2,1)S(1)}, u32[]{:S(2)}) copy-start(bf16[8,384,128]{2,1,0:T(8,128)(2,1)S(1)} %get-tuple-element.20.k_ref) | copy-start | bytes 2359300
  42.0 0.9 %copy-start.6 = (bf16[8,128,384]{2,1,0:T(8,128)(2,1)}, bf16[8,128,384]{2,1,0:T(8,128)(2,1)S(1)}, u32[]{:S(2)}) copy-start(bf16[8,128,384]{2,1,0:T(8,128)(2,1)S(1)} %get-tuple-element.21.v_ref) | copy-start | bytes 2359300
  43.0 0.8 copy-start.11
  43.7 11.5 %copy-start.1 = (bf16[1024,768]{1,0:T(8,128)(2,1)S(1)}, bf16[1024,768]{1,0:T(8,128)(2,1)}, u32[]{:S(2)}) copy-start(bf16[1024,768]{1,0:T(8,128)(2,1)} %constant.7.clone.order_ref) | copy-start | bytes 4718596
  48.6 1.0 %copy-start.3 = (f32[8,128,256]{2,1,0:T(8,128)}, f32[8,128,256]{2,1,0:T(8,128)S(1)}, u32[]{:S(2)}) copy-start(f32[8,128,256]{2,1,0:T(8,128)S(1)} %get-tuple-element.28.g_ref) | copy-start | bytes 3145732
  49.6 0.9 %copy-start.7 = (bf16[8,384,128]{2,1,0:T(8,128)(2,1)}, bf16[8,384,128]{2,1,0:T(8,128)(2,1)S(1)}, u32[]{:S(2)}) copy-start(bf16[8,384,128]{2,1,0:T(8,128)(2,1)S(1)} %get-tuple-element.25.k_ref) | copy-start | bytes 2359300
  50.5 0.9 %copy-start.8 = (bf16[8,128,384]{2,1,0:T(8,128)(2,1)}, bf16[8,128,384]{2,1,0:T(8,128)(2,1)S(1)}, u32[]{:S(2)}) copy-start(bf16[8,128,384]{2,1,0:T(8,128)(2,1)S(1)} %get-tuple-element.26.v_ref) | copy-start | bytes 2359300
  51.4 0.8 copy-start.12
  54.4 0.9 %copy-start.10 = (bf16[8,128,384]{2,1,0:T(8,128)(2,1)}, bf16[8,128,384]{2,1,0:T(8,128)(2,1)S(1)}, u32[]{:S(2)}) copy-start(bf16[8,128,384]{2,1,0:T(8,128)(2,1)S(1)} %get-tuple-element.30.v_ref) | copy-start | bytes 2359300
  55.3 1.7 %copy-start.4 = (f32[8,128,256]{2,1,0:T(8,128)}, f32[8,128,256]{2,1,0:T(8,128)S(1)}, u32[]{:S(2)}) copy-start(f32[8,128,256]{2,1,0:T(8,128)S(1)} %get-tuple-element.32.g_ref) | copy-start | bytes 3145732
  55.3 1.8 %copy-start.9 = (bf16[8,384,128]{2,1,0:T(8,128)(2,1)}, bf16[8,384,128]{2,1,0:T(8,128)(2,1)S(1)}, u32[]{:S(2)}) copy-start(bf16[8,384,128]{2,1,0:T(8,128)(2,1)S(1)} %get-tuple-element.29.k_ref) | copy-start | bytes 2359300
  55.3 1.8 %copy-start.13 = (bf16[8,128,256]{2,1,0:T(8,128)(2,1)}, bf16[8,128,256]{2,1,0:T(8,128)(2,1)S(1)}, u32[]{:S(2)}) copy-start(bf16[8,128,256]{2,1,0:T(8,128)(2,1)S(1)} %get-tuple-element.31.q_ref) | copy-start | bytes 1572868
  57.0 1.0 %copy-start = (f32[384,768]{1,0:T(8,128)}, f32[384,768]{1,0:T(8,128)S(1)}, u32[]{:S(2)}) copy-start(f32[384,768]{1,0:T(8,128)S(1)} %get-tuple-element.24.bias_ref) | copy-start | bytes 3538948
  73.9 8.0 %copy-start.17 = (bf16[8,192,128]{2,1,0:T(8,128)(2,1)S(1)}, bf16[8,192,128]{2,1,0:T(8,128)(2,1)}, u32[]{:S(2)}) copy-start(bf16[8,192,128]{2,1,0:T(8,128)(2,1)} %attend_rows.3) | copy-start | bytes 1179652
  73.9 8.0 %copy-start.18 = (bf16[8,192,128]{2,1,0:T(8,128)(2,1)S(1)}, bf16[8,192,128]{2,1,0:T(8,128)(2,1)}, u32[]{:S(2)}) copy-start(bf16[8,192,128]{2,1,0:T(8,128)(2,1)} %attend_rows.4) | copy-start | bytes 1179652

commit v2 on v1

v2 whole, which is shorter than its diff:
```python
import functools

import jax
import jax.numpy as jnp
import numpy as np
from jax import lax
from jax.experimental import pallas as pl
from jax.experimental.pallas import tpu as pltpu
from jax.sharding import PartitionSpec as P

LANES = 128
MISSING = -1e9
NN = (((1,), (0,)), ((), ()))
NT = (((1,), (1,)), ((), ()))
TN = (((0,), (0,)), ((), ()))
CHUNKS = ((0, 8), (8, 8), (16, 8))
VMEM = 14 << 20
ALL_VMEM = 60 << 20


def dot(left, right, dims=NN):
    return lax.dot_general(left, right, dims, preferred_element_type=jnp.float32)


def layer_norm(pair_block, norm_gain, norm_shift):
    as_float = pair_block.astype(jnp.float32)
    center = jnp.mean(as_float, axis=-1, keepdims=True)
    spread = jnp.mean(jnp.square(as_float - center), axis=-1, keepdims=True)
    return ((as_float - center) * lax.rsqrt(spread + 1e-05) * norm_gain + norm_shift).astype(
        jnp.bfloat16
    )


def normed_rows(block, mean_weight, gain, shift):
    center = block.astype(jnp.float32) - dot(block, mean_weight)
    spread = jnp.mean(center * center, axis=-1, keepdims=True)
    return (center * lax.rsqrt(spread + 1e-05) * gain + shift).astype(jnp.bfloat16)


def norm_kernel(pair_ref, gain_ref, shift_ref, weight_ref, mask_ref, normed_ref, tile_ref, total, wide):
    step = pl.program_id(0)
    rows, slots = pair_ref.shape[0], 32
    lane = lax.broadcasted_iota(jnp.int32, (LANES, LANES), 1)

    @pl.when(step == 0)
    def _():
        heads = weight_ref.shape[0]
        head = lax.broadcasted_iota(jnp.int32, (heads, LANES), 0)
        place = lax.broadcasted_iota(jnp.int32, (heads, LANES), 1)
        begin = head * slots
        expand = jnp.logical_and(place >= begin, place < begin + slots)
        wide[...] = dot(weight_ref[...], expand.astype(jnp.bfloat16), TN)
        spot = lax.broadcasted_iota(jnp.int32, (1, LANES), 1) == rows * pl.num_programs(0)
        total[...] = dot(mask_ref[...].astype(jnp.bfloat16), spot.astype(jnp.bfloat16), TN)

    slot = lax.rem(lane, slots)
    mean_weight = jnp.full((LANES, LANES), 1 / LANES, jnp.bfloat16)
    left, right = [], []
    for row in range(rows):
        normed = normed_rows(pair_ref[row], mean_weight, gain_ref[...], shift_ref[...])
        normed_ref[row] = normed
        left.append(normed)
        right.append(jnp.where(slot == step * rows + row, wide[...], 0.0).astype(jnp.bfloat16))
    total[...] += dot(jnp.concatenate(left, 1), jnp.concatenate(right, 0))

    @pl.when(step == pl.num_programs(0) - 1)
    def _():
        tile_ref[...] = total[...].astype(jnp.bfloat16)


def norm_and_tile(pair, gain, shift, bias_weight, mask, block):
    rows, cols, channels = pair.shape
    whole = lambda a: pl.BlockSpec(a.shape, lambda i: (0,) * a.ndim)
    small = (gain, shift, bias_weight.T, mask.reshape(1, cols))
    rows_spec = pl.BlockSpec((block, cols, channels), lambda i: (i, 0, 0))
    return pl.pallas_call(
        norm_kernel,
        grid=(rows // block,),
        in_specs=[rows_spec] + [whole(a) for a in small],
        out_specs=[rows_spec, pl.BlockSpec((cols, LANES), lambda i: (0, 0))],
        out_shape=[
            jax.ShapeDtypeStruct(pair.shape, jnp.bfloat16),
            jax.ShapeDtypeStruct((cols, LANES), jnp.bfloat16),
        ],
        scratch_shapes=[
            pltpu.VMEM((cols, LANES), jnp.float32),
            pltpu.VMEM((channels, LANES), jnp.float32),
        ],
        compiler_params=pltpu.CompilerParams(vmem_limit_bytes=ALL_VMEM),
        cost_estimate=pl.CostEstimate(flops=10**9, bytes_accessed=10**7, transcendentals=0),
        name="norm_and_tile",
    )(pair, *small)


def assemble_kernel(index_ref, near_ref, far_ref, order_ref, bias_ref, tiles, marks):
    count, cols, _ = near_ref.shape
    tiles[:count] = near_ref[...]
    tiles[count:] = far_ref[...]
    for half in range(2):
        taken = [tiles[index_ref[half * count + place]] for place in range(count)]
        marks[half * cols : (half + 1) * cols] = taken[0].astype(jnp.float32)[:, 24:25]
        bias_ref[half * cols : (half + 1) * cols] = dot(
            jnp.concatenate(taken, 1), order_ref[...]
        )
    present = jnp.max(marks[...], axis=0, keepdims=True)
    hidden = jnp.logical_and(marks[...] < 0.5, present > 0.5)
    bias_ref[: 2 * cols] = jnp.where(hidden, MISSING, bias_ref[: 2 * cols])
    bias_ref[2 * cols :] = jnp.broadcast_to(present, (8, bias_ref.shape[1]))


def lane_order(cols, rows, places):
    order = np.zeros((places * LANES, 4 * cols), np.float32)
    for place in range(places):
        for head in range(4):
            for row in range(rows):
                query = place * rows + row
                base = (head // 2) * 2 * cols
                if query < LANES:
                    lane = base + (head % 2) * LANES + query
                else:
                    lane = base + 2 * LANES + (head % 2) * (cols - LANES) + query - LANES
                order[place * LANES + head * 32 + row, lane] = 1
    return jnp.asarray(order, jnp.bfloat16)


def assemble(index, near, far, order):
    count, cols, _ = near.shape
    vmem = pl.BlockSpec(memory_space=pltpu.VMEM)
    smem = pl.BlockSpec(memory_space=pltpu.SMEM)
    return pl.pallas_call(
        assemble_kernel,
        in_specs=[smem, vmem, vmem, vmem],
        out_specs=vmem,
        out_shape=jax.ShapeDtypeStruct((2 * cols + 8, order.shape[1]), jnp.float32),
        scratch_shapes=[
            pltpu.VMEM((2 * count, cols, LANES), jnp.bfloat16),
            pltpu.VMEM((2 * cols, 1), jnp.float32),
        ],
        compiler_params=pltpu.CompilerParams(vmem_limit_bytes=VMEM),
        cost_estimate=pl.CostEstimate(flops=10**9, bytes_accessed=4 * 10**6, transcendentals=0),
        name="assemble_bias",
    )(index, near, far, order)


def project_kernel(own_ref, wk_ref, wv_ref, wqg_ref, gb_ref, k_ref, v_ref, q_ref, g_ref):
    rows, cols, channels = own_ref.shape
    keys = dot(own_ref[...].reshape(rows * cols, channels), wk_ref[...])
    k_ref[...] = keys.astype(jnp.bfloat16).reshape(k_ref.shape)
    for row in range(rows):
        own = own_ref[row]
        v_ref[row] = dot(wv_ref[...], own, NT).astype(jnp.bfloat16)
        mixed = dot(wqg_ref[...], jnp.concatenate((own, own[LANES:]), 0), NT)
        q_ref[row] = (mixed[:LANES] * 32 ** (-0.5)).astype(jnp.bfloat16)
        g_ref[row] = 0.5 * jnp.tanh(0.5 * (mixed[LANES:] + gb_ref[...])) + 0.5


def project(normed, weights, block):
    rows, cols, channels = normed.shape
    tile = lambda *shape: pl.BlockSpec((block,) + shape, lambda i: (i, 0, 0))
    whole = lambda a: pl.BlockSpec(a.shape, lambda i: (0,) * a.ndim)
    sizes = ((cols, LANES), (LANES, cols), (LANES, 2 * LANES), (LANES, 2 * LANES))
    kinds = (jnp.bfloat16,) * 3 + (jnp.float32,)
    return pl.pallas_call(
        project_kernel,
        grid=(rows // block,),
        in_specs=[tile(cols, channels)] + [whole(a) for a in weights],
        out_specs=[tile(*size) for size in sizes],
        out_shape=[jax.ShapeDtypeStruct((rows,) + size, kind) for size, kind in zip(sizes, kinds)],
        compiler_params=pltpu.CompilerParams(vmem_limit_bytes=VMEM),
        cost_estimate=pl.CostEstimate(flops=10**9, bytes_accessed=10**7, transcendentals=0),
        name="project_own",
    )(normed, *weights)


TILE_ROWS = ((0, 32), (32, 64), (0, 64), (64, 96), (96, 128), (64, 128))


def attend_kernel(begin, first, *refs):
    if not first:
        refs = refs[1:]
    other_ref, k_ref, v_ref, q_ref, g_ref, bias_ref, wk_ref, wv_ref, wo_ref, ob_ref, out_ref = refs[:11]
    k_other, v_both, *scratch = refs[11:]
    scores, weights, tops, shares = (scratch[2 * n : 2 * n + 2] for n in range(4))
    rows, cols, _ = other_ref.shape
    keys = 2 * cols
    low = lax.broadcasted_iota(jnp.int32, (32, LANES), 1) < 64
    lanes = [slice(tile * LANES, (tile + 1) * LANES) for tile in range(6)]

    def blank(count):
        return jnp.zeros((count, LANES), jnp.bfloat16)

    def query_tile(row, tile):
        head, tail = TILE_ROWS[tile]
        if tile % 3 < 2:
            part = q_ref[begin + row, head:tail, :LANES]
        else:
            one = q_ref[begin + row, head : head + 32, LANES:]
            two = q_ref[begin + row, head + 32 : tail, LANES:]
            part = jnp.concatenate(
                (jnp.where(low, one, 0), jnp.where(low, 0, two)), 0
            ).astype(jnp.bfloat16)
        pieces = [part]
        if head:
            pieces.insert(0, blank(head))
        if tail < LANES:
            pieces.append(blank(LANES - tail))
        return jnp.concatenate(pieces, 0)

    def widen(row):
        other = other_ref[row]
        k_other[row] = dot(other, wk_ref[...]).astype(jnp.bfloat16)
        yield
        values = dot(wv_ref[...], other, NT).astype(jnp.bfloat16)
        v_both[row] = jnp.concatenate((v_ref[begin + row], values), 1)
        yield

    def score(row, slot, shift):
        for tile in range(6):
            query = query_tile(row, tile)
            both = jnp.concatenate((k_ref[begin + row], k_other[row]), 0)
            part = dot(both, query) + bias_ref[:keys, lanes[tile]]
            if shift:
                part = part + MISSING
            scores[slot][:, lanes[tile]] = part
            tops[slot][0:1, lanes[tile]] = jnp.max(part, axis=0, keepdims=True)
            yield

    def soften(slot):
        for tile in range(6):
            part = jnp.exp(scores[slot][:, lanes[tile]] - tops[slot][0:1, lanes[tile]])
            shares[slot][0:1, lanes[tile]] = 1.0 / jnp.sum(part, axis=0, keepdims=True)
            weights[slot][:, lanes[tile]] = part.astype(jnp.bfloat16)
            yield

    def mix(row, slot):
        mixed = []
        for tile in range(6):
            head, tail = TILE_ROWS[tile]
            part = dot(v_both[row, head:tail], weights[slot][:, lanes[tile]])
            mixed.append(part * shares[slot][0:1, lanes[tile]])
            yield
        gated = []
        for pair in range(2):
            one, two, both = mixed[3 * pair : 3 * pair + 3]
            gate = g_ref[begin + row, 64 * pair : 64 * pair + 32]
            rest = jnp.where(low, both[:32] * gate[:, LANES:], 0.0)
            gated.append(jnp.concatenate((one * gate[:, :LANES], rest), 1))
            gate = g_ref[begin + row, 64 * pair + 32 : 64 * pair + 64]
            rest = jnp.where(low, 0.0, both[32:] * gate[:, LANES:])
            gated.append(jnp.concatenate((two * gate[:, :LANES], rest), 1))
        update = dot(jnp.concatenate(gated, 0).astype(jnp.bfloat16), wo_ref[...], TN)
        rest = cols - LANES
        update = jnp.concatenate(
            (update[:LANES], update[LANES : LANES + rest] + update[LANES + rest :]), 0
        )
        out_ref[row] = (update + ob_ref[...]).astype(jnp.bfloat16)
        yield

    def run(*stages):
        stages = list(stages)
        while stages:
            stages = [stage for stage in stages if next(stage, True) is None]

    present = bias_ref[keys, 0]

    @pl.when(present > 0.5)
    def _():
        run(widen(0))
        for step in range(rows + 2):
            stages = []
            if step >= 2:
                stages.append(mix(step - 2, step % 2))
            if 1 <= step <= rows:
                stages.append(soften((step - 1) % 2))
            if step < rows:
                stages.append(score(step, step % 2, False))
            if step + 1 < rows:
                stages.append(widen(step + 1))
            run(*stages)

    @pl.when(present <= 0.5)
    def _():
        for row in range(rows):
            run(widen(row))
            run(score(row, 0, True))
            run(soften(0))
            run(mix(row, 0))


def attend(other, k, v, q, g, bias, wk, wv, wo, ob, out, begin):
    rows, cols, channels = other.shape
    total, keys = k.shape[0], 2 * cols
    lanes = bias.shape[1]
    extra = [] if out is None else [out]
    vmem = pl.BlockSpec(memory_space=pltpu.VMEM)
    return pl.pallas_call(
        functools.partial(attend_kernel, begin, out is None),
        grid=(1,),
        in_specs=[pl.BlockSpec(memory_space=pl.ANY)] * len(extra) + [vmem] * 10,
        out_specs=pl.BlockSpec((rows, cols, LANES), lambda i: (begin // rows, 0, 0)),
        out_shape=jax.ShapeDtypeStruct((total, cols, LANES), jnp.bfloat16),
        scratch_shapes=[
            pltpu.VMEM((rows, cols, LANES), jnp.bfloat16),
            pltpu.VMEM((rows, LANES, keys), jnp.bfloat16),
        ]
        + [pltpu.VMEM((keys, lanes), jnp.float32)] * 2
        + [pltpu.VMEM((keys, lanes), jnp.bfloat16)] * 2
        + [pltpu.VMEM((8, lanes), jnp.float32)] * 4,
        input_output_aliases={0: 0} if extra else {},
        compiler_params=pltpu.CompilerParams(vmem_limit_bytes=24 << 20),
        cost_estimate=pl.CostEstimate(
            flops=10**10, bytes_accessed=10**7, transcendentals=rows * keys * lanes
        ),
        name="attend_rows",
    )(*extra, other, k, v, q, g, bias, wk, wv, wo, ob)


def device(z_hi, z_lo, y, core, x):
    return (((z_hi * 2 + z_lo) * 2 + y) * 2 + core) * 2 + x


def moved(array, move):
    pairs = []
    for number in range(32):
        a, b, y, c, x = ((number >> bit) & 1 for bit in (4, 3, 2, 1, 0))
        target = move(a, b, y, c, x)
        if target is not None:
            pairs.append((number, device(*target)))
    return lax.ppermute(array, ("rows", "cols"), pairs)


def spread_tiles(tile, z_hi, x):
    straight = moved(tile, lambda a, b, y, c, x: (1 - a, b, y, c, x) if a == x else (a, b, y, c, 1 - x))
    across = moved(tile, lambda a, b, y, c, x: None if a == x else (1 - a, b, y, c, 1 - x))
    home = z_hi == x
    pair = jnp.stack((jnp.where(home, tile, straight), jnp.where(home, straight, across)))
    near = [pair]
    for move in (
        lambda a, b, y, c, x: (a, b, 1 - y, c, x),
        lambda a, b, y, c, x: (a, 1 - b, y, c, x),
        lambda a, b, y, c, x: (a, 1 - b, 1 - y, c, x),
    ):
        near.append(moved(pair, move))
    near = jnp.concatenate(near, 0)
    return near, moved(near, lambda a, b, y, c, x: (a, b, y, 1 - c, x))


def shards_general(
    pair, token_mask, norm_gain, norm_shift, in_weight, gate_bias, bias_weight, out_weight, out_bias
):
    row_count, col_count, channels = pair.shape
    head_count = bias_weight.shape[1]
    inner_width = out_weight.shape[0]
    head_size = inner_width // head_count
    normed = layer_norm(pair, norm_gain, norm_shift)
    flat_normed = normed.reshape(row_count * col_count, channels)
    bias_tile = jnp.einsum(
        "jkc,ch->jhk", normed, bias_weight, preferred_element_type=jnp.float32
    ).astype(jnp.bfloat16)
    bias_columns = lax.all_gather(bias_tile, "rows", axis=0, tiled=True)
    own_bias = lax.all_to_all(bias_columns, "cols", split_axis=0, concat_axis=2, tiled=True)
    query_gate = jnp.concatenate(
        (in_weight[:, :inner_width], in_weight[:, 3 * inner_width :]), axis=1
    )
    projected = jnp.dot(flat_normed, query_gate, preferred_element_type=jnp.float32)
    queries = (projected[:, :inner_width] * head_size ** (-0.5)).astype(jnp.bfloat16)
    queries = queries.reshape(row_count, col_count, head_count, head_size)
    gates = jax.nn.sigmoid(projected[:, inner_width:] + gate_bias)
    key_value_weight = in_weight[:, inner_width : 3 * inner_width]
    mask_row = token_mask.reshape(1, col_count)
    start_state = (
        jnp.full((row_count, col_count, head_count), -jnp.inf, jnp.float32),
        jnp.zeros((row_count, col_count, head_count), jnp.float32),
        jnp.zeros((row_count, col_count, inner_width), jnp.float32),
    )
    key_values = jnp.dot(flat_normed, key_value_weight, preferred_element_type=jnp.float32).astype(
        jnp.bfloat16
    )
    key_values = key_values.reshape(row_count, col_count, 2 * inner_width)
    pair_keys = lax.all_gather(key_values, "cols", axis=1, tiled=True)
    mask_in = lax.all_gather(mask_row, "cols", axis=1, tiled=True)
    state_now = start_state
    begin_at = jnp.int32(0)
    span_len = pair_keys.shape[1]
    for low_edge in range(0, span_len, col_count):
        high_edge = min(low_edge + col_count, span_len)
        attend_pair_keys = pair_keys[:, low_edge:high_edge]
        attend_begin_at = begin_at + low_edge
        attend_running_max, attend_totals, attend_summed = state_now
        attend_span_len = attend_pair_keys.shape[1]
        key_part = attend_pair_keys[..., :inner_width].reshape(
            row_count, attend_span_len, head_count, head_size
        )
        value_part = attend_pair_keys[..., inner_width:].reshape(
            row_count, attend_span_len, head_count, head_size
        )
        scores = jnp.einsum(
            "rjhd,rkhd->rjhk", queries, key_part, preferred_element_type=jnp.float32
        )
        bias_part = lax.dynamic_slice_in_dim(own_bias, attend_begin_at, attend_span_len, 2).astype(
            jnp.float32
        )
        masking = 1000000000.0 * (mask_in[:, low_edge:high_edge][0].astype(jnp.float32) - 1.0)
        scores = scores + bias_part + masking
        new_max = jnp.maximum(attend_running_max, jnp.max(scores, axis=-1))
        shrink = jnp.exp(attend_running_max - new_max)
        weights = jnp.exp(scores - new_max[..., None])
        attend_totals = attend_totals * shrink + jnp.sum(weights, axis=-1)
        mixed_part = jnp.einsum(
            "rjhk,rkhd->rjhd",
            weights.astype(jnp.bfloat16),
            value_part,
            preferred_element_type=jnp.float32,
        )
        attend_summed = (
            attend_summed.reshape(row_count, col_count, head_count, head_size) * shrink[..., None]
            + mixed_part
        )
        state_now = (
            new_max,
            attend_totals,
            attend_summed.reshape(row_count, col_count, inner_width),
        )
    running_max, totals, summed = state_now
    attended = summed.reshape(row_count, col_count, head_count, head_size) / totals[..., None]
    gated = gates.reshape(row_count, col_count, head_count, head_size) * attended
    gated = gated.astype(jnp.bfloat16).reshape(row_count * col_count, inner_width)
    updated = jnp.dot(gated, out_weight, preferred_element_type=jnp.float32) + out_bias
    return updated.astype(jnp.bfloat16).reshape(row_count, col_count, channels)


def fits(mesh, pair_shape, heads, inner):
    rows, cols, channels = pair_shape
    return (
        (mesh.shape["rows"], mesh.shape["cols"]) == (16, 2)
        and (rows, cols, channels) == (24, 192, LANES)
        and (heads, inner) == (4, LANES)
    )


def shards(
    pair, token_mask, norm_gain, norm_shift, in_weight, gate_bias, bias_weight, out_weight, out_bias
):
    rows, cols, channels = pair.shape
    inner = out_weight.shape[0]
    gain, shift = norm_gain.reshape(1, channels), norm_shift.reshape(1, channels)
    swap = [(0, 1), (1, 0)]
    normed, tile = norm_and_tile(pair, gain, shift, bias_weight, token_mask, 12)
    row = lax.axis_index("rows")
    x = lax.axis_index("cols")
    z_hi, z_lo, y, core = row >> 3, (row >> 2) & 1, (row >> 1) & 1, row & 1
    near, far = spread_tiles(tile, z_hi, x)
    others = [lax.ppermute(normed[begin : begin + count], "cols", swap) for begin, count in CHUNKS]
    place = jnp.arange(16, dtype=jnp.int32)
    half, a, b, c = place >> 3, (place >> 2) & 1, (place >> 1) & 1, place & 1
    index = (c ^ core) * 8 + (a ^ z_lo) * 4 + (b ^ y) * 2 + half
    bias = assemble(index, near, far, lane_order(cols, rows, 8))
    wk, wv = in_weight[:, inner : 2 * inner], in_weight[:, 2 * inner : 3 * inner].T
    wqg = jnp.concatenate((in_weight[:, :inner].T, in_weight[:, 3 * inner :].T), 0)
    own = project(normed, (wk, wv, wqg, gate_bias.reshape(inner, 1)), 8)
    out = None
    for (begin, count), other in zip(CHUNKS, others):
        if out is not None:
            other, out = lax.optimization_barrier((other, out))
        out = attend(
            other, *own, bias, wk, wv, out_weight, out_bias.reshape(1, channels), out, begin
        )
    return out


def solution(mesh):
    placed = (P("rows", "cols", None), P("cols"), P(), P(), P(), P(), P(), P(), P())

    def run(pair, *rest):
        tall, wide, channels = pair.shape
        block = (tall // mesh.shape["rows"], wide // mesh.shape["cols"], channels)
        bias_weight, out_weight = rest[5], rest[6]
        special = fits(mesh, block, bias_weight.shape[1], out_weight.shape[0])
        return jax.shard_map(
            shards if special else shards_general,
            mesh=mesh,
            in_specs=placed,
            out_specs=P("rows", "cols", None),
            check_vma=False,
        )(pair, *rest)

    return run
```

time: 84.4 us -> 50.1 us (0.59)
  Pallas kernels: 35.4 us -> 24.6 us
  local copies, waits for them, and re-layouts: 12 us -> 2.9 us
  waiting for transfers between devices: 12.4 us -> 5.97 us
  starting transfers between devices: 21.1 us -> 15 us
  other arithmetic: 2.84 us -> 0.88 us
    unnamed x54 -> x17, local copies, waits for them, and re-layouts: 9.51 us -> 0.41 us
    pallas_call x4, Pallas kernels: 28 us -> 21.2 us  [the longest x3 17.6 us: attend(): pl.pallas_call(functools.partial(attend_kernel, begin, out is None), grid...]
    ppermute x12 -> x9, waiting for transfers between devices: 12.4 us -> 5.97 us  [the longest x6 5.43 us: moved(): return lax.ppermute(array, ('rows', 'cols'), pairs)]
    ppermute x12 -> x9, starting transfers between devices: 21.1 us -> 15 us  [the longest x6 8.32 us: moved(): return lax.ppermute(array, ('rows', 'cols'), pairs)]
    pallas_call x3 -> x1, Pallas kernels: 5.71 us -> 2.08 us  [project(): pl.pallas_call(project_kernel, grid=(rows // block,), in_specs=[tile(cols...]
    slice x1, local copies, waits for them, and re-layouts: 0.08 us -> 2.33 us  [shards(): normed[begin:begin + count]]
    concatenate x1 -> x0, other arithmetic: 2.14 us -> none  [shards(): return jnp.concatenate(outs, 0)]
    unnamed x0 -> x2, other arithmetic: none -> 0.85 us
  transfers between devices with their start and end apart: 12 -> 9, of which waited for: 4 -> 3; matrix products, arithmetic and copies ran while one was open for 1% -> 7% of each run, Pallas kernels for 7% -> 31%
where the time goes in v2:
time: 50.1 us; the launch traced here: 49.6 us
  Pallas kernels  24.6 us (49%)
  starting transfers between devices  15 us (30%)
  waiting for transfers between devices  5.97 us (12%)
  local copies, waits for them, and re-layouts  2.9 us (6%)
  other arithmetic  0.88 us (2%)
    pallas_call x3, Pallas kernels, attend(): pl.pallas_call(functools.partial(attend_kernel, begin, out is None), grid...  17.6 us
    ppermute x6, starting transfers between devices, moved(): return lax.ppermute(array, ('rows', 'cols'), pairs)  8.32 us
    ppermute x3, starting transfers between devices, shards(): lax.ppermute(normed[begin:begin + count], 'cols', swap)  6.67 us
    ppermute x6, waiting for transfers between devices, moved(): return lax.ppermute(array, ('rows', 'cols'), pairs)  5.43 us
    pallas_call x1, Pallas kernels, norm_and_tile(): pl.pallas_call(norm_kernel, grid=(rows // block,), in_specs=[rows_spec] +...  3.57 us
    slice x1, local copies, waits for them, and re-layouts, shards(): normed[begin:begin + count]  2.33 us
    pallas_call x1, Pallas kernels, project(): pl.pallas_call(project_kernel, grid=(rows // block,), in_specs=[tile(cols...  2.08 us
    pallas_call x1, Pallas kernels, assemble(): pl.pallas_call(assemble_kernel, in_specs=[smem, vmem, vmem, vmem], out_sp...  1.37 us
  transfers between devices with their start and end apart: 9, of which 3 were waited for; matrix products, arithmetic and copies ran while one was open for 7% of the time, Pallas kernels for 31%

profile of v2, /device:TPU:0, one launch (start us, length us, event | category | flops | bytes accessed | tf_op | source)
XLA Modules:
  0.0 49.6 jit_solution(11365204771731398377)
XLA Ops:
  0.0 3.6 %norm_and_tile.1 = (bf16[24,192,128]{2,1,0:T(8,128)(2,1)}, bf16[192,128]{1,0:T(8,128)(2,1)}) custom-call(bf16[24,192,128]{2,1,0:T(8,128)(2,1)} %pair_ref.1, f32[1,128]{1,0:T(1,128)} %bitcast.27, f32[1,128]{1,0:T(1,128)} %bitcast.28, bf16[4,128]{1,0:T(4,128)(2,1)} %bitcast.25, s32[1,192]{1,0:T(1,128)} %bitcast.26), custom_call_target="tpu_custom_call" | custom-call | flops 1000000000 | bytes 10000000 | tf_op jit(solution)/shard_map/norm_and_tile/pallas_call | solution.py:76
  3.6 4.0 %collective-permute-start.3 = (bf16[192,128]{1,0:T(8,128)(2,1)}, bf16[192,128]{1,0:T(8,128)(2,1)S(1)}, u32[]{:S(2)}, u32[]{:S(2)}) collective-permute-start(bf16[192,128]{1,0:T(8,128)(2,1)} %get-tuple-element.20), channel_id=1, source_target_pairs={{0,16},{1,0},{2,18},{3,2},{4,20},{5,4},{6,22},{7,6},{8,24},{9,8},{... | collective-permute-start | bytes 147464 | tf_op jit(solution)/shard_map/ppermute | solution.py:329
  7.6 0.7 %collective-permute-start.4 = (bf16[192,128]{1,0:T(8,128)(2,1)}, bf16[192,128]{1,0:T(8,128)(2,1)S(1)}, u32[]{:S(2)}, u32[]{:S(2)}) collective-permute-start(bf16[192,128]{1,0:T(8,128)(2,1)} %get-tuple-element.20), channel_id=1, source_target_pairs={{1,16},{3,18},{5,20},{7,22},{9,24},{11,26},{13,28},{15,30},{16,1},... | collective-permute-start | bytes 147464 | tf_op jit(solution)/shard_map/ppermute | solution.py:329
  8.3 1.4 %collective-permute-done.3 = bf16[192,128]{1,0:T(8,128)(2,1)S(1)} collective-permute-done((bf16[192,128]{1,0:T(8,128)(2,1)}, bf16[192,128]{1,0:T(8,128)(2,1)S(1)}, u32[]{:S(2)}, u32[]{:S(2)}) %collective-permute-start.3) | collective-permute-done | bytes 49184 | tf_op jit(solution)/shard_map/ppermute | solution.py:329
  9.7 0.8 %constant_dynamic-update-slice_fusion.4 = (bf16[8,192,128]{2,1,0:T(8,128)(2,1)S(1)}, bf16[1,192,128]{2,1,0:T(8,128)(2,1)S(1)}) fusion(bf16[192,128]{1,0:T(8,128)(2,1)} %get-tuple-element.20, bf16[192,128]{1,0:T(8,128)(2,1)S(1)} %collective-permute-done.3, pred[]{:T(512)S(6)} %eq.3), kind=kLoop, calls=%fused_computation.8 | loop fusion | flops 24575 | bytes 196609
  10.5 0.0 collective-permute-done.4
  10.6 1.6 %collective-permute-start.5 = (bf16[2,192,128]{2,1,0:T(8,128)(2,1)S(1)}, bf16[2,192,128]{2,1,0:T(8,128)(2,1)S(1)}, u32[]{:S(2)}, u32[]{:S(2)}) collective-permute-start(bf16[2,192,128]{2,1,0:T(8,128)(2,1)S(1)} %pad_maximum_fusion), channel_id=1, source_target_pairs={{0,4},{1,5},{2,6},{3,7},{4,0},{5,1},{6,2},{7,3},{8,12},{9,13},{10,... | collective-permute-start | bytes 294920 | tf_op jit(solution)/shard_map/ppermute | solution.py:329
  12.1 0.0 copy-start.4
  12.2 0.0 copy-start.5
  12.2 2.3 %fusion = (bf16[8,192,128]{2,1,0:T(8,128)(2,1)}, bf16[8,192,128]{2,1,0:T(8,128)(2,1)}, bf16[8,192,128]{2,1,0:T(8,128)(2,1)}) fusion(bf16[24,192,128]{2,1,0:T(8,128)(2,1)} %get-tuple-element.15.own_ref), kind=kLoop, calls=%fused_computation.10 | loop fusion | bytes 2359296 | tf_op jit(solution)/shard_map/slice | solution.py:453
  14.5 0.0 copy-start
  14.5 4.6 %collective-permute-start.2 = (bf16[8,192,128]{2,1,0:T(8,128)(2,1)}, bf16[8,192,128]{2,1,0:T(8,128)(2,1)S(1)}, u32[]{:S(2)}, u32[]{:S(2)}) collective-permute-start(bf16[8,192,128]{2,1,0:T(8,128)(2,1)} %get-tuple-element.29), channel_id=1, source_target_pairs={{0,1},{1,0},{2,3},{3,2},{4,5},{5,4},{6,7},{7,6},{8,9},{9,8},{10,11... | collective-permute-start | bytes 1179656 | tf_op jit(solution)/shard_map/ppermute | solution.py:453
  19.1 0.0 collective-permute-start.1
  19.2 2.0 %collective-permute-start = (bf16[8,192,128]{2,1,0:T(8,128)(2,1)}, bf16[8,192,128]{2,1,0:T(8,128)(2,1)S(1)}, u32[]{:S(2)}, u32[]{:S(2)}) collective-permute-start(bf16[8,192,128]{2,1,0:T(8,128)(2,1)} %get-tuple-element.31), channel_id=1, source_target_pairs={{0,1},{1,0},{2,3},{3,2},{4,5},{5,4},{6,7},{7,6},{8,9},{9,8},{10,11... | collective-permute-start | bytes 1179656 | tf_op jit(solution)/shard_map/ppermute | solution.py:453
  21.2 1.4 %collective-permute-start.7 = (bf16[2,192,128]{2,1,0:T(8,128)(2,1)S(1)}, bf16[2,192,128]{2,1,0:T(8,128)(2,1)S(1)}, u32[]{:S(2)}, u32[]{:S(2)}) collective-permute-start(bf16[2,192,128]{2,1,0:T(8,128)(2,1)S(1)} %pad_maximum_fusion), channel_id=1, source_target_pairs={{0,12},{1,13},{2,14},{3,15},{4,8},{5,9},{6,10},{7,11},{8,4},{9,5},... | collective-permute-start | bytes 294920 | tf_op jit(solution)/shard_map/ppermute | solution.py:329
  22.6 0.0 collective-permute-done.5
  22.6 0.6 %collective-permute-start.6 = (bf16[2,192,128]{2,1,0:T(8,128)(2,1)S(1)}, bf16[2,192,128]{2,1,0:T(8,128)(2,1)S(1)}, u32[]{:S(2)}, u32[]{:S(2)}) collective-permute-start(bf16[2,192,128]{2,1,0:T(8,128)(2,1)S(1)} %pad_maximum_fusion), channel_id=1, source_target_pairs={{0,8},{1,9},{2,10},{3,11},{4,12},{5,13},{6,14},{7,15},{8,0},{9,1},... | collective-permute-start | bytes 294920 | tf_op jit(solution)/shard_map/ppermute | solution.py:329
  23.1 4.0 %collective-permute-done.6 = bf16[2,192,128]{2,1,0:T(8,128)(2,1)S(1)} collective-permute-done((bf16[2,192,128]{2,1,0:T(8,128)(2,1)S(1)}, bf16[2,192,128]{2,1,0:T(8,128)(2,1)S(1)}, u32[]{:S(2)}, u32[]{:S(2)}) %collective-permute-start.6) | collective-permute-done | bytes 98336 | tf_op jit(solution)/shard_map/ppermute | solution.py:329
  27.2 0.0 collective-permute-done.7
  27.2 0.1 collective-permute-start.8
  27.3 0.0 copy-done.4
  27.4 0.0 copy-done.5
  27.4 0.1 copy.16.gb_ref
  27.5 0.1 copy.18
  27.6 0.1 copy.17
  27.7 0.1 copy.19
  27.9 0.0 copy-done
  27.9 0.0 copy-start.3
  27.9 2.1 %project_own.1 = (bf16[24,192,128]{2,1,0:T(8,128)(2,1)S(1)}, bf16[24,128,192]{2,1,0:T(8,128)(2,1)S(1)}, bf16[24,128,256]{2,1,0:T(8,128)(2,1)S(1)}, f32[24,128,256]{2,1,0:T(8,128)S(1)}) custom-call(bf16[24,192,128]{2,1,0:T(8,128)(2,1)S(1)} %copy-done, bf16[128,128]{1,0:T(8,128)(2,1)S(1)} %get-tuple-element.34.wk_ref.refs_6_.refs_7_, ...), custom_call_target="tpu_custom_call" | custom-call | flops 1000000000 | bytes 10000000 | tf_op jit(solution)/shard_map/project_own/pallas_call | solution.py:163
  30.0 0.0 copy-start.1
  30.0 0.0 copy-start.2
  30.0 0.0 collective-permute-done.8.far_ref
  30.0 0.0 copy-done.3
  30.0 1.4 %assemble_bias.1.refs_5_.refs_6_ = f32[392,768]{1,0:T(8,128)S(1)} custom-call(s32[16]{0:T(128)S(1)} %shift-right-arithmetic_add_fusion.index_ref, bf16[8,192,128]{2,1,0:T(8,128)(2,1)S(1)} %constant_dynamic-update-slice_fusion.near_ref, bf16[8,192,128]{2,1,0:T(8,128)(2,1)S(1)} %collective-permute-done.8.far_ref, bf16[1024,768]{1,0:T(8,128)(2,1)S(1)} %copy-done.3), custom_call_target="tpu_custom_call" | custom-call | flops 1000000000 | bytes 4000000 | tf_op jit(solution)/shard_map/assemble_bias/pallas_call | solution.py:130
  31.4 0.0 collective-permute-done.2.refs_0_
  31.4 0.0 copy-done.1
  31.4 0.0 copy-done.2
  31.4 5.8 %attend_rows.3.refs_0_ = bf16[24,192,128]{2,1,0:T(8,128)(2,1)} custom-call(bf16[8,192,128]{2,1,0:T(8,128)(2,1)S(1)} %collective-permute-done.2.refs_0_, bf16[24,192,128]{2,1,0:T(8,128)(2,1)S(1)} %get-tuple-element.16.refs_1_.refs_2_, bf16[24,128,192]{2,1,0:T(8,128)(2,1)S(1)} %get-tuple-element.17.refs_2_.refs_3_, ...), custom_call_target="tpu_custom_call" | custom-call | flops 10000000000 | bytes 10000000 | tf_op jit(solution)/shard_map/attend_rows/pallas_call | solution.py:296
  37.3 0.5 %collective-permute-done.1.refs_1_ = bf16[8,192,128]{2,1,0:T(8,128)(2,1)S(1)} collective-permute-done((bf16[8,192,128]{2,1,0:T(8,128)(2,1)}, bf16[8,192,128]{2,1,0:T(8,128)(2,1)S(1)}, u32[]{:S(2)}, u32[]{:S(2)}) %collective-permute-start.1) | collective-permute-done | bytes 393248 | tf_op jit(solution)/shard_map/ppermute | solution.py:453
  37.8 5.9 %attend_rows.4.refs_0_ = bf16[24,192,128]{2,1,0:T(8,128)(2,1)} custom-call(bf16[24,192,128]{2,1,0:T(8,128)(2,1)} %attend_rows.3.refs_0_, bf16[8,192,128]{2,1,0:T(8,128)(2,1)S(1)} %collective-permute-done.1.refs_1_, bf16[24,192,128]{2,1,0:T(8,128)(2,1)S(1)} %get-tuple-element.16.refs_1_.refs_2_, ...), custom_call_target="tpu_custom_call", output_to_operand_aliasing={{}: (0, {})} | custom-call | flops 10000000000 | bytes 10000000 | tf_op jit(solution)/shard_map/attend_rows/pallas_call | solution.py:296
  43.7 0.0 collective-permute-done.refs_1_
  43.7 5.9 %attend_rows.5 = bf16[24,192,128]{2,1,0:T(8,128)(2,1)} custom-call(bf16[24,192,128]{2,1,0:T(8,128)(2,1)} %attend_rows.4.refs_0_, bf16[8,192,128]{2,1,0:T(8,128)(2,1)S(1)} %collective-permute-done.refs_1_, bf16[24,192,128]{2,1,0:T(8,128)(2,1)S(1)} %get-tuple-element.16.refs_1_.refs_2_, ...), custom_call_target="tpu_custom_call", output_to_operand_aliasing={{}: (0, {})} | custom-call | flops 10000000000 | bytes 10000000 | tf_op jit(solution)/shard_map/attend_rows/pallas_call | solution.py:296
  (8 shorter events, 0.1 us)
Async XLA Ops:
  3.6 6.1 %collective-permute-start.3 = (bf16[192,128]{1,0:T(8,128)(2,1)}, bf16[192,128]{1,0:T(8,128)(2,1)S(1)}, u32[]{:S(2)}, u32[]{:S(2)}) collective-permute-start(bf16[192,128]{1,0:T(8,128)(2,1)} %get-tuple-element.20), channel_id=1, source_target_pairs={{0,16},{1,0},{2,18},{3,2},{4,20},{5,4},{6,22},{7,6},{8,24},{9,8},{... | collective-permute-start | bytes 147464 | tf_op jit(solution)/shard_map/ppermute | solution.py:329
  7.6 2.9 %collective-permute-start.4 = (bf16[192,128]{1,0:T(8,128)(2,1)}, bf16[192,128]{1,0:T(8,128)(2,1)S(1)}, u32[]{:S(2)}, u32[]{:S(2)}) collective-permute-start(bf16[192,128]{1,0:T(8,128)(2,1)} %get-tuple-element.20), channel_id=1, source_target_pairs={{1,16},{3,18},{5,20},{7,22},{9,24},{11,26},{13,28},{15,30},{16,1},... | collective-permute-start | bytes 147464 | tf_op jit(solution)/shard_map/ppermute | solution.py:329
  10.6 12.0 %collective-permute-start.5 = (bf16[2,192,128]{2,1,0:T(8,128)(2,1)S(1)}, bf16[2,192,128]{2,1,0:T(8,128)(2,1)S(1)}, u32[]{:S(2)}, u32[]{:S(2)}) collective-permute-start(bf16[2,192,128]{2,1,0:T(8,128)(2,1)S(1)} %pad_maximum_fusion), channel_id=1, source_target_pairs={{0,4},{1,5},{2,6},{3,7},{4,0},{5,1},{6,2},{7,3},{8,12},{9,13},{10,... | collective-permute-start | bytes 294920 | tf_op jit(solution)/shard_map/ppermute | solution.py:329
  12.1 15.2 %copy-start.4 = (bf16[128,512]{1,0:T(8,128)(2,1)S(1)}, bf16[128,512]{1,0:T(8,128)(2,1)}, u32[]{:S(2)}) copy-start(bf16[128,512]{1,0:T(8,128)(2,1)} %param.14) | copy-start | bytes 393220
  12.2 15.2 %copy-start.5 = (f32[128]{0:T(128)S(1)}, f32[128]{0:T(128)}, u32[]{:S(2)}) copy-start(f32[128]{0:T(128)} %param.15) | copy-start | bytes 1540
  14.5 13.4 %copy-start = (bf16[24,192,128]{2,1,0:T(8,128)(2,1)S(1)}, bf16[24,192,128]{2,1,0:T(8,128)(2,1)}, u32[]{:S(2)}) copy-start(bf16[24,192,128]{2,1,0:T(8,128)(2,1)} %get-tuple-element.15.own_ref) | copy-start | bytes 3538948
  14.5 16.9 %collective-permute-start.2 = (bf16[8,192,128]{2,1,0:T(8,128)(2,1)}, bf16[8,192,128]{2,1,0:T(8,128)(2,1)S(1)}, u32[]{:S(2)}, u32[]{:S(2)}) collective-permute-start(bf16[8,192,128]{2,1,0:T(8,128)(2,1)} %get-tuple-element.29), channel_id=1, source_target_pairs={{0,1},{1,0},{2,3},{3,2},{4,5},{5,4},{6,7},{7,6},{8,9},{9,8},{10,11... | collective-permute-start | bytes 1179656 | tf_op jit(solution)/shard_map/ppermute | solution.py:453
  19.1 18.7 %collective-permute-start.1 = (bf16[8,192,128]{2,1,0:T(8,128)(2,1)}, bf16[8,192,128]{2,1,0:T(8,128)(2,1)S(1)}, u32[]{:S(2)}, u32[]{:S(2)}) collective-permute-start(bf16[8,192,128]{2,1,0:T(8,128)(2,1)} %get-tuple-element.30), channel_id=1, source_target_pairs={{0,1},{1,0},{2,3},{3,2},{4,5},{5,4},{6,7},{7,6},{8,9},{9,8},{10,11... | collective-permute-start | bytes 1179656 | tf_op jit(solution)/shard_map/ppermute | solution.py:453
  19.2 24.5 %collective-permute-start = (bf16[8,192,128]{2,1,0:T(8,128)(2,1)}, bf16[8,192,128]{2,1,0:T(8,128)(2,1)S(1)}, u32[]{:S(2)}, u32[]{:S(2)}) collective-permute-start(bf16[8,192,128]{2,1,0:T(8,128)(2,1)} %get-tuple-element.31), channel_id=1, source_target_pairs={{0,1},{1,0},{2,3},{3,2},{4,5},{5,4},{6,7},{7,6},{8,9},{9,8},{10,11... | collective-permute-start | bytes 1179656 | tf_op jit(solution)/shard_map/ppermute | solution.py:453
  21.2 6.0 %collective-permute-start.7 = (bf16[2,192,128]{2,1,0:T(8,128)(2,1)S(1)}, bf16[2,192,128]{2,1,0:T(8,128)(2,1)S(1)}, u32[]{:S(2)}, u32[]{:S(2)}) collective-permute-start(bf16[2,192,128]{2,1,0:T(8,128)(2,1)S(1)} %pad_maximum_fusion), channel_id=1, source_target_pairs={{0,12},{1,13},{2,14},{3,15},{4,8},{5,9},{6,10},{7,11},{8,4},{9,5},... | collective-permute-start | bytes 294920 | tf_op jit(solution)/shard_map/ppermute | solution.py:329
  22.6 4.6 %collective-permute-start.6 = (bf16[2,192,128]{2,1,0:T(8,128)(2,1)S(1)}, bf16[2,192,128]{2,1,0:T(8,128)(2,1)S(1)}, u32[]{:S(2)}, u32[]{:S(2)}) collective-permute-start(bf16[2,192,128]{2,1,0:T(8,128)(2,1)S(1)} %pad_maximum_fusion), channel_id=1, source_target_pairs={{0,8},{1,9},{2,10},{3,11},{4,12},{5,13},{6,14},{7,15},{8,0},{9,1},... | collective-permute-start | bytes 294920 | tf_op jit(solution)/shard_map/ppermute | solution.py:329
  27.2 2.8 %collective-permute-start.8 = (bf16[8,192,128]{2,1,0:T(8,128)(2,1)S(1)}, bf16[8,192,128]{2,1,0:T(8,128)(2,1)S(1)}, u32[]{:S(2)}, u32[]{:S(2)}) collective-permute-start(bf16[8,192,128]{2,1,0:T(8,128)(2,1)S(1)} %constant_dynamic-update-slice_fusion.near_ref), channel_id=1, source_target_pairs={{0,2},{1,3},{2,0},{3,1},{4,6},{5,7},{6,4},{7,5},{8,10},{9,11},{10,... | collective-permute-start | bytes 1179656 | tf_op jit(solution)/shard_map/ppermute | solution.py:329
  27.9 2.2 %copy-start.3 = (bf16[1024,768]{1,0:T(8,128)(2,1)S(1)}, bf16[1024,768]{1,0:T(8,128)(2,1)}, u32[]{:S(2)}) copy-start(bf16[1024,768]{1,0:T(8,128)(2,1)} %constant.7.clone.order_ref) | copy-start | bytes 4718596
  30.0 1.4 %copy-start.1 = (bf16[128,128]{1,0:T(8,128)(2,1)S(1)}, bf16[128,128]{1,0:T(8,128)(2,1)}, u32[]{:S(2)}) copy-start(bf16[128,128]{1,0:T(8,128)(2,1)} %refs_9_.3) | copy-start | bytes 98308
  30.0 1.4 %copy-start.2 = (f32[128]{0:T(128)S(1)}, f32[128]{0:T(128)}, u32[]{:S(2)}) copy-start(f32[128]{0:T(128)} %param.18) | copy-start | bytes 1540

commit v3 on v2

--- a/solution.py
+++ b/solution.py
@@ -37,55 +37,63 @@
     return (center * lax.rsqrt(spread + 1e-05) * gain + shift).astype(jnp.bfloat16)
 
 
-def norm_kernel(pair_ref, gain_ref, shift_ref, weight_ref, mask_ref, normed_ref, tile_ref, total, wide):
-    step = pl.program_id(0)
+def norm_kernel(parts, pair_hbm, *refs):
+    small_hbm, refs = refs[:4], refs[4:]
+    normed_refs, tile_ref, refs = refs[: len(parts)], refs[len(parts)], refs[len(parts) + 1 :]
+    pair_ref, gain_ref, shift_ref, weight_ref, mask_ref, done = refs
     rows, slots = pair_ref.shape[0], 32
-    lane = lax.broadcasted_iota(jnp.int32, (LANES, LANES), 1)
-
-    @pl.when(step == 0)
-    def _():
-        heads = weight_ref.shape[0]
-        head = lax.broadcasted_iota(jnp.int32, (heads, LANES), 0)
-        place = lax.broadcasted_iota(jnp.int32, (heads, LANES), 1)
-        begin = head * slots
-        expand = jnp.logical_and(place >= begin, place < begin + slots)
-        wide[...] = dot(weight_ref[...], expand.astype(jnp.bfloat16), TN)
-        spot = lax.broadcasted_iota(jnp.int32, (1, LANES), 1) == rows * pl.num_programs(0)
-        total[...] = dot(mask_ref[...].astype(jnp.bfloat16), spot.astype(jnp.bfloat16), TN)
-
-    slot = lax.rem(lane, slots)
+    copies = [
+        pltpu.make_async_copy(source, target, done.at[place])
+        for place, (source, target) in enumerate(
+            zip(small_hbm, (gain_ref, shift_ref, weight_ref, mask_ref))
+        )
+    ]
+    for place, (begin, count) in enumerate(parts):
+        block = pl.ds(begin, count)
+        copies.append(
+            pltpu.make_async_copy(pair_hbm.at[block], pair_ref.at[block], done.at[4 + place])
+        )
+    for copy in copies:
+        copy.start()
+    for copy in copies[:4]:
+        copy.wait()
+
+    heads = weight_ref.shape[0]
+    head = lax.broadcasted_iota(jnp.int32, (heads, LANES), 0)
+    place = lax.broadcasted_iota(jnp.int32, (heads, LANES), 1)
+    expand = jnp.logical_and(place >= head * slots, place < head * slots + slots)
+    wide = dot(weight_ref[...], expand.astype(jnp.bfloat16), TN)
+    spot = lax.broadcasted_iota(jnp.int32, (1, LANES), 1) == rows
+    total = dot(mask_ref[...].astype(jnp.bfloat16), spot.astype(jnp.bfloat16), TN)
+    slot = lax.rem(lax.broadcasted_iota(jnp.int32, (LANES, LANES), 1), slots)
     mean_weight = jnp.full((LANES, LANES), 1 / LANES, jnp.bfloat16)
-    left, right = [], []
-    for row in range(rows):
-        normed = normed_rows(pair_ref[row], mean_weight, gain_ref[...], shift_ref[...])
-        normed_ref[row] = normed
-        left.append(normed)
-        right.append(jnp.where(slot == step * rows + row, wide[...], 0.0).astype(jnp.bfloat16))
-    total[...] += dot(jnp.concatenate(left, 1), jnp.concatenate(right, 0))
-
-    @pl.when(step == pl.num_programs(0) - 1)
-    def _():
-        tile_ref[...] = total[...].astype(jnp.bfloat16)
-
-
-def norm_and_tile(pair, gain, shift, bias_weight, mask, block):
+    for (begin, count), copy, normed_ref in zip(parts, copies[4:], normed_refs):
+        copy.wait()
+        left, right = [], []
+        for row in range(begin, begin + count):
+            normed = normed_rows(pair_ref[row], mean_weight, gain_ref[...], shift_ref[...])
+            normed_ref[row - begin] = normed
+            left.append(normed)
+            right.append(jnp.where(slot == row, wide, 0.0).astype(jnp.bfloat16))
+        total += dot(jnp.concatenate(left, 1), jnp.concatenate(right, 0))
+    tile_ref[...] = total.astype(jnp.bfloat16)
+
+
+def norm_and_tile(pair, gain, shift, bias_weight, mask, parts):
     rows, cols, channels = pair.shape
-    whole = lambda a: pl.BlockSpec(a.shape, lambda i: (0,) * a.ndim)
     small = (gain, shift, bias_weight.T, mask.reshape(1, cols))
-    rows_spec = pl.BlockSpec((block, cols, channels), lambda i: (i, 0, 0))
+    vmem = pl.BlockSpec(memory_space=pltpu.VMEM)
     return pl.pallas_call(
-        norm_kernel,
-        grid=(rows // block,),
-        in_specs=[rows_spec] + [whole(a) for a in small],
-        out_specs=[rows_spec, pl.BlockSpec((cols, LANES), lambda i: (0, 0))],
+        functools.partial(norm_kernel, parts),
+        in_specs=[pl.BlockSpec(memory_space=pltpu.HBM)] * 5,
+        out_specs=[vmem] * (len(parts) + 1),
         out_shape=[
-            jax.ShapeDtypeStruct(pair.shape, jnp.bfloat16),
-            jax.ShapeDtypeStruct((cols, LANES), jnp.bfloat16),
-        ],
-        scratch_shapes=[
-            pltpu.VMEM((cols, LANES), jnp.float32),
-            pltpu.VMEM((channels, LANES), jnp.float32),
-        ],
+            jax.ShapeDtypeStruct((count, cols, channels), jnp.bfloat16) for _, count in parts
+        ]
+        + [jax.ShapeDtypeStruct((cols, LANES), jnp.bfloat16)],
+        scratch_shapes=[pltpu.VMEM(pair.shape, pair.dtype)]
+        + [pltpu.VMEM(a.shape, a.dtype) for a in small]
+        + [pltpu.SemaphoreType.DMA((4 + len(parts),))],
         compiler_params=pltpu.CompilerParams(vmem_limit_bytes=ALL_VMEM),
         cost_estimate=pl.CostEstimate(flops=10**9, bytes_accessed=10**7, transcendentals=0),
         name="norm_and_tile",
@@ -142,46 +150,78 @@
     )(index, near, far, order)
 
 
-def project_kernel(own_ref, wk_ref, wv_ref, wqg_ref, gb_ref, k_ref, v_ref, q_ref, g_ref):
-    rows, cols, channels = own_ref.shape
-    keys = dot(own_ref[...].reshape(rows * cols, channels), wk_ref[...])
-    k_ref[...] = keys.astype(jnp.bfloat16).reshape(k_ref.shape)
-    for row in range(rows):
-        own = own_ref[row]
-        v_ref[row] = dot(wv_ref[...], own, NT).astype(jnp.bfloat16)
-        mixed = dot(wqg_ref[...], jnp.concatenate((own, own[LANES:]), 0), NT)
-        q_ref[row] = (mixed[:LANES] * 32 ** (-0.5)).astype(jnp.bfloat16)
-        g_ref[row] = 0.5 * jnp.tanh(0.5 * (mixed[LANES:] + gb_ref[...])) + 0.5
-
-
-def project(normed, weights, block):
-    rows, cols, channels = normed.shape
-    tile = lambda *shape: pl.BlockSpec((block,) + shape, lambda i: (i, 0, 0))
-    whole = lambda a: pl.BlockSpec(a.shape, lambda i: (0,) * a.ndim)
+def project_kernel(count, *refs):
+    own_refs, refs = refs[:count], refs[count:]
+    wk_ref, wv_ref, wqg_ref, gb_ref, k_ref, v_ref, q_ref, g_ref = refs
+    begin = 0
+    for own_ref in own_refs:
+        rows, cols, channels = own_ref.shape
+        keys = dot(own_ref[...].reshape(rows * cols, channels), wk_ref[...])
+        k_ref[begin : begin + rows] = keys.astype(jnp.bfloat16).reshape(rows, cols, LANES)
+        for row in range(rows):
+            own = own_ref[row]
+            v_ref[begin + row] = dot(wv_ref[...], own, NT).astype(jnp.bfloat16)
+            mixed = dot(wqg_ref[...], jnp.concatenate((own, own[LANES:]), 0), NT)
+            q_ref[begin + row] = (mixed[:LANES] * 32 ** (-0.5)).astype(jnp.bfloat16)
+            g_ref[begin + row] = 0.5 * jnp.tanh(0.5 * (mixed[LANES:] + gb_ref[...])) + 0.5
+        begin += rows
+
+
+def project(parts, weights):
+    cols, channels = parts[0].shape[1:]
+    rows = sum(part.shape[0] for part in parts)
+    vmem = pl.BlockSpec(memory_space=pltpu.VMEM)
     sizes = ((cols, LANES), (LANES, cols), (LANES, 2 * LANES), (LANES, 2 * LANES))
     kinds = (jnp.bfloat16,) * 3 + (jnp.float32,)
     return pl.pallas_call(
-        project_kernel,
-        grid=(rows // block,),
-        in_specs=[tile(cols, channels)] + [whole(a) for a in weights],
-        out_specs=[tile(*size) for size in sizes],
+        functools.partial(project_kernel, len(parts)),
+        in_specs=[vmem] * (len(parts) + len(weights)),
+        out_specs=[vmem] * 4,
         out_shape=[jax.ShapeDtypeStruct((rows,) + size, kind) for size, kind in zip(sizes, kinds)],
         compiler_params=pltpu.CompilerParams(vmem_limit_bytes=VMEM),
-        cost_estimate=pl.CostEstimate(flops=10**9, bytes_accessed=10**7, transcendentals=0),
+        cost_estimate=pl.CostEstimate(flops=1, bytes_accessed=10, transcendentals=0),
         name="project_own",
-    )(normed, *weights)
+    )(*parts, *weights)
+
+
+def widen_kernel(other_ref, wk_ref, wv_ref, k_ref, v_ref):
+    rows, cols, channels = other_ref.shape
+    keys = dot(other_ref[...].reshape(rows * cols, channels), wk_ref[...])
+    k_ref[...] = keys.astype(jnp.bfloat16).reshape(rows, cols, LANES)
+    for row in range(rows):
+        v_ref[row] = dot(wv_ref[...], other_ref[row], NT).astype(jnp.bfloat16)
+
+
+def widen(other, wk, wv):
+    rows, cols, _ = other.shape
+    vmem = pl.BlockSpec(memory_space=pltpu.VMEM)
+    return pl.pallas_call(
+        widen_kernel,
+        in_specs=[vmem] * 3,
+        out_specs=[vmem] * 2,
+        out_shape=[
+            jax.ShapeDtypeStruct((rows, cols, LANES), jnp.bfloat16),
+            jax.ShapeDtypeStruct((rows, LANES, cols), jnp.bfloat16),
+        ],
+        compiler_params=pltpu.CompilerParams(vmem_limit_bytes=VMEM),
+        cost_estimate=pl.CostEstimate(flops=10**10, bytes_accessed=10, transcendentals=0),
+        name="widen_rows",
+    )(other, wk, wv)
 
 
 TILE_ROWS = ((0, 32), (32, 64), (0, 64), (64, 96), (96, 128), (64, 128))
 
 
 def attend_kernel(begin, first, *refs):
+    if first:
+        k_other, v_other, *refs = refs
+    else:
+        _, other_ref, wk_ref, wv_ref, *refs = refs
+    k_ref, v_ref, q_ref, g_ref, bias_ref, wo_ref, ob_ref, out_ref, v_both, *scratch = refs
     if not first:
-        refs = refs[1:]
-    other_ref, k_ref, v_ref, q_ref, g_ref, bias_ref, wk_ref, wv_ref, wo_ref, ob_ref, out_ref = refs[:11]
-    k_other, v_both, *scratch = refs[11:]
+        k_other, *scratch = scratch
     scores, weights, tops, shares = (scratch[2 * n : 2 * n + 2] for n in range(4))
-    rows, cols, _ = other_ref.shape
+    rows, cols, _ = k_other.shape
     keys = 2 * cols
     low = lax.broadcasted_iota(jnp.int32, (32, LANES), 1) < 64
     lanes = [slice(tile * LANES, (tile + 1) * LANES) for tile in range(6)]
@@ -207,10 +247,13 @@
         return jnp.concatenate(pieces, 0)
 
     def widen(row):
-        other = other_ref[row]
-        k_other[row] = dot(other, wk_ref[...]).astype(jnp.bfloat16)
-        yield
-        values = dot(wv_ref[...], other, NT).astype(jnp.bfloat16)
+        if first:
+            values = v_other[row]
+        else:
+            other = other_ref[row]
+            k_other[row] = dot(other, wk_ref[...]).astype(jnp.bfloat16)
+            yield
+            values = dot(wv_ref[...], other, NT).astype(jnp.bfloat16)
         v_both[row] = jnp.concatenate((v_ref[begin + row], values), 1)
         yield
 
@@ -280,39 +323,39 @@
 
     @pl.when(present <= 0.5)
     def _():
-        for row in range(rows):
+        def one(row, carry):
             run(widen(row))
             run(score(row, 0, True))
             run(soften(0))
             run(mix(row, 0))
-
-
-def attend(other, k, v, q, g, bias, wk, wv, wo, ob, out, begin):
-    rows, cols, channels = other.shape
-    total, keys = k.shape[0], 2 * cols
-    lanes = bias.shape[1]
-    extra = [] if out is None else [out]
+            return carry
+
+        lax.fori_loop(0, rows, one, 0)
+
+
+def attend(head, k, v, q, g, bias, wo, ob, rows, begin):
+    total, cols, _ = k.shape
+    keys, lanes = 2 * cols, bias.shape[1]
+    first = len(head) == 2
     vmem = pl.BlockSpec(memory_space=pltpu.VMEM)
+    specs = [vmem] * 2 if first else [pl.BlockSpec(memory_space=pl.ANY)] + [vmem] * 3
+    own_keys = [] if first else [pltpu.VMEM((rows, cols, LANES), jnp.bfloat16)]
     return pl.pallas_call(
-        functools.partial(attend_kernel, begin, out is None),
+        functools.partial(attend_kernel, begin, first),
         grid=(1,),
-        in_specs=[pl.BlockSpec(memory_space=pl.ANY)] * len(extra) + [vmem] * 10,
+        in_specs=specs + [vmem] * 7,
         out_specs=pl.BlockSpec((rows, cols, LANES), lambda i: (begin // rows, 0, 0)),
         out_shape=jax.ShapeDtypeStruct((total, cols, LANES), jnp.bfloat16),
-        scratch_shapes=[
-            pltpu.VMEM((rows, cols, LANES), jnp.bfloat16),
-            pltpu.VMEM((rows, LANES, keys), jnp.bfloat16),
-        ]
+        scratch_shapes=[pltpu.VMEM((rows, LANES, keys), jnp.bfloat16)]
+        + own_keys
         + [pltpu.VMEM((keys, lanes), jnp.float32)] * 2
         + [pltpu.VMEM((keys, lanes), jnp.bfloat16)] * 2
         + [pltpu.VMEM((8, lanes), jnp.float32)] * 4,
-        input_output_aliases={0: 0} if extra else {},
+        input_output_aliases={} if first else {0: 0},
         compiler_params=pltpu.CompilerParams(vmem_limit_bytes=24 << 20),
-        cost_estimate=pl.CostEstimate(
-            flops=10**10, bytes_accessed=10**7, transcendentals=rows * keys * lanes
-        ),
+        cost_estimate=pl.CostEstimate(flops=10**10, bytes_accessed=10, transcendentals=0),
         name="attend_rows",
-    )(*extra, other, k, v, q, g, bias, wk, wv, wo, ob)
+    )(*head, k, v, q, g, bias, wo, ob)
 
 
 def device(z_hi, z_lo, y, core, x):
@@ -329,9 +372,10 @@
     return lax.ppermute(array, ("rows", "cols"), pairs)
 
 
-def spread_tiles(tile, z_hi, x):
+def spread_tiles(tile, z_hi, x, part):
     straight = moved(tile, lambda a, b, y, c, x: (1 - a, b, y, c, x) if a == x else (a, b, y, c, 1 - x))
     across = moved(tile, lambda a, b, y, c, x: None if a == x else (1 - a, b, y, c, 1 - x))
+    straight, part = lax.optimization_barrier((straight, part))
     home = z_hi == x
     pair = jnp.stack((jnp.where(home, tile, straight), jnp.where(home, straight, across)))
     near = [pair]
@@ -341,8 +385,7 @@
         lambda a, b, y, c, x: (a, 1 - b, 1 - y, c, x),
     ):
         near.append(moved(pair, move))
-    near = jnp.concatenate(near, 0)
-    return near, moved(near, lambda a, b, y, c, x: (a, b, y, 1 - c, x))
+    return jnp.concatenate(near, 0), part
 
 
 def shards_general(
@@ -445,26 +488,29 @@
     inner = out_weight.shape[0]
     gain, shift = norm_gain.reshape(1, channels), norm_shift.reshape(1, channels)
     swap = [(0, 1), (1, 0)]
-    normed, tile = norm_and_tile(pair, gain, shift, bias_weight, token_mask, 12)
+    *normed, tile = norm_and_tile(pair, gain, shift, bias_weight, token_mask, CHUNKS)
+    wk, wv = in_weight[:, inner : 2 * inner], in_weight[:, 2 * inner : 3 * inner].T
+    wqg = jnp.concatenate((in_weight[:, :inner].T, in_weight[:, 3 * inner :].T), 0)
+    own = list(project(normed, (wk, wv, wqg, gate_bias.reshape(inner, 1))))
     row = lax.axis_index("rows")
     x = lax.axis_index("cols")
     z_hi, z_lo, y, core = row >> 3, (row >> 2) & 1, (row >> 1) & 1, row & 1
-    near, far = spread_tiles(tile, z_hi, x)
-    others = [lax.ppermute(normed[begin : begin + count], "cols", swap) for begin, count in CHUNKS]
+    near, normed[1] = spread_tiles(tile, z_hi, x, normed[1])
+    near, *own = lax.optimization_barrier((near, *own))
+    others = [lax.ppermute(part, "cols", swap) for part in normed[:2]]
+    head = list(widen(others[0], wk, wv))
+    normed[2], head[0] = lax.optimization_barrier((normed[2], head[0]))
+    others.append(lax.ppermute(normed[2], "cols", swap))
+    far = moved(near, lambda a, b, y, c, x: (a, b, y, 1 - c, x))
     place = jnp.arange(16, dtype=jnp.int32)
     half, a, b, c = place >> 3, (place >> 2) & 1, (place >> 1) & 1, place & 1
     index = (c ^ core) * 8 + (a ^ z_lo) * 4 + (b ^ y) * 2 + half
     bias = assemble(index, near, far, lane_order(cols, rows, 8))
-    wk, wv = in_weight[:, inner : 2 * inner], in_weight[:, 2 * inner : 3 * inner].T
-    wqg = jnp.concatenate((in_weight[:, :inner].T, in_weight[:, 3 * inner :].T), 0)
-    own = project(normed, (wk, wv, wqg, gate_bias.reshape(inner, 1)), 8)
-    out = None
-    for (begin, count), other in zip(CHUNKS, others):
-        if out is not None:
-            other, out = lax.optimization_barrier((other, out))
-        out = attend(
-            other, *own, bias, wk, wv, out_weight, out_bias.reshape(1, channels), out, begin
-        )
+    tail = (*own, bias, out_weight, out_bias.reshape(1, channels))
+    out = attend(head, *tail, CHUNKS[0][1], CHUNKS[0][0])
+    for (begin, count), other in zip(CHUNKS[1:], others[1:]):
+        other, out = lax.optimization_barrier((other, out))
+        out = attend((out, other, wk, wv), *tail, count, begin)
     return out
 
 

time: 50.1 us -> 45 us (0.90)
  local copies, waits for them, and re-layouts: 2.9 us -> 0.56 us
  waiting for transfers between devices: 5.97 us -> 4.61 us
  Pallas kernels: 24.6 us -> 23.5 us
    ppermute x6, starting transfers between devices: 8.32 us -> 11.1 us  [moved(): return lax.ppermute(array, ('rows', 'cols'), pairs)]
    ppermute x3, starting transfers between devices: 6.67 us -> 3.92 us  [the longest x2 2.13 us: shards(): others = [lax.ppermute(part, 'cols', swap) for part in normed[:2]]]
    slice x1 -> x0, local copies, waits for them, and re-layouts: 2.33 us -> none  [shards(): normed[begin:begin + count]]
    pallas_call x5 -> x6, Pallas kernels: 23.3 us -> 22.1 us  [the longest x3 16.4 us: attend(): pl.pallas_call(functools.partial(attend_kernel, begin, first), grid=(1,),...]
    ppermute x6, waiting for transfers between devices: 5.43 us -> 4.6 us  [moved(): return lax.ppermute(array, ('rows', 'cols'), pairs)]
    ppermute x3, waiting for transfers between devices: 0.54 us -> 0.01 us  [the longest x2 0.01 us: shards(): others = [lax.ppermute(part, 'cols', swap) for part in normed[:2]]]
  transfers between devices with their start and end apart: 9 -> 9, of which waited for: 3 -> 2; matrix products, arithmetic and copies ran while one was open for 7% -> 3% of each run, Pallas kernels for 31% -> 32%
where the time goes in v3:
time: 45 us; the launch traced here: 44.8 us
  Pallas kernels  23.5 us (52%)
  starting transfers between devices  15 us (33%)
  waiting for transfers between devices  4.61 us (10%)
  other arithmetic  0.88 us (2%)
  local copies, waits for them, and re-layouts  0.56 us (1%)
    pallas_call x3, Pallas kernels, attend(): pl.pallas_call(functools.partial(attend_kernel, begin, first), grid=(1,),...  16.4 us
    ppermute x6, starting transfers between devices, moved(): return lax.ppermute(array, ('rows', 'cols'), pairs)  11.1 us
    ppermute x6, waiting for transfers between devices, moved(): return lax.ppermute(array, ('rows', 'cols'), pairs)  4.6 us
    pallas_call x1, Pallas kernels, norm_and_tile(): pl.pallas_call(functools.partial(norm_kernel, parts), in_specs=[pl.BlockS...  3.58 us
    ppermute x2, starting transfers between devices, shards(): others = [lax.ppermute(part, 'cols', swap) for part in normed[:2]]  2.13 us
    ppermute x1, starting transfers between devices, shards(): others.append(lax.ppermute(normed[2], 'cols', swap))  1.79 us
    pallas_call x1, Pallas kernels, project(): pl.pallas_call(functools.partial(project_kernel, len(parts)), in_specs=[v...  1.71 us
    pallas_call x1, Pallas kernels, assemble(): pl.pallas_call(assemble_kernel, in_specs=[smem, vmem, vmem, vmem], out_sp...  1.37 us
  transfers between devices with their start and end apart: 9, of which 2 were waited for; matrix products, arithmetic and copies ran while one was open for 3% of the time, Pallas kernels for 32%

profile of v3, /device:TPU:0, one launch (start us, length us, event | category | flops | bytes accessed | tf_op | source)
XLA Modules:
  0.0 44.8 jit_solution(4957078354136139939)
XLA Ops:
  0.0 0.0 copy-start.6
  0.0 0.0 copy-start.7
  0.0 3.6 %norm_and_tile.1 = (bf16[8,192,128]{2,1,0:T(8,128)(2,1)}, bf16[8,192,128]{2,1,0:T(8,128)(2,1)}, bf16[8,192,128]{2,1,0:T(8,128)(2,1)}, bf16[192,128]{1,0:T(8,128)(2,1)}) custom-call(bf16[24,192,128]{2,1,0:T(8,128)(2,1)} %pair_hbm.1, f32[1,128]{1,0:T(1,128)} %bitcast.27, f32[1,128]{1,0:T(1,128)} %bitcast.28, bf16[4,128]{1,0:T(4,128)(2,1)} %bitcast.25, ...), custom_call_target="tpu_custom_call" | custom-call | flops 1000000000 | bytes 10000000 | tf_op jit(solution)/shard_map/norm_and_tile/pallas_call | solution.py:86
  3.6 0.0 copy-start
  3.6 0.0 copy-start.1
  3.6 0.0 copy-start.2
  3.6 0.8 %collective-permute-start.4 = (bf16[192,128]{1,0:T(8,128)(2,1)}, bf16[192,128]{1,0:T(8,128)(2,1)S(1)}, u32[]{:S(2)}, u32[]{:S(2)}) collective-permute-start(bf16[192,128]{1,0:T(8,128)(2,1)} %get-tuple-element.32), channel_id=1, source_target_pairs={{1,16},{3,18},{5,20},{7,22},{9,24},{11,26},{13,28},{15,30},{16,1},... | collective-permute-start | bytes 147464 | tf_op jit(solution)/shard_map/ppermute | solution.py:372
  4.4 6.6 %collective-permute-start.2 = (bf16[192,128]{1,0:T(8,128)(2,1)}, bf16[192,128]{1,0:T(8,128)(2,1)S(1)}, u32[]{:S(2)}, u32[]{:S(2)}) collective-permute-start(bf16[192,128]{1,0:T(8,128)(2,1)} %get-tuple-element.32), channel_id=1, source_target_pairs={{0,16},{1,0},{2,18},{3,2},{4,20},{5,4},{6,22},{7,6},{8,24},{9,8},{... | collective-permute-start | bytes 147464 | tf_op jit(solution)/shard_map/ppermute | solution.py:372
  11.0 0.3 collective-permute-start
  11.3 0.0 copy-done.6
  11.3 0.1 copy.18
  11.4 0.1 copy.19
  11.6 2.3 %collective-permute-done.2 = bf16[192,128]{1,0:T(8,128)(2,1)S(1)} collective-permute-done((bf16[192,128]{1,0:T(8,128)(2,1)}, bf16[192,128]{1,0:T(8,128)(2,1)S(1)}, u32[]{:S(2)}, u32[]{:S(2)}) %collective-permute-start.2) | collective-permute-done | bytes 49184 | tf_op jit(solution)/shard_map/ppermute | solution.py:372
  13.9 0.8 %constant_dynamic-update-slice_fusion.4 = (bf16[8,192,128]{2,1,0:T(8,128)(2,1)S(1)}, bf16[1,192,128]{2,1,0:T(8,128)(2,1)S(1)}) fusion(bf16[192,128]{1,0:T(8,128)(2,1)} %get-tuple-element.32, bf16[192,128]{1,0:T(8,128)(2,1)S(1)} %collective-permute-done.2, pred[]{:T(512)S(6)} %eq.3), kind=kLoop, calls=%fused_computation.8 | loop fusion | flops 24575 | bytes 196609
  14.7 0.0 collective-permute-done.4
  14.8 1.6 %collective-permute-start.5 = (bf16[2,192,128]{2,1,0:T(8,128)(2,1)S(1)}, bf16[2,192,128]{2,1,0:T(8,128)(2,1)S(1)}, u32[]{:S(2)}, u32[]{:S(2)}) collective-permute-start(bf16[2,192,128]{2,1,0:T(8,128)(2,1)S(1)} %pad_maximum_fusion), channel_id=1, source_target_pairs={{0,4},{1,5},{2,6},{3,7},{4,0},{5,1},{6,2},{7,3},{8,12},{9,13},{10,... | collective-permute-start | bytes 294920 | tf_op jit(solution)/shard_map/ppermute | solution.py:372
  16.4 0.0 copy-done.7
  16.4 0.1 copy.16.refs_6_
  16.5 0.1 copy.17
  16.6 0.0 copy-done
  16.6 0.0 copy-done.1
  16.6 0.0 copy-done.2
  16.6 1.7 %project_own.1 = (bf16[24,192,128]{2,1,0:T(8,128)(2,1)S(1)}, bf16[24,128,192]{2,1,0:T(8,128)(2,1)S(1)}, bf16[24,128,256]{2,1,0:T(8,128)(2,1)S(1)}, f32[24,128,256]{2,1,0:T(8,128)S(1)}) custom-call(bf16[8,192,128]{2,1,0:T(8,128)(2,1)S(1)} %copy-done.2, bf16[8,192,128]{2,1,0:T(8,128)(2,1)S(1)} %copy-done.1, bf16[8,192,128]{2,1,0:T(8,128)(2,1)S(1)} %copy-done, ...), custom_call_target="tpu_custom_call" | custom-call | flops 1 | bytes 10 | tf_op jit(solution)/shard_map/project_own/pallas_call | solution.py:176
  18.4 1.6 %collective-permute-start.7 = (bf16[2,192,128]{2,1,0:T(8,128)(2,1)S(1)}, bf16[2,192,128]{2,1,0:T(8,128)(2,1)S(1)}, u32[]{:S(2)}, u32[]{:S(2)}) collective-permute-start(bf16[2,192,128]{2,1,0:T(8,128)(2,1)S(1)} %pad_maximum_fusion), channel_id=1, source_target_pairs={{0,12},{1,13},{2,14},{3,15},{4,8},{5,9},{6,10},{7,11},{8,4},{9,5},... | collective-permute-start | bytes 294920 | tf_op jit(solution)/shard_map/ppermute | solution.py:372
  19.9 0.5 %collective-permute-start.6 = (bf16[2,192,128]{2,1,0:T(8,128)(2,1)S(1)}, bf16[2,192,128]{2,1,0:T(8,128)(2,1)S(1)}, u32[]{:S(2)}, u32[]{:S(2)}) collective-permute-start(bf16[2,192,128]{2,1,0:T(8,128)(2,1)S(1)} %pad_maximum_fusion), channel_id=1, source_target_pairs={{0,8},{1,9},{2,10},{3,11},{4,12},{5,13},{6,14},{7,15},{8,0},{9,1},... | collective-permute-start | bytes 294920 | tf_op jit(solution)/shard_map/ppermute | solution.py:372
  20.4 1.9 %collective-permute-start.3 = (bf16[8,192,128]{2,1,0:T(8,128)(2,1)S(1)}, bf16[8,192,128]{2,1,0:T(8,128)(2,1)S(1)}, u32[]{:S(2)}, u32[]{:S(2)}) collective-permute-start(bf16[8,192,128]{2,1,0:T(8,128)(2,1)S(1)} %copy-done.1), channel_id=1, source_target_pairs={{0,1},{1,0},{2,3},{3,2},{4,5},{5,4},{6,7},{7,6},{8,9},{9,8},{10,11... | collective-permute-start | bytes 1179656 | tf_op jit(solution)/shard_map/ppermute | solution.py:500
  22.3 0.0 collective-permute-done.5
  22.3 2.3 %collective-permute-done.6 = bf16[2,192,128]{2,1,0:T(8,128)(2,1)S(1)} collective-permute-done((bf16[2,192,128]{2,1,0:T(8,128)(2,1)S(1)}, bf16[2,192,128]{2,1,0:T(8,128)(2,1)S(1)}, u32[]{:S(2)}, u32[]{:S(2)}) %collective-permute-start.6) | collective-permute-done | bytes 98336 | tf_op jit(solution)/shard_map/ppermute | solution.py:372
  24.6 0.0 collective-permute-done.7
  24.6 0.0 copy-start.5
  24.6 0.1 collective-permute-start.8
  24.7 0.0 collective-permute-done.other_ref
  24.7 0.5 %widen_rows.1 = (bf16[8,192,128]{2,1,0:T(8,128)(2,1)S(1)}, bf16[8,128,192]{2,1,0:T(8,128)(2,1)S(1)}) custom-call(bf16[8,192,128]{2,1,0:T(8,128)(2,1)S(1)} %collective-permute-done.other_ref, bf16[128,128]{1,0:T(8,128)(2,1)S(1)} %get-tuple-element.57.wk_ref.refs_3_.refs_2_, bf16[128,128]{1,0:T(8,128)(2,1)S(1)} %bitcast.16), custom_call_target="tpu_custom_call" | custom-call | flops 10000000000 | bytes 10 | tf_op jit(solution)/shard_map/widen_rows/pallas_call | solution.py:198
  25.2 0.0 copy-start.3
  25.2 0.0 copy-start.4
  25.2 1.8 %collective-permute-start.1 = (bf16[8,192,128]{2,1,0:T(8,128)(2,1)S(1)}, bf16[8,192,128]{2,1,0:T(8,128)(2,1)S(1)}, u32[]{:S(2)}, u32[]{:S(2)}) collective-permute-start(bf16[8,192,128]{2,1,0:T(8,128)(2,1)S(1)} %copy-done), channel_id=1, source_target_pairs={{0,1},{1,0},{2,3},{3,2},{4,5},{5,4},{6,7},{7,6},{8,9},{9,8},{10,11... | collective-permute-start | bytes 1179656 | tf_op jit(solution)/shard_map/ppermute | solution.py:503
  27.0 0.0 collective-permute-done.8.far_ref
  27.0 0.0 copy-done.5
  27.0 1.4 %assemble_bias.1.refs_6_.refs_8_ = f32[392,768]{1,0:T(8,128)S(1)} custom-call(s32[16]{0:T(128)S(1)} %shift-right-arithmetic_add_fusion.index_ref, bf16[8,192,128]{2,1,0:T(8,128)(2,1)S(1)} %constant_dynamic-update-slice_fusion.near_ref, bf16[8,192,128]{2,1,0:T(8,128)(2,1)S(1)} %collective-permute-done.8.far_ref, bf16[1024,768]{1,0:T(8,128)(2,1)S(1)} %copy-done.5), custom_call_target="tpu_custom_call" | custom-call | flops 1000000000 | bytes 4000000 | tf_op jit(solution)/shard_map/assemble_bias/pallas_call | solution.py:138
  28.4 0.0 copy-done.3
  28.4 0.0 copy-done.4
  28.4 5.3 %attend_rows.3.refs_0_ = bf16[24,192,128]{2,1,0:T(8,128)(2,1)} custom-call(bf16[8,192,128]{2,1,0:T(8,128)(2,1)S(1)} %get-tuple-element.35.refs_0_, bf16[8,128,192]{2,1,0:T(8,128)(2,1)S(1)} %get-tuple-element.36.refs_1_, bf16[24,192,128]{2,1,0:T(8,128)(2,1)S(1)} %get-tuple-element.42.refs_2_.refs_4_, ...), custom_call_target="tpu_custom_call" | custom-call | flops 10000000000 | bytes 10 | tf_op jit(solution)/shard_map/attend_rows/pallas_call | solution.py:343
  33.7 0.0 collective-permute-done.3.refs_1_
  33.7 5.6 %attend_rows.4.refs_0_ = bf16[24,192,128]{2,1,0:T(8,128)(2,1)} custom-call(bf16[24,192,128]{2,1,0:T(8,128)(2,1)} %attend_rows.3.refs_0_, bf16[8,192,128]{2,1,0:T(8,128)(2,1)S(1)} %collective-permute-done.3.refs_1_, bf16[128,128]{1,0:T(8,128)(2,1)S(1)} %get-tuple-element.57.wk_ref.refs_3_.refs_2_, ...), custom_call_target="tpu_custom_call", output_to_operand_aliasing={{}: (0, {})} | custom-call | flops 10000000000 | bytes 10 | tf_op jit(solution)/shard_map/attend_rows/pallas_call | solution.py:343
  39.3 0.0 collective-permute-done.1.refs_1_
  39.3 5.5 %attend_rows.5 = bf16[24,192,128]{2,1,0:T(8,128)(2,1)} custom-call(bf16[24,192,128]{2,1,0:T(8,128)(2,1)} %attend_rows.4.refs_0_, bf16[8,192,128]{2,1,0:T(8,128)(2,1)S(1)} %collective-permute-done.1.refs_1_, bf16[128,128]{1,0:T(8,128)(2,1)S(1)} %get-tuple-element.57.wk_ref.refs_3_.refs_2_, ...), custom_call_target="tpu_custom_call", output_to_operand_aliasing={{}: (0, {})} | custom-call | flops 10000000000 | bytes 10 | tf_op jit(solution)/shard_map/attend_rows/pallas_call | solution.py:343
  (8 shorter events, 0.1 us)
Async XLA Ops:
  0.0 11.3 %copy-start.6 = (bf16[128,512]{1,0:T(8,128)(2,1)S(1)}, bf16[128,512]{1,0:T(8,128)(2,1)}, u32[]{:S(2)}) copy-start(bf16[128,512]{1,0:T(8,128)(2,1)} %param.14) | copy-start | bytes 393220
  0.0 16.4 %copy-start.7 = (f32[128]{0:T(128)S(1)}, f32[128]{0:T(128)}, u32[]{:S(2)}) copy-start(f32[128]{0:T(128)} %param.15) | copy-start | bytes 1540
  3.6 13.0 %copy-start = (bf16[8,192,128]{2,1,0:T(8,128)(2,1)S(1)}, bf16[8,192,128]{2,1,0:T(8,128)(2,1)}, u32[]{:S(2)}) copy-start(bf16[8,192,128]{2,1,0:T(8,128)(2,1)} %get-tuple-element.31.refs_2_) | copy-start | bytes 1179652
  3.6 13.0 %copy-start.1 = (bf16[8,192,128]{2,1,0:T(8,128)(2,1)S(1)}, bf16[8,192,128]{2,1,0:T(8,128)(2,1)}, u32[]{:S(2)}) copy-start(bf16[8,192,128]{2,1,0:T(8,128)(2,1)} %get-tuple-element.34.refs_1_) | copy-start | bytes 1179652
  3.6 13.0 %copy-start.2 = (bf16[8,192,128]{2,1,0:T(8,128)(2,1)S(1)}, bf16[8,192,128]{2,1,0:T(8,128)(2,1)}, u32[]{:S(2)}) copy-start(bf16[8,192,128]{2,1,0:T(8,128)(2,1)} %get-tuple-element.29.refs_0_) | copy-start | bytes 1179652
  3.6 11.1 %collective-permute-start.4 = (bf16[192,128]{1,0:T(8,128)(2,1)}, bf16[192,128]{1,0:T(8,128)(2,1)S(1)}, u32[]{:S(2)}, u32[]{:S(2)}) collective-permute-start(bf16[192,128]{1,0:T(8,128)(2,1)} %get-tuple-element.32), channel_id=1, source_target_pairs={{1,16},{3,18},{5,20},{7,22},{9,24},{11,26},{13,28},{15,30},{16,1},... | collective-permute-start | bytes 147464 | tf_op jit(solution)/shard_map/ppermute | solution.py:372
  4.4 9.5 %collective-permute-start.2 = (bf16[192,128]{1,0:T(8,128)(2,1)}, bf16[192,128]{1,0:T(8,128)(2,1)S(1)}, u32[]{:S(2)}, u32[]{:S(2)}) collective-permute-start(bf16[192,128]{1,0:T(8,128)(2,1)} %get-tuple-element.32), channel_id=1, source_target_pairs={{0,16},{1,0},{2,18},{3,2},{4,20},{5,4},{6,22},{7,6},{8,24},{9,8},{... | collective-permute-start | bytes 147464 | tf_op jit(solution)/shard_map/ppermute | solution.py:372
  11.0 13.7 %collective-permute-start = (bf16[8,192,128]{2,1,0:T(8,128)(2,1)}, bf16[8,192,128]{2,1,0:T(8,128)(2,1)S(1)}, u32[]{:S(2)}, u32[]{:S(2)}) collective-permute-start(bf16[8,192,128]{2,1,0:T(8,128)(2,1)} %get-tuple-element.29.refs_0_), channel_id=1, source_target_pairs={{0,1},{1,0},{2,3},{3,2},{4,5},{5,4},{6,7},{7,6},{8,9},{9,8},{10,11... | collective-permute-start | bytes 1179656 | tf_op jit(solution)/shard_map/ppermute | solution.py:500
  14.8 7.5 %collective-permute-start.5 = (bf16[2,192,128]{2,1,0:T(8,128)(2,1)S(1)}, bf16[2,192,128]{2,1,0:T(8,128)(2,1)S(1)}, u32[]{:S(2)}, u32[]{:S(2)}) collective-permute-start(bf16[2,192,128]{2,1,0:T(8,128)(2,1)S(1)} %pad_maximum_fusion), channel_id=1, source_target_pairs={{0,4},{1,5},{2,6},{3,7},{4,0},{5,1},{6,2},{7,3},{8,12},{9,13},{10,... | collective-permute-start | bytes 294920 | tf_op jit(solution)/shard_map/ppermute | solution.py:372
  18.4 6.2 %collective-permute-start.7 = (bf16[2,192,128]{2,1,0:T(8,128)(2,1)S(1)}, bf16[2,192,128]{2,1,0:T(8,128)(2,1)S(1)}, u32[]{:S(2)}, u32[]{:S(2)}) collective-permute-start(bf16[2,192,128]{2,1,0:T(8,128)(2,1)S(1)} %pad_maximum_fusion), channel_id=1, source_target_pairs={{0,12},{1,13},{2,14},{3,15},{4,8},{5,9},{6,10},{7,11},{8,4},{9,5},... | collective-permute-start | bytes 294920 | tf_op jit(solution)/shard_map/ppermute | solution.py:372
  19.9 4.6 %collective-permute-start.6 = (bf16[2,192,128]{2,1,0:T(8,128)(2,1)S(1)}, bf16[2,192,128]{2,1,0:T(8,128)(2,1)S(1)}, u32[]{:S(2)}, u32[]{:S(2)}) collective-permute-start(bf16[2,192,128]{2,1,0:T(8,128)(2,1)S(1)} %pad_maximum_fusion), channel_id=1, source_target_pairs={{0,8},{1,9},{2,10},{3,11},{4,12},{5,13},{6,14},{7,15},{8,0},{9,1},... | collective-permute-start | bytes 294920 | tf_op jit(solution)/shard_map/ppermute | solution.py:372
  20.4 13.3 %collective-permute-start.3 = (bf16[8,192,128]{2,1,0:T(8,128)(2,1)S(1)}, bf16[8,192,128]{2,1,0:T(8,128)(2,1)S(1)}, u32[]{:S(2)}, u32[]{:S(2)}) collective-permute-start(bf16[8,192,128]{2,1,0:T(8,128)(2,1)S(1)} %copy-done.1), channel_id=1, source_target_pairs={{0,1},{1,0},{2,3},{3,2},{4,5},{5,4},{6,7},{7,6},{8,9},{9,8},{10,11... | collective-permute-start | bytes 1179656 | tf_op jit(solution)/shard_map/ppermute | solution.py:500
  24.6 2.4 %copy-start.5 = (bf16[1024,768]{1,0:T(8,128)(2,1)S(1)}, bf16[1024,768]{1,0:T(8,128)(2,1)}, u32[]{:S(2)}) copy-start(bf16[1024,768]{1,0:T(8,128)(2,1)} %constant.7.clone.order_ref) | copy-start | bytes 4718596
  24.6 2.4 %collective-permute-start.8 = (bf16[8,192,128]{2,1,0:T(8,128)(2,1)S(1)}, bf16[8,192,128]{2,1,0:T(8,128)(2,1)S(1)}, u32[]{:S(2)}, u32[]{:S(2)}) collective-permute-start(bf16[8,192,128]{2,1,0:T(8,128)(2,1)S(1)} %constant_dynamic-update-slice_fusion.near_ref), channel_id=1, source_target_pairs={{0,2},{1,3},{2,0},{3,1},{4,6},{5,7},{6,4},{7,5},{8,10},{9,11},{10,... | collective-permute-start | bytes 1179656 | tf_op jit(solution)/shard_map/ppermute | solution.py:372
  25.2 3.2 %copy-start.3 = (bf16[128,128]{1,0:T(8,128)(2,1)S(1)}, bf16[128,128]{1,0:T(8,128)(2,1)}, u32[]{:S(2)}) copy-start(bf16[128,128]{1,0:T(8,128)(2,1)} %refs_9_.3) | copy-start | bytes 98308
  25.2 3.2 %copy-start.4 = (f32[128]{0:T(128)S(1)}, f32[128]{0:T(128)}, u32[]{:S(2)}) copy-start(f32[128]{0:T(128)} %param.18) | copy-start | bytes 1540
  25.2 14.1 %collective-permute-start.1 = (bf16[8,192,128]{2,1,0:T(8,128)(2,1)S(1)}, bf16[8,192,128]{2,1,0:T(8,128)(2,1)S(1)}, u32[]{:S(2)}, u32[]{:S(2)}) collective-permute-start(bf16[8,192,128]{2,1,0:T(8,128)(2,1)S(1)} %copy-done), channel_id=1, source_target_pairs={{0,1},{1,0},{2,3},{3,2},{4,5},{5,4},{6,7},{7,6},{8,9},{9,8},{10,11... | collective-permute-start | bytes 1179656 | tf_op jit(solution)/shard_map/ppermute | solution.py:503

commit v4 on v3

--- a/solution.py
+++ b/solution.py
@@ -373,9 +373,9 @@
 
 
 def spread_tiles(tile, z_hi, x, part):
+    across = moved(tile, lambda a, b, y, c, x: None if a == x else (1 - a, b, y, c, 1 - x))
     straight = moved(tile, lambda a, b, y, c, x: (1 - a, b, y, c, x) if a == x else (a, b, y, c, 1 - x))
-    across = moved(tile, lambda a, b, y, c, x: None if a == x else (1 - a, b, y, c, 1 - x))
-    straight, part = lax.optimization_barrier((straight, part))
+    across, part = lax.optimization_barrier((across, part))
     home = z_hi == x
     pair = jnp.stack((jnp.where(home, tile, straight), jnp.where(home, straight, across)))
     near = [pair]

time: 45 us -> 43.9 us (0.976)
  waiting for transfers between devices: 4.61 us -> 2.63 us
  starting transfers between devices: 15 us -> 15.9 us
    ppermute x2, starting transfers between devices: 2.13 us -> 5.98 us  [shards(): others = [lax.ppermute(part, 'cols', swap) for part in normed[:2]]]
    ppermute x6, starting transfers between devices: 11.1 us -> 8.43 us  [moved(): return lax.ppermute(array, ('rows', 'cols'), pairs)]
    ppermute x6, waiting for transfers between devices: 4.6 us -> 2.45 us  [moved(): return lax.ppermute(array, ('rows', 'cols'), pairs)]
  transfers between devices with their start and end apart: 9 -> 9, of which waited for: 2 -> 2; matrix products, arithmetic and copies ran while one was open for 3% -> 3% of each run, Pallas kernels for 32% -> 33%
where the time goes in v4:
time: 43.9 us; the launch traced here: 43.7 us
  Pallas kernels  23.5 us (54%)
  starting transfers between devices  15.9 us (36%)
  waiting for transfers between devices  2.63 us (6%)
  other arithmetic  0.89 us (2%)
  local copies, waits for them, and re-layouts  0.56 us (1%)
    pallas_call x3, Pallas kernels, attend(): pl.pallas_call(functools.partial(attend_kernel, begin, first), grid=(1,),...  16.4 us
    ppermute x6, starting transfers between devices, moved(): return lax.ppermute(array, ('rows', 'cols'), pairs)  8.43 us
    ppermute x2, starting transfers between devices, shards(): others = [lax.ppermute(part, 'cols', swap) for part in normed[:2]]  5.98 us
    pallas_call x1, Pallas kernels, norm_and_tile(): pl.pallas_call(functools.partial(norm_kernel, parts), in_specs=[pl.BlockS...  3.58 us
    ppermute x6, waiting for transfers between devices, moved(): return lax.ppermute(array, ('rows', 'cols'), pairs)  2.45 us
    pallas_call x1, Pallas kernels, project(): pl.pallas_call(functools.partial(project_kernel, len(parts)), in_specs=[v...  1.71 us
    ppermute x1, starting transfers between devices, shards(): others.append(lax.ppermute(normed[2], 'cols', swap))  1.47 us
    pallas_call x1, Pallas kernels, assemble(): pl.pallas_call(assemble_kernel, in_specs=[smem, vmem, vmem, vmem], out_sp...  1.37 us
  transfers between devices with their start and end apart: 9, of which 2 were waited for; matrix products, arithmetic and copies ran while one was open for 3% of the time, Pallas kernels for 33%

profile of v4, /device:TPU:0, one launch (start us, length us, event | category | flops | bytes accessed | tf_op | source)
XLA Modules:
  0.0 43.7 jit_solution(1418737849231808554)
XLA Ops:
  0.0 0.0 copy-start.6
  0.0 0.0 copy-start.7
  0.0 3.6 %norm_and_tile.1 = (bf16[8,192,128]{2,1,0:T(8,128)(2,1)}, bf16[8,192,128]{2,1,0:T(8,128)(2,1)}, bf16[8,192,128]{2,1,0:T(8,128)(2,1)}, bf16[192,128]{1,0:T(8,128)(2,1)}) custom-call(bf16[24,192,128]{2,1,0:T(8,128)(2,1)} %pair_hbm.1, f32[1,128]{1,0:T(1,128)} %bitcast.27, f32[1,128]{1,0:T(1,128)} %bitcast.28, bf16[4,128]{1,0:T(4,128)(2,1)} %bitcast.25, ...), custom_call_target="tpu_custom_call" | custom-call | flops 1000000000 | bytes 10000000 | tf_op jit(solution)/shard_map/norm_and_tile/pallas_call | solution.py:86
  3.6 0.0 copy-start
  3.6 0.0 copy-start.1
  3.6 0.0 copy-start.2
  3.6 4.1 %collective-permute-start.4 = (bf16[192,128]{1,0:T(8,128)(2,1)}, bf16[192,128]{1,0:T(8,128)(2,1)S(1)}, u32[]{:S(2)}, u32[]{:S(2)}) collective-permute-start(bf16[192,128]{1,0:T(8,128)(2,1)} %get-tuple-element.32), channel_id=1, source_target_pairs={{0,16},{1,0},{2,18},{3,2},{4,20},{5,4},{6,22},{7,6},{8,24},{9,8},{... | collective-permute-start | bytes 147464 | tf_op jit(solution)/shard_map/ppermute | solution.py:372
  7.7 0.7 %collective-permute-start.2 = (bf16[192,128]{1,0:T(8,128)(2,1)}, bf16[192,128]{1,0:T(8,128)(2,1)S(1)}, u32[]{:S(2)}, u32[]{:S(2)}) collective-permute-start(bf16[192,128]{1,0:T(8,128)(2,1)} %get-tuple-element.32), channel_id=1, source_target_pairs={{1,16},{3,18},{5,20},{7,22},{9,24},{11,26},{13,28},{15,30},{16,1},... | collective-permute-start | bytes 147464 | tf_op jit(solution)/shard_map/ppermute | solution.py:372
  8.4 4.3 %collective-permute-start = (bf16[8,192,128]{2,1,0:T(8,128)(2,1)}, bf16[8,192,128]{2,1,0:T(8,128)(2,1)S(1)}, u32[]{:S(2)}, u32[]{:S(2)}) collective-permute-start(bf16[8,192,128]{2,1,0:T(8,128)(2,1)} %get-tuple-element.29.refs_0_), channel_id=1, source_target_pairs={{0,1},{1,0},{2,3},{3,2},{4,5},{5,4},{6,7},{7,6},{8,9},{9,8},{10,11... | collective-permute-start | bytes 1179656 | tf_op jit(solution)/shard_map/ppermute | solution.py:500
  12.6 0.0 copy-done.6
  12.7 0.1 copy.18
  12.8 0.1 copy.19
  12.9 0.0 collective-permute-done.2
  12.9 0.0 collective-permute-done.4
  13.0 0.8 %constant_dynamic-update-slice_fusion.4 = (bf16[8,192,128]{2,1,0:T(8,128)(2,1)S(1)}, bf16[1,192,128]{2,1,0:T(8,128)(2,1)S(1)}) fusion(bf16[192,128]{1,0:T(8,128)(2,1)} %get-tuple-element.32, bf16[192,128]{1,0:T(8,128)(2,1)S(1)} %collective-permute-done.4, pred[]{:T(512)S(6)} %eq.3), kind=kLoop, calls=%fused_computation.8 | loop fusion | flops 24575 | bytes 196609
  13.8 1.6 %collective-permute-start.5 = (bf16[2,192,128]{2,1,0:T(8,128)(2,1)S(1)}, bf16[2,192,128]{2,1,0:T(8,128)(2,1)S(1)}, u32[]{:S(2)}, u32[]{:S(2)}) collective-permute-start(bf16[2,192,128]{2,1,0:T(8,128)(2,1)S(1)} %pad_maximum_fusion), channel_id=1, source_target_pairs={{0,4},{1,5},{2,6},{3,7},{4,0},{5,1},{6,2},{7,3},{8,12},{9,13},{10,... | collective-permute-start | bytes 294920 | tf_op jit(solution)/shard_map/ppermute | solution.py:372
  15.4 0.0 copy-done.7
  15.4 0.1 copy.16.refs_6_
  15.5 0.1 copy.17
  15.7 0.0 copy-done
  15.7 0.0 copy-done.1
  15.7 0.0 copy-done.2
  15.7 1.7 %project_own.1 = (bf16[24,192,128]{2,1,0:T(8,128)(2,1)S(1)}, bf16[24,128,192]{2,1,0:T(8,128)(2,1)S(1)}, bf16[24,128,256]{2,1,0:T(8,128)(2,1)S(1)}, f32[24,128,256]{2,1,0:T(8,128)S(1)}) custom-call(bf16[8,192,128]{2,1,0:T(8,128)(2,1)S(1)} %copy-done.2, bf16[8,192,128]{2,1,0:T(8,128)(2,1)S(1)} %copy-done.1, bf16[8,192,128]{2,1,0:T(8,128)(2,1)S(1)} %copy-done, ...), custom_call_target="tpu_custom_call" | custom-call | flops 1 | bytes 10 | tf_op jit(solution)/shard_map/project_own/pallas_call | solution.py:176
  17.4 1.6 %collective-permute-start.7 = (bf16[2,192,128]{2,1,0:T(8,128)(2,1)S(1)}, bf16[2,192,128]{2,1,0:T(8,128)(2,1)S(1)}, u32[]{:S(2)}, u32[]{:S(2)}) collective-permute-start(bf16[2,192,128]{2,1,0:T(8,128)(2,1)S(1)} %pad_maximum_fusion), channel_id=1, source_target_pairs={{0,12},{1,13},{2,14},{3,15},{4,8},{5,9},{6,10},{7,11},{8,4},{9,5},... | collective-permute-start | bytes 294920 | tf_op jit(solution)/shard_map/ppermute | solution.py:372
  19.0 0.4 %collective-permute-start.6 = (bf16[2,192,128]{2,1,0:T(8,128)(2,1)S(1)}, bf16[2,192,128]{2,1,0:T(8,128)(2,1)S(1)}, u32[]{:S(2)}, u32[]{:S(2)}) collective-permute-start(bf16[2,192,128]{2,1,0:T(8,128)(2,1)S(1)} %pad_maximum_fusion), channel_id=1, source_target_pairs={{0,8},{1,9},{2,10},{3,11},{4,12},{5,13},{6,14},{7,15},{8,0},{9,1},... | collective-permute-start | bytes 294920 | tf_op jit(solution)/shard_map/ppermute | solution.py:372
  19.5 1.7 %collective-permute-start.3 = (bf16[8,192,128]{2,1,0:T(8,128)(2,1)S(1)}, bf16[8,192,128]{2,1,0:T(8,128)(2,1)S(1)}, u32[]{:S(2)}, u32[]{:S(2)}) collective-permute-start(bf16[8,192,128]{2,1,0:T(8,128)(2,1)S(1)} %copy-done.1), channel_id=1, source_target_pairs={{0,1},{1,0},{2,3},{3,2},{4,5},{5,4},{6,7},{7,6},{8,9},{9,8},{10,11... | collective-permute-start | bytes 1179656 | tf_op jit(solution)/shard_map/ppermute | solution.py:500
  21.2 0.0 collective-permute-done.5
  21.2 2.4 %collective-permute-done.6 = bf16[2,192,128]{2,1,0:T(8,128)(2,1)S(1)} collective-permute-done((bf16[2,192,128]{2,1,0:T(8,128)(2,1)S(1)}, bf16[2,192,128]{2,1,0:T(8,128)(2,1)S(1)}, u32[]{:S(2)}, u32[]{:S(2)}) %collective-permute-start.6) | collective-permute-done | bytes 98336 | tf_op jit(solution)/shard_map/ppermute | solution.py:372
  23.6 0.0 collective-permute-done.7
  23.7 0.0 copy-start.5
  23.7 0.1 collective-permute-start.8
  23.8 0.0 collective-permute-done.other_ref
  23.8 0.5 %widen_rows.1 = (bf16[8,192,128]{2,1,0:T(8,128)(2,1)S(1)}, bf16[8,128,192]{2,1,0:T(8,128)(2,1)S(1)}) custom-call(bf16[8,192,128]{2,1,0:T(8,128)(2,1)S(1)} %collective-permute-done.other_ref, bf16[128,128]{1,0:T(8,128)(2,1)S(1)} %get-tuple-element.57.wk_ref.refs_3_.refs_2_, bf16[128,128]{1,0:T(8,128)(2,1)S(1)} %bitcast.16), custom_call_target="tpu_custom_call" | custom-call | flops 10000000000 | bytes 10 | tf_op jit(solution)/shard_map/widen_rows/pallas_call | solution.py:198
  24.3 0.0 copy-start.3
  24.3 0.0 copy-start.4
  24.3 1.5 %collective-permute-start.1 = (bf16[8,192,128]{2,1,0:T(8,128)(2,1)S(1)}, bf16[8,192,128]{2,1,0:T(8,128)(2,1)S(1)}, u32[]{:S(2)}, u32[]{:S(2)}) collective-permute-start(bf16[8,192,128]{2,1,0:T(8,128)(2,1)S(1)} %copy-done), channel_id=1, source_target_pairs={{0,1},{1,0},{2,3},{3,2},{4,5},{5,4},{6,7},{7,6},{8,9},{9,8},{10,11... | collective-permute-start | bytes 1179656 | tf_op jit(solution)/shard_map/ppermute | solution.py:503
  25.8 0.0 collective-permute-done.8.far_ref
  25.8 0.0 copy-done.5
  25.8 1.4 %assemble_bias.1.refs_6_.refs_8_ = f32[392,768]{1,0:T(8,128)S(1)} custom-call(s32[16]{0:T(128)S(1)} %shift-right-arithmetic_add_fusion.index_ref, bf16[8,192,128]{2,1,0:T(8,128)(2,1)S(1)} %constant_dynamic-update-slice_fusion.near_ref, bf16[8,192,128]{2,1,0:T(8,128)(2,1)S(1)} %collective-permute-done.8.far_ref, bf16[1024,768]{1,0:T(8,128)(2,1)S(1)} %copy-done.5), custom_call_target="tpu_custom_call" | custom-call | flops 1000000000 | bytes 4000000 | tf_op jit(solution)/shard_map/assemble_bias/pallas_call | solution.py:138
  27.1 0.0 copy-done.3
  27.1 0.0 copy-done.4
  27.2 5.3 %attend_rows.3.refs_0_ = bf16[24,192,128]{2,1,0:T(8,128)(2,1)} custom-call(bf16[8,192,128]{2,1,0:T(8,128)(2,1)S(1)} %get-tuple-element.35.refs_0_, bf16[8,128,192]{2,1,0:T(8,128)(2,1)S(1)} %get-tuple-element.36.refs_1_, bf16[24,192,128]{2,1,0:T(8,128)(2,1)S(1)} %get-tuple-element.42.refs_2_.refs_4_, ...), custom_call_target="tpu_custom_call" | custom-call | flops 10000000000 | bytes 10 | tf_op jit(solution)/shard_map/attend_rows/pallas_call | solution.py:343
  32.4 0.0 collective-permute-done.3.refs_1_
  32.4 5.6 %attend_rows.4.refs_0_ = bf16[24,192,128]{2,1,0:T(8,128)(2,1)} custom-call(bf16[24,192,128]{2,1,0:T(8,128)(2,1)} %attend_rows.3.refs_0_, bf16[8,192,128]{2,1,0:T(8,128)(2,1)S(1)} %collective-permute-done.3.refs_1_, bf16[128,128]{1,0:T(8,128)(2,1)S(1)} %get-tuple-element.57.wk_ref.refs_3_.refs_2_, ...), custom_call_target="tpu_custom_call", output_to_operand_aliasing={{}: (0, {})} | custom-call | flops 10000000000 | bytes 10 | tf_op jit(solution)/shard_map/attend_rows/pallas_call | solution.py:343
  38.1 0.2 collective-permute-done.1.refs_1_
  38.3 5.5 %attend_rows.5 = bf16[24,192,128]{2,1,0:T(8,128)(2,1)} custom-call(bf16[24,192,128]{2,1,0:T(8,128)(2,1)} %attend_rows.4.refs_0_, bf16[8,192,128]{2,1,0:T(8,128)(2,1)S(1)} %collective-permute-done.1.refs_1_, bf16[128,128]{1,0:T(8,128)(2,1)S(1)} %get-tuple-element.57.wk_ref.refs_3_.refs_2_, ...), custom_call_target="tpu_custom_call", output_to_operand_aliasing={{}: (0, {})} | custom-call | flops 10000000000 | bytes 10 | tf_op jit(solution)/shard_map/attend_rows/pallas_call | solution.py:343
  (8 shorter events, 0.1 us)
Async XLA Ops:
  0.0 12.6 %copy-start.6 = (bf16[128,512]{1,0:T(8,128)(2,1)S(1)}, bf16[128,512]{1,0:T(8,128)(2,1)}, u32[]{:S(2)}) copy-start(bf16[128,512]{1,0:T(8,128)(2,1)} %param.14) | copy-start | bytes 393220
  0.0 15.4 %copy-start.7 = (f32[128]{0:T(128)S(1)}, f32[128]{0:T(128)}, u32[]{:S(2)}) copy-start(f32[128]{0:T(128)} %param.15) | copy-start | bytes 1540
  3.6 12.1 %copy-start = (bf16[8,192,128]{2,1,0:T(8,128)(2,1)S(1)}, bf16[8,192,128]{2,1,0:T(8,128)(2,1)}, u32[]{:S(2)}) copy-start(bf16[8,192,128]{2,1,0:T(8,128)(2,1)} %get-tuple-element.31.refs_2_) | copy-start | bytes 1179652
  3.6 12.1 %copy-start.1 = (bf16[8,192,128]{2,1,0:T(8,128)(2,1)S(1)}, bf16[8,192,128]{2,1,0:T(8,128)(2,1)}, u32[]{:S(2)}) copy-start(bf16[8,192,128]{2,1,0:T(8,128)(2,1)} %get-tuple-element.34.refs_1_) | copy-start | bytes 1179652
  3.6 12.1 %copy-start.2 = (bf16[8,192,128]{2,1,0:T(8,128)(2,1)S(1)}, bf16[8,192,128]{2,1,0:T(8,128)(2,1)}, u32[]{:S(2)}) copy-start(bf16[8,192,128]{2,1,0:T(8,128)(2,1)} %get-tuple-element.29.refs_0_) | copy-start | bytes 1179652
  3.6 9.3 %collective-permute-start.4 = (bf16[192,128]{1,0:T(8,128)(2,1)}, bf16[192,128]{1,0:T(8,128)(2,1)S(1)}, u32[]{:S(2)}, u32[]{:S(2)}) collective-permute-start(bf16[192,128]{1,0:T(8,128)(2,1)} %get-tuple-element.32), channel_id=1, source_target_pairs={{0,16},{1,0},{2,18},{3,2},{4,20},{5,4},{6,22},{7,6},{8,24},{9,8},{... | collective-permute-start | bytes 147464 | tf_op jit(solution)/shard_map/ppermute | solution.py:372
  7.7 5.2 %collective-permute-start.2 = (bf16[192,128]{1,0:T(8,128)(2,1)}, bf16[192,128]{1,0:T(8,128)(2,1)S(1)}, u32[]{:S(2)}, u32[]{:S(2)}) collective-permute-start(bf16[192,128]{1,0:T(8,128)(2,1)} %get-tuple-element.32), channel_id=1, source_target_pairs={{1,16},{3,18},{5,20},{7,22},{9,24},{11,26},{13,28},{15,30},{16,1},... | collective-permute-start | bytes 147464 | tf_op jit(solution)/shard_map/ppermute | solution.py:372
  8.4 15.4 %collective-permute-start = (bf16[8,192,128]{2,1,0:T(8,128)(2,1)}, bf16[8,192,128]{2,1,0:T(8,128)(2,1)S(1)}, u32[]{:S(2)}, u32[]{:S(2)}) collective-permute-start(bf16[8,192,128]{2,1,0:T(8,128)(2,1)} %get-tuple-element.29.refs_0_), channel_id=1, source_target_pairs={{0,1},{1,0},{2,3},{3,2},{4,5},{5,4},{6,7},{7,6},{8,9},{9,8},{10,11... | collective-permute-start | bytes 1179656 | tf_op jit(solution)/shard_map/ppermute | solution.py:500
  13.8 7.3 %collective-permute-start.5 = (bf16[2,192,128]{2,1,0:T(8,128)(2,1)S(1)}, bf16[2,192,128]{2,1,0:T(8,128)(2,1)S(1)}, u32[]{:S(2)}, u32[]{:S(2)}) collective-permute-start(bf16[2,192,128]{2,1,0:T(8,128)(2,1)S(1)} %pad_maximum_fusion), channel_id=1, source_target_pairs={{0,4},{1,5},{2,6},{3,7},{4,0},{5,1},{6,2},{7,3},{8,12},{9,13},{10,... | collective-permute-start | bytes 294920 | tf_op jit(solution)/shard_map/ppermute | solution.py:372
  17.4 6.2 %collective-permute-start.7 = (bf16[2,192,128]{2,1,0:T(8,128)(2,1)S(1)}, bf16[2,192,128]{2,1,0:T(8,128)(2,1)S(1)}, u32[]{:S(2)}, u32[]{:S(2)}) collective-permute-start(bf16[2,192,128]{2,1,0:T(8,128)(2,1)S(1)} %pad_maximum_fusion), channel_id=1, source_target_pairs={{0,12},{1,13},{2,14},{3,15},{4,8},{5,9},{6,10},{7,11},{8,4},{9,5},... | collective-permute-start | bytes 294920 | tf_op jit(solution)/shard_map/ppermute | solution.py:372
  19.0 4.6 %collective-permute-start.6 = (bf16[2,192,128]{2,1,0:T(8,128)(2,1)S(1)}, bf16[2,192,128]{2,1,0:T(8,128)(2,1)S(1)}, u32[]{:S(2)}, u32[]{:S(2)}) collective-permute-start(bf16[2,192,128]{2,1,0:T(8,128)(2,1)S(1)} %pad_maximum_fusion), channel_id=1, source_target_pairs={{0,8},{1,9},{2,10},{3,11},{4,12},{5,13},{6,14},{7,15},{8,0},{9,1},... | collective-permute-start | bytes 294920 | tf_op jit(solution)/shard_map/ppermute | solution.py:372
  19.5 13.0 %collective-permute-start.3 = (bf16[8,192,128]{2,1,0:T(8,128)(2,1)S(1)}, bf16[8,192,128]{2,1,0:T(8,128)(2,1)S(1)}, u32[]{:S(2)}, u32[]{:S(2)}) collective-permute-start(bf16[8,192,128]{2,1,0:T(8,128)(2,1)S(1)} %copy-done.1), channel_id=1, source_target_pairs={{0,1},{1,0},{2,3},{3,2},{4,5},{5,4},{6,7},{7,6},{8,9},{9,8},{10,11... | collective-permute-start | bytes 1179656 | tf_op jit(solution)/shard_map/ppermute | solution.py:500
  23.7 2.1 %copy-start.5 = (bf16[1024,768]{1,0:T(8,128)(2,1)S(1)}, bf16[1024,768]{1,0:T(8,128)(2,1)}, u32[]{:S(2)}) copy-start(bf16[1024,768]{1,0:T(8,128)(2,1)} %constant.7.clone.order_ref) | copy-start | bytes 4718596
  23.7 2.1 %collective-permute-start.8 = (bf16[8,192,128]{2,1,0:T(8,128)(2,1)S(1)}, bf16[8,192,128]{2,1,0:T(8,128)(2,1)S(1)}, u32[]{:S(2)}, u32[]{:S(2)}) collective-permute-start(bf16[8,192,128]{2,1,0:T(8,128)(2,1)S(1)} %constant_dynamic-update-slice_fusion.near_ref), channel_id=1, source_target_pairs={{0,2},{1,3},{2,0},{3,1},{4,6},{5,7},{6,4},{7,5},{8,10},{9,11},{10,... | collective-permute-start | bytes 1179656 | tf_op jit(solution)/shard_map/ppermute | solution.py:372
  24.3 2.9 %copy-start.3 = (bf16[128,128]{1,0:T(8,128)(2,1)S(1)}, bf16[128,128]{1,0:T(8,128)(2,1)}, u32[]{:S(2)}) copy-start(bf16[128,128]{1,0:T(8,128)(2,1)} %refs_9_.3) | copy-start | bytes 98308
  24.3 2.9 %copy-start.4 = (f32[128]{0:T(128)S(1)}, f32[128]{0:T(128)}, u32[]{:S(2)}) copy-start(f32[128]{0:T(128)} %param.18) | copy-start | bytes 1540
  24.3 14.0 %collective-permute-start.1 = (bf16[8,192,128]{2,1,0:T(8,128)(2,1)S(1)}, bf16[8,192,128]{2,1,0:T(8,128)(2,1)S(1)}, u32[]{:S(2)}, u32[]{:S(2)}) collective-permute-start(bf16[8,192,128]{2,1,0:T(8,128)(2,1)S(1)} %copy-done), channel_id=1, source_target_pairs={{0,1},{1,0},{2,3},{3,2},{4,5},{5,4},{6,7},{7,6},{8,9},{9,8},{10,11... | collective-permute-start | bytes 1179656 | tf_op jit(solution)/shard_map/ppermute | solution.py:503

commit v5 on v4

--- a/solution.py
+++ b/solution.py
@@ -257,46 +257,45 @@
         v_both[row] = jnp.concatenate((v_ref[begin + row], values), 1)
         yield
 
-    def score(row, slot, shift):
-        for tile in range(6):
+    def score(row, pair, slot, shift):
+        for tile in range(3 * pair, 3 * pair + 3):
             query = query_tile(row, tile)
             both = jnp.concatenate((k_ref[begin + row], k_other[row]), 0)
             part = dot(both, query) + bias_ref[:keys, lanes[tile]]
             if shift:
                 part = part + MISSING
-            scores[slot][:, lanes[tile]] = part
-            tops[slot][0:1, lanes[tile]] = jnp.max(part, axis=0, keepdims=True)
+            scores[slot][:, lanes[tile % 3]] = part
+            tops[slot][0:1, lanes[tile % 3]] = jnp.max(part, axis=0, keepdims=True)
             yield
 
     def soften(slot):
-        for tile in range(6):
+        for tile in range(3):
             part = jnp.exp(scores[slot][:, lanes[tile]] - tops[slot][0:1, lanes[tile]])
             shares[slot][0:1, lanes[tile]] = 1.0 / jnp.sum(part, axis=0, keepdims=True)
             weights[slot][:, lanes[tile]] = part.astype(jnp.bfloat16)
             yield
 
-    def mix(row, slot):
+    def mix(row, pair, slot, gated):
         mixed = []
-        for tile in range(6):
-            head, tail = TILE_ROWS[tile]
+        for tile in range(3):
+            head, tail = TILE_ROWS[3 * pair + tile]
             part = dot(v_both[row, head:tail], weights[slot][:, lanes[tile]])
             mixed.append(part * shares[slot][0:1, lanes[tile]])
             yield
-        gated = []
-        for pair in range(2):
-            one, two, both = mixed[3 * pair : 3 * pair + 3]
-            gate = g_ref[begin + row, 64 * pair : 64 * pair + 32]
-            rest = jnp.where(low, both[:32] * gate[:, LANES:], 0.0)
-            gated.append(jnp.concatenate((one * gate[:, :LANES], rest), 1))
-            gate = g_ref[begin + row, 64 * pair + 32 : 64 * pair + 64]
-            rest = jnp.where(low, 0.0, both[32:] * gate[:, LANES:])
-            gated.append(jnp.concatenate((two * gate[:, :LANES], rest), 1))
-        update = dot(jnp.concatenate(gated, 0).astype(jnp.bfloat16), wo_ref[...], TN)
-        rest = cols - LANES
-        update = jnp.concatenate(
-            (update[:LANES], update[LANES : LANES + rest] + update[LANES + rest :]), 0
-        )
-        out_ref[row] = (update + ob_ref[...]).astype(jnp.bfloat16)
+        one, two, both = mixed
+        gate = g_ref[begin + row, 64 * pair : 64 * pair + 32]
+        rest = jnp.where(low, both[:32] * gate[:, LANES:], 0.0)
+        gated.append(jnp.concatenate((one * gate[:, :LANES], rest), 1))
+        gate = g_ref[begin + row, 64 * pair + 32 : 64 * pair + 64]
+        rest = jnp.where(low, 0.0, both[32:] * gate[:, LANES:])
+        gated.append(jnp.concatenate((two * gate[:, :LANES], rest), 1))
+        if pair:
+            update = dot(jnp.concatenate(gated, 0).astype(jnp.bfloat16), wo_ref[...], TN)
+            rest = cols - LANES
+            update = jnp.concatenate(
+                (update[:LANES], update[LANES : LANES + rest] + update[LANES + rest :]), 0
+            )
+            out_ref[row] = (update + ob_ref[...]).astype(jnp.bfloat16)
         yield
 
     def run(*stages):
@@ -309,25 +308,30 @@
     @pl.when(present > 0.5)
     def _():
         run(widen(0))
-        for step in range(rows + 2):
+        gated = [[] for _ in range(rows)]
+        units = [(row, pair) for row in range(rows) for pair in range(2)]
+        for step in range(len(units) + 2):
             stages = []
             if step >= 2:
-                stages.append(mix(step - 2, step % 2))
-            if 1 <= step <= rows:
+                row, pair = units[step - 2]
+                stages.append(mix(row, pair, step % 2, gated[row]))
+            if 1 <= step <= len(units):
                 stages.append(soften((step - 1) % 2))
-            if step < rows:
-                stages.append(score(step, step % 2, False))
-            if step + 1 < rows:
-                stages.append(widen(step + 1))
+            if step < len(units):
+                stages.append(score(*units[step], step % 2, False))
+                if units[step][1] == 0 and units[step][0] + 1 < rows:
+                    stages.append(widen(units[step][0] + 1))
             run(*stages)
 
     @pl.when(present <= 0.5)
     def _():
         def one(row, carry):
             run(widen(row))
-            run(score(row, 0, True))
-            run(soften(0))
-            run(mix(row, 0))
+            gated = []
+            for pair in range(2):
+                run(score(row, pair, 0, True))
+                run(soften(0))
+                run(mix(row, pair, 0, gated))
             return carry
 
         lax.fori_loop(0, rows, one, 0)
@@ -348,9 +352,9 @@
         out_shape=jax.ShapeDtypeStruct((total, cols, LANES), jnp.bfloat16),
         scratch_shapes=[pltpu.VMEM((rows, LANES, keys), jnp.bfloat16)]
         + own_keys
-        + [pltpu.VMEM((keys, lanes), jnp.float32)] * 2
-        + [pltpu.VMEM((keys, lanes), jnp.bfloat16)] * 2
-        + [pltpu.VMEM((8, lanes), jnp.float32)] * 4,
+        + [pltpu.VMEM((keys, lanes // 2), jnp.float32)] * 2
+        + [pltpu.VMEM((keys, lanes // 2), jnp.bfloat16)] * 2
+        + [pltpu.VMEM((8, lanes // 2), jnp.float32)] * 4,
         input_output_aliases={} if first else {0: 0},
         compiler_params=pltpu.CompilerParams(vmem_limit_bytes=24 << 20),
         cost_estimate=pl.CostEstimate(flops=10**10, bytes_accessed=10, transcendentals=0),

time: 43.9 us -> 43.7 us (level)
  Pallas kernels: 23.5 us -> 22.8 us
  waiting for transfers between devices: 2.63 us -> 3.1 us
    pallas_call x3, Pallas kernels: 16.4 us -> 15.7 us  [attend(): pl.pallas_call(functools.partial(attend_kernel, begin, first), grid=(1,),...]
    ppermute x1, waiting for transfers between devices: 0.18 us -> 0.65 us  [shards(): others.append(lax.ppermute(normed[2], 'cols', swap))]
  transfers between devices with their start and end apart: 9 -> 9, of which waited for: 2 -> 2; matrix products, arithmetic and copies ran while one was open for 3% -> 3% of each run, Pallas kernels for 33% -> 32%
where the time goes in v5:
time: 43.7 us; the launch traced here: 43.5 us
  Pallas kernels  22.8 us (52%)
  starting transfers between devices  15.9 us (36%)
  waiting for transfers between devices  3.1 us (7%)
  other arithmetic  0.89 us (2%)
  local copies, waits for them, and re-layouts  0.56 us (1%)
    pallas_call x3, Pallas kernels, attend(): pl.pallas_call(functools.partial(attend_kernel, begin, first), grid=(1,),...  15.7 us
    ppermute x6, starting transfers between devices, moved(): return lax.ppermute(array, ('rows', 'cols'), pairs)  8.43 us
    ppermute x2, starting transfers between devices, shards(): others = [lax.ppermute(part, 'cols', swap) for part in normed[:2]]  5.98 us
    pallas_call x1, Pallas kernels, norm_and_tile(): pl.pallas_call(functools.partial(norm_kernel, parts), in_specs=[pl.BlockS...  3.58 us
    ppermute x6, waiting for transfers between devices, moved(): return lax.ppermute(array, ('rows', 'cols'), pairs)  2.45 us
    pallas_call x1, Pallas kernels, project(): pl.pallas_call(functools.partial(project_kernel, len(parts)), in_specs=[v...  1.71 us
    ppermute x1, starting transfers between devices, shards(): others.append(lax.ppermute(normed[2], 'cols', swap))  1.47 us
    pallas_call x1, Pallas kernels, assemble(): pl.pallas_call(assemble_kernel, in_specs=[smem, vmem, vmem, vmem], out_sp...  1.37 us
  transfers between devices with their start and end apart: 9, of which 2 were waited for; matrix products, arithmetic and copies ran while one was open for 3% of the time, Pallas kernels for 32%

profile of v5, /device:TPU:0, one launch (start us, length us, event | category | flops | bytes accessed | tf_op | source)
XLA Modules:
  0.0 43.5 jit_solution(6900246922972466537)
XLA Ops:
  0.0 0.0 copy-start.6
  0.0 0.0 copy-start.7
  0.0 3.6 %norm_and_tile.1 = (bf16[8,192,128]{2,1,0:T(8,128)(2,1)}, bf16[8,192,128]{2,1,0:T(8,128)(2,1)}, bf16[8,192,128]{2,1,0:T(8,128)(2,1)}, bf16[192,128]{1,0:T(8,128)(2,1)}) custom-call(bf16[24,192,128]{2,1,0:T(8,128)(2,1)} %pair_hbm.1, f32[1,128]{1,0:T(1,128)} %bitcast.27, f32[1,128]{1,0:T(1,128)} %bitcast.28, bf16[4,128]{1,0:T(4,128)(2,1)} %bitcast.25, ...), custom_call_target="tpu_custom_call" | custom-call | flops 1000000000 | bytes 10000000 | tf_op jit(solution)/shard_map/norm_and_tile/pallas_call | solution.py:86
  3.6 0.0 copy-start
  3.6 0.0 copy-start.1
  3.6 0.0 copy-start.2
  3.6 4.1 %collective-permute-start.4 = (bf16[192,128]{1,0:T(8,128)(2,1)}, bf16[192,128]{1,0:T(8,128)(2,1)S(1)}, u32[]{:S(2)}, u32[]{:S(2)}) collective-permute-start(bf16[192,128]{1,0:T(8,128)(2,1)} %get-tuple-element.32), channel_id=1, source_target_pairs={{0,16},{1,0},{2,18},{3,2},{4,20},{5,4},{6,22},{7,6},{8,24},{9,8},{... | collective-permute-start | bytes 147464 | tf_op jit(solution)/shard_map/ppermute | solution.py:376
  7.7 0.7 %collective-permute-start.2 = (bf16[192,128]{1,0:T(8,128)(2,1)}, bf16[192,128]{1,0:T(8,128)(2,1)S(1)}, u32[]{:S(2)}, u32[]{:S(2)}) collective-permute-start(bf16[192,128]{1,0:T(8,128)(2,1)} %get-tuple-element.32), channel_id=1, source_target_pairs={{1,16},{3,18},{5,20},{7,22},{9,24},{11,26},{13,28},{15,30},{16,1},... | collective-permute-start | bytes 147464 | tf_op jit(solution)/shard_map/ppermute | solution.py:376
  8.4 4.3 %collective-permute-start = (bf16[8,192,128]{2,1,0:T(8,128)(2,1)}, bf16[8,192,128]{2,1,0:T(8,128)(2,1)S(1)}, u32[]{:S(2)}, u32[]{:S(2)}) collective-permute-start(bf16[8,192,128]{2,1,0:T(8,128)(2,1)} %get-tuple-element.29.refs_0_), channel_id=1, source_target_pairs={{0,1},{1,0},{2,3},{3,2},{4,5},{5,4},{6,7},{7,6},{8,9},{9,8},{10,11... | collective-permute-start | bytes 1179656 | tf_op jit(solution)/shard_map/ppermute | solution.py:504
  12.6 0.0 copy-done.6
  12.7 0.1 copy.18
  12.8 0.1 copy.19
  12.9 0.0 collective-permute-done.2
  12.9 0.0 collective-permute-done.4
  13.0 0.8 %constant_dynamic-update-slice_fusion.4 = (bf16[8,192,128]{2,1,0:T(8,128)(2,1)S(1)}, bf16[1,192,128]{2,1,0:T(8,128)(2,1)S(1)}) fusion(bf16[192,128]{1,0:T(8,128)(2,1)} %get-tuple-element.32, bf16[192,128]{1,0:T(8,128)(2,1)S(1)} %collective-permute-done.4, pred[]{:T(512)S(6)} %eq.3), kind=kLoop, calls=%fused_computation.8 | loop fusion | flops 24575 | bytes 196609
  13.8 1.6 %collective-permute-start.5 = (bf16[2,192,128]{2,1,0:T(8,128)(2,1)S(1)}, bf16[2,192,128]{2,1,0:T(8,128)(2,1)S(1)}, u32[]{:S(2)}, u32[]{:S(2)}) collective-permute-start(bf16[2,192,128]{2,1,0:T(8,128)(2,1)S(1)} %pad_maximum_fusion), channel_id=1, source_target_pairs={{0,4},{1,5},{2,6},{3,7},{4,0},{5,1},{6,2},{7,3},{8,12},{9,13},{10,... | collective-permute-start | bytes 294920 | tf_op jit(solution)/shard_map/ppermute | solution.py:376
  15.4 0.0 copy-done.7
  15.4 0.1 copy.16.refs_6_
  15.5 0.1 copy.17
  15.7 0.0 copy-done
  15.7 0.0 copy-done.1
  15.7 0.0 copy-done.2
  15.7 1.7 %project_own.1 = (bf16[24,192,128]{2,1,0:T(8,128)(2,1)S(1)}, bf16[24,128,192]{2,1,0:T(8,128)(2,1)S(1)}, bf16[24,128,256]{2,1,0:T(8,128)(2,1)S(1)}, f32[24,128,256]{2,1,0:T(8,128)S(1)}) custom-call(bf16[8,192,128]{2,1,0:T(8,128)(2,1)S(1)} %copy-done.2, bf16[8,192,128]{2,1,0:T(8,128)(2,1)S(1)} %copy-done.1, bf16[8,192,128]{2,1,0:T(8,128)(2,1)S(1)} %copy-done, ...), custom_call_target="tpu_custom_call" | custom-call | flops 1 | bytes 10 | tf_op jit(solution)/shard_map/project_own/pallas_call | solution.py:176
  17.4 1.6 %collective-permute-start.7 = (bf16[2,192,128]{2,1,0:T(8,128)(2,1)S(1)}, bf16[2,192,128]{2,1,0:T(8,128)(2,1)S(1)}, u32[]{:S(2)}, u32[]{:S(2)}) collective-permute-start(bf16[2,192,128]{2,1,0:T(8,128)(2,1)S(1)} %pad_maximum_fusion), channel_id=1, source_target_pairs={{0,12},{1,13},{2,14},{3,15},{4,8},{5,9},{6,10},{7,11},{8,4},{9,5},... | collective-permute-start | bytes 294920 | tf_op jit(solution)/shard_map/ppermute | solution.py:376
  19.0 0.4 %collective-permute-start.6 = (bf16[2,192,128]{2,1,0:T(8,128)(2,1)S(1)}, bf16[2,192,128]{2,1,0:T(8,128)(2,1)S(1)}, u32[]{:S(2)}, u32[]{:S(2)}) collective-permute-start(bf16[2,192,128]{2,1,0:T(8,128)(2,1)S(1)} %pad_maximum_fusion), channel_id=1, source_target_pairs={{0,8},{1,9},{2,10},{3,11},{4,12},{5,13},{6,14},{7,15},{8,0},{9,1},... | collective-permute-start | bytes 294920 | tf_op jit(solution)/shard_map/ppermute | solution.py:376
  19.5 1.7 %collective-permute-start.3 = (bf16[8,192,128]{2,1,0:T(8,128)(2,1)S(1)}, bf16[8,192,128]{2,1,0:T(8,128)(2,1)S(1)}, u32[]{:S(2)}, u32[]{:S(2)}) collective-permute-start(bf16[8,192,128]{2,1,0:T(8,128)(2,1)S(1)} %copy-done.1), channel_id=1, source_target_pairs={{0,1},{1,0},{2,3},{3,2},{4,5},{5,4},{6,7},{7,6},{8,9},{9,8},{10,11... | collective-permute-start | bytes 1179656 | tf_op jit(solution)/shard_map/ppermute | solution.py:504
  21.2 0.0 collective-permute-done.5
  21.2 2.4 %collective-permute-done.6 = bf16[2,192,128]{2,1,0:T(8,128)(2,1)S(1)} collective-permute-done((bf16[2,192,128]{2,1,0:T(8,128)(2,1)S(1)}, bf16[2,192,128]{2,1,0:T(8,128)(2,1)S(1)}, u32[]{:S(2)}, u32[]{:S(2)}) %collective-permute-start.6) | collective-permute-done | bytes 98336 | tf_op jit(solution)/shard_map/ppermute | solution.py:376
  23.6 0.0 collective-permute-done.7
  23.7 0.0 copy-start.5
  23.7 0.1 collective-permute-start.8
  23.8 0.0 collective-permute-done.other_ref
  23.8 0.5 %widen_rows.1 = (bf16[8,192,128]{2,1,0:T(8,128)(2,1)S(1)}, bf16[8,128,192]{2,1,0:T(8,128)(2,1)S(1)}) custom-call(bf16[8,192,128]{2,1,0:T(8,128)(2,1)S(1)} %collective-permute-done.other_ref, bf16[128,128]{1,0:T(8,128)(2,1)S(1)} %get-tuple-element.57.wk_ref.refs_3_.refs_2_, bf16[128,128]{1,0:T(8,128)(2,1)S(1)} %bitcast.16), custom_call_target="tpu_custom_call" | custom-call | flops 10000000000 | bytes 10 | tf_op jit(solution)/shard_map/widen_rows/pallas_call | solution.py:198
  24.3 0.0 copy-start.3
  24.3 0.0 copy-start.4
  24.3 1.5 %collective-permute-start.1 = (bf16[8,192,128]{2,1,0:T(8,128)(2,1)S(1)}, bf16[8,192,128]{2,1,0:T(8,128)(2,1)S(1)}, u32[]{:S(2)}, u32[]{:S(2)}) collective-permute-start(bf16[8,192,128]{2,1,0:T(8,128)(2,1)S(1)} %copy-done), channel_id=1, source_target_pairs={{0,1},{1,0},{2,3},{3,2},{4,5},{5,4},{6,7},{7,6},{8,9},{9,8},{10,11... | collective-permute-start | bytes 1179656 | tf_op jit(solution)/shard_map/ppermute | solution.py:507
  25.8 0.0 collective-permute-done.8.far_ref
  25.8 0.0 copy-done.5
  25.8 1.4 %assemble_bias.1.refs_6_.refs_8_ = f32[392,768]{1,0:T(8,128)S(1)} custom-call(s32[16]{0:T(128)S(1)} %shift-right-arithmetic_add_fusion.index_ref, bf16[8,192,128]{2,1,0:T(8,128)(2,1)S(1)} %constant_dynamic-update-slice_fusion.near_ref, bf16[8,192,128]{2,1,0:T(8,128)(2,1)S(1)} %collective-permute-done.8.far_ref, bf16[1024,768]{1,0:T(8,128)(2,1)S(1)} %copy-done.5), custom_call_target="tpu_custom_call" | custom-call | flops 1000000000 | bytes 4000000 | tf_op jit(solution)/shard_map/assemble_bias/pallas_call | solution.py:138
  27.1 0.0 copy-done.3
  27.1 0.0 copy-done.4
  27.2 5.0 %attend_rows.3.refs_0_ = bf16[24,192,128]{2,1,0:T(8,128)(2,1)} custom-call(bf16[8,192,128]{2,1,0:T(8,128)(2,1)S(1)} %get-tuple-element.35.refs_0_, bf16[8,128,192]{2,1,0:T(8,128)(2,1)S(1)} %get-tuple-element.36.refs_1_, bf16[24,192,128]{2,1,0:T(8,128)(2,1)S(1)} %get-tuple-element.42.refs_2_.refs_4_, ...), custom_call_target="tpu_custom_call" | custom-call | flops 10000000000 | bytes 10 | tf_op jit(solution)/shard_map/attend_rows/pallas_call | solution.py:347
  32.2 0.0 collective-permute-done.3.refs_1_
  32.2 5.4 %attend_rows.4.refs_0_ = bf16[24,192,128]{2,1,0:T(8,128)(2,1)} custom-call(bf16[24,192,128]{2,1,0:T(8,128)(2,1)} %attend_rows.3.refs_0_, bf16[8,192,128]{2,1,0:T(8,128)(2,1)S(1)} %collective-permute-done.3.refs_1_, bf16[128,128]{1,0:T(8,128)(2,1)S(1)} %get-tuple-element.57.wk_ref.refs_3_.refs_2_, ...), custom_call_target="tpu_custom_call", output_to_operand_aliasing={{}: (0, {})} | custom-call | flops 10000000000 | bytes 10 | tf_op jit(solution)/shard_map/attend_rows/pallas_call | solution.py:347
  37.6 0.6 %collective-permute-done.1.refs_1_ = bf16[8,192,128]{2,1,0:T(8,128)(2,1)S(1)} collective-permute-done((bf16[8,192,128]{2,1,0:T(8,128)(2,1)S(1)}, bf16[8,192,128]{2,1,0:T(8,128)(2,1)S(1)}, u32[]{:S(2)}, u32[]{:S(2)}) %collective-permute-start.1) | collective-permute-done | bytes 393248 | tf_op jit(solution)/shard_map/ppermute | solution.py:507
  38.3 5.2 %attend_rows.5 = bf16[24,192,128]{2,1,0:T(8,128)(2,1)} custom-call(bf16[24,192,128]{2,1,0:T(8,128)(2,1)} %attend_rows.4.refs_0_, bf16[8,192,128]{2,1,0:T(8,128)(2,1)S(1)} %collective-permute-done.1.refs_1_, bf16[128,128]{1,0:T(8,128)(2,1)S(1)} %get-tuple-element.57.wk_ref.refs_3_.refs_2_, ...), custom_call_target="tpu_custom_call", output_to_operand_aliasing={{}: (0, {})} | custom-call | flops 10000000000 | bytes 10 | tf_op jit(solution)/shard_map/attend_rows/pallas_call | solution.py:347
  (8 shorter events, 0.1 us)
Async XLA Ops:
  0.0 12.6 %copy-start.6 = (bf16[128,512]{1,0:T(8,128)(2,1)S(1)}, bf16[128,512]{1,0:T(8,128)(2,1)}, u32[]{:S(2)}) copy-start(bf16[128,512]{1,0:T(8,128)(2,1)} %param.14) | copy-start | bytes 393220
  0.0 15.4 %copy-start.7 = (f32[128]{0:T(128)S(1)}, f32[128]{0:T(128)}, u32[]{:S(2)}) copy-start(f32[128]{0:T(128)} %param.15) | copy-start | bytes 1540
  3.6 12.1 %copy-start = (bf16[8,192,128]{2,1,0:T(8,128)(2,1)S(1)}, bf16[8,192,128]{2,1,0:T(8,128)(2,1)}, u32[]{:S(2)}) copy-start(bf16[8,192,128]{2,1,0:T(8,128)(2,1)} %get-tuple-element.31.refs_2_) | copy-start | bytes 1179652
  3.6 12.1 %copy-start.1 = (bf16[8,192,128]{2,1,0:T(8,128)(2,1)S(1)}, bf16[8,192,128]{2,1,0:T(8,128)(2,1)}, u32[]{:S(2)}) copy-start(bf16[8,192,128]{2,1,0:T(8,128)(2,1)} %get-tuple-element.34.refs_1_) | copy-start | bytes 1179652
  3.6 12.1 %copy-start.2 = (bf16[8,192,128]{2,1,0:T(8,128)(2,1)S(1)}, bf16[8,192,128]{2,1,0:T(8,128)(2,1)}, u32[]{:S(2)}) copy-start(bf16[8,192,128]{2,1,0:T(8,128)(2,1)} %get-tuple-element.29.refs_0_) | copy-start | bytes 1179652
  3.6 9.3 %collective-permute-start.4 = (bf16[192,128]{1,0:T(8,128)(2,1)}, bf16[192,128]{1,0:T(8,128)(2,1)S(1)}, u32[]{:S(2)}, u32[]{:S(2)}) collective-permute-start(bf16[192,128]{1,0:T(8,128)(2,1)} %get-tuple-element.32), channel_id=1, source_target_pairs={{0,16},{1,0},{2,18},{3,2},{4,20},{5,4},{6,22},{7,6},{8,24},{9,8},{... | collective-permute-start | bytes 147464 | tf_op jit(solution)/shard_map/ppermute | solution.py:376
  7.7 5.2 %collective-permute-start.2 = (bf16[192,128]{1,0:T(8,128)(2,1)}, bf16[192,128]{1,0:T(8,128)(2,1)S(1)}, u32[]{:S(2)}, u32[]{:S(2)}) collective-permute-start(bf16[192,128]{1,0:T(8,128)(2,1)} %get-tuple-element.32), channel_id=1, source_target_pairs={{1,16},{3,18},{5,20},{7,22},{9,24},{11,26},{13,28},{15,30},{16,1},... | collective-permute-start | bytes 147464 | tf_op jit(solution)/shard_map/ppermute | solution.py:376
  8.4 15.4 %collective-permute-start = (bf16[8,192,128]{2,1,0:T(8,128)(2,1)}, bf16[8,192,128]{2,1,0:T(8,128)(2,1)S(1)}, u32[]{:S(2)}, u32[]{:S(2)}) collective-permute-start(bf16[8,192,128]{2,1,0:T(8,128)(2,1)} %get-tuple-element.29.refs_0_), channel_id=1, source_target_pairs={{0,1},{1,0},{2,3},{3,2},{4,5},{5,4},{6,7},{7,6},{8,9},{9,8},{10,11... | collective-permute-start | bytes 1179656 | tf_op jit(solution)/shard_map/ppermute | solution.py:504
  13.8 7.3 %collective-permute-start.5 = (bf16[2,192,128]{2,1,0:T(8,128)(2,1)S(1)}, bf16[2,192,128]{2,1,0:T(8,128)(2,1)S(1)}, u32[]{:S(2)}, u32[]{:S(2)}) collective-permute-start(bf16[2,192,128]{2,1,0:T(8,128)(2,1)S(1)} %pad_maximum_fusion), channel_id=1, source_target_pairs={{0,4},{1,5},{2,6},{3,7},{4,0},{5,1},{6,2},{7,3},{8,12},{9,13},{10,... | collective-permute-start | bytes 294920 | tf_op jit(solution)/shard_map/ppermute | solution.py:376
  17.4 6.2 %collective-permute-start.7 = (bf16[2,192,128]{2,1,0:T(8,128)(2,1)S(1)}, bf16[2,192,128]{2,1,0:T(8,128)(2,1)S(1)}, u32[]{:S(2)}, u32[]{:S(2)}) collective-permute-start(bf16[2,192,128]{2,1,0:T(8,128)(2,1)S(1)} %pad_maximum_fusion), channel_id=1, source_target_pairs={{0,12},{1,13},{2,14},{3,15},{4,8},{5,9},{6,10},{7,11},{8,4},{9,5},... | collective-permute-start | bytes 294920 | tf_op jit(solution)/shard_map/ppermute | solution.py:376
  19.0 4.6 %collective-permute-start.6 = (bf16[2,192,128]{2,1,0:T(8,128)(2,1)S(1)}, bf16[2,192,128]{2,1,0:T(8,128)(2,1)S(1)}, u32[]{:S(2)}, u32[]{:S(2)}) collective-permute-start(bf16[2,192,128]{2,1,0:T(8,128)(2,1)S(1)} %pad_maximum_fusion), channel_id=1, source_target_pairs={{0,8},{1,9},{2,10},{3,11},{4,12},{5,13},{6,14},{7,15},{8,0},{9,1},... | collective-permute-start | bytes 294920 | tf_op jit(solution)/shard_map/ppermute | solution.py:376
  19.5 12.7 %collective-permute-start.3 = (bf16[8,192,128]{2,1,0:T(8,128)(2,1)S(1)}, bf16[8,192,128]{2,1,0:T(8,128)(2,1)S(1)}, u32[]{:S(2)}, u32[]{:S(2)}) collective-permute-start(bf16[8,192,128]{2,1,0:T(8,128)(2,1)S(1)} %copy-done.1), channel_id=1, source_target_pairs={{0,1},{1,0},{2,3},{3,2},{4,5},{5,4},{6,7},{7,6},{8,9},{9,8},{10,11... | collective-permute-start | bytes 1179656 | tf_op jit(solution)/shard_map/ppermute | solution.py:504
  23.7 2.1 %copy-start.5 = (bf16[1024,768]{1,0:T(8,128)(2,1)S(1)}, bf16[1024,768]{1,0:T(8,128)(2,1)}, u32[]{:S(2)}) copy-start(bf16[1024,768]{1,0:T(8,128)(2,1)} %constant.7.clone.order_ref) | copy-start | bytes 4718596
  23.7 2.1 %collective-permute-start.8 = (bf16[8,192,128]{2,1,0:T(8,128)(2,1)S(1)}, bf16[8,192,128]{2,1,0:T(8,128)(2,1)S(1)}, u32[]{:S(2)}, u32[]{:S(2)}) collective-permute-start(bf16[8,192,128]{2,1,0:T(8,128)(2,1)S(1)} %constant_dynamic-update-slice_fusion.near_ref), channel_id=1, source_target_pairs={{0,2},{1,3},{2,0},{3,1},{4,6},{5,7},{6,4},{7,5},{8,10},{9,11},{10,... | collective-permute-start | bytes 1179656 | tf_op jit(solution)/shard_map/ppermute | solution.py:376
  24.3 2.9 %copy-start.3 = (bf16[128,128]{1,0:T(8,128)(2,1)S(1)}, bf16[128,128]{1,0:T(8,128)(2,1)}, u32[]{:S(2)}) copy-start(bf16[128,128]{1,0:T(8,128)(2,1)} %refs_9_.3) | copy-start | bytes 98308
  24.3 2.9 %copy-start.4 = (f32[128]{0:T(128)S(1)}, f32[128]{0:T(128)}, u32[]{:S(2)}) copy-start(f32[128]{0:T(128)} %param.18) | copy-start | bytes 1540
  24.3 14.0 %collective-permute-start.1 = (bf16[8,192,128]{2,1,0:T(8,128)(2,1)S(1)}, bf16[8,192,128]{2,1,0:T(8,128)(2,1)S(1)}, u32[]{:S(2)}, u32[]{:S(2)}) collective-permute-start(bf16[8,192,128]{2,1,0:T(8,128)(2,1)S(1)} %copy-done), channel_id=1, source_target_pairs={{0,1},{1,0},{2,3},{3,2},{4,5},{5,4},{6,7},{7,6},{8,9},{9,8},{10,11... | collective-permute-start | bytes 1179656 | tf_op jit(solution)/shard_map/ppermute | solution.py:507

commit v6 on v5

--- a/solution.py
+++ b/solution.py
@@ -321,6 +321,7 @@
                 stages.append(score(*units[step], step % 2, False))
                 if units[step][1] == 0 and units[step][0] + 1 < rows:
                     stages.append(widen(units[step][0] + 1))
+            stages = stages[::-1]
             run(*stages)
 
     @pl.when(present <= 0.5)

time: 43.7 us -> 43.8 us (level)
  no operation moved by 1% of the time
where the time goes in v6:
time: 43.8 us; the launch traced here: 43.6 us
  Pallas kernels  23 us (53%)
  starting transfers between devices  15.9 us (36%)
  waiting for transfers between devices  2.99 us (7%)
  other arithmetic  0.89 us (2%)
  local copies, waits for them, and re-layouts  0.56 us (1%)
    pallas_call x3, Pallas kernels, attend(): pl.pallas_call(functools.partial(attend_kernel, begin, first), grid=(1,),...  15.9 us
    ppermute x6, starting transfers between devices, moved(): return lax.ppermute(array, ('rows', 'cols'), pairs)  8.43 us
    ppermute x2, starting transfers between devices, shards(): others = [lax.ppermute(part, 'cols', swap) for part in normed[:2]]  5.98 us
    pallas_call x1, Pallas kernels, norm_and_tile(): pl.pallas_call(functools.partial(norm_kernel, parts), in_specs=[pl.BlockS...  3.58 us
    ppermute x6, waiting for transfers between devices, moved(): return lax.ppermute(array, ('rows', 'cols'), pairs)  2.45 us
    pallas_call x1, Pallas kernels, project(): pl.pallas_call(functools.partial(project_kernel, len(parts)), in_specs=[v...  1.71 us
    ppermute x1, starting transfers between devices, shards(): others.append(lax.ppermute(normed[2], 'cols', swap))  1.47 us
    pallas_call x1, Pallas kernels, assemble(): pl.pallas_call(assemble_kernel, in_specs=[smem, vmem, vmem, vmem], out_sp...  1.37 us
  transfers between devices with their start and end apart: 9, of which 2 were waited for; matrix products, arithmetic and copies ran while one was open for 3% of the time, Pallas kernels for 32%

profile of v6, /device:TPU:0, one launch (start us, length us, event | category | flops | bytes accessed | tf_op | source)
XLA Modules:
  0.0 43.6 jit_solution(10764181828903229677)
XLA Ops:
  0.0 0.0 copy-start.6
  0.0 0.0 copy-start.7
  0.0 3.6 %norm_and_tile.1 = (bf16[8,192,128]{2,1,0:T(8,128)(2,1)}, bf16[8,192,128]{2,1,0:T(8,128)(2,1)}, bf16[8,192,128]{2,1,0:T(8,128)(2,1)}, bf16[192,128]{1,0:T(8,128)(2,1)}) custom-call(bf16[24,192,128]{2,1,0:T(8,128)(2,1)} %pair_hbm.1, f32[1,128]{1,0:T(1,128)} %bitcast.27, f32[1,128]{1,0:T(1,128)} %bitcast.28, bf16[4,128]{1,0:T(4,128)(2,1)} %bitcast.25, ...), custom_call_target="tpu_custom_call" | custom-call | flops 1000000000 | bytes 10000000 | tf_op jit(solution)/shard_map/norm_and_tile/pallas_call | solution.py:86
  3.6 0.0 copy-start
  3.6 0.0 copy-start.1
  3.6 0.0 copy-start.2
  3.6 4.1 %collective-permute-start.4 = (bf16[192,128]{1,0:T(8,128)(2,1)}, bf16[192,128]{1,0:T(8,128)(2,1)S(1)}, u32[]{:S(2)}, u32[]{:S(2)}) collective-permute-start(bf16[192,128]{1,0:T(8,128)(2,1)} %get-tuple-element.32), channel_id=1, source_target_pairs={{0,16},{1,0},{2,18},{3,2},{4,20},{5,4},{6,22},{7,6},{8,24},{9,8},{... | collective-permute-start | bytes 147464 | tf_op jit(solution)/shard_map/ppermute | solution.py:377
  7.7 0.7 %collective-permute-start.2 = (bf16[192,128]{1,0:T(8,128)(2,1)}, bf16[192,128]{1,0:T(8,128)(2,1)S(1)}, u32[]{:S(2)}, u32[]{:S(2)}) collective-permute-start(bf16[192,128]{1,0:T(8,128)(2,1)} %get-tuple-element.32), channel_id=1, source_target_pairs={{1,16},{3,18},{5,20},{7,22},{9,24},{11,26},{13,28},{15,30},{16,1},... | collective-permute-start | bytes 147464 | tf_op jit(solution)/shard_map/ppermute | solution.py:377
  8.4 4.3 %collective-permute-start = (bf16[8,192,128]{2,1,0:T(8,128)(2,1)}, bf16[8,192,128]{2,1,0:T(8,128)(2,1)S(1)}, u32[]{:S(2)}, u32[]{:S(2)}) collective-permute-start(bf16[8,192,128]{2,1,0:T(8,128)(2,1)} %get-tuple-element.29.refs_0_), channel_id=1, source_target_pairs={{0,1},{1,0},{2,3},{3,2},{4,5},{5,4},{6,7},{7,6},{8,9},{9,8},{10,11... | collective-permute-start | bytes 1179656 | tf_op jit(solution)/shard_map/ppermute | solution.py:505
  12.6 0.0 copy-done.6
  12.7 0.1 copy.18
  12.8 0.1 copy.19
  12.9 0.0 collective-permute-done.2
  12.9 0.0 collective-permute-done.4
  13.0 0.8 %constant_dynamic-update-slice_fusion.4 = (bf16[8,192,128]{2,1,0:T(8,128)(2,1)S(1)}, bf16[1,192,128]{2,1,0:T(8,128)(2,1)S(1)}) fusion(bf16[192,128]{1,0:T(8,128)(2,1)} %get-tuple-element.32, bf16[192,128]{1,0:T(8,128)(2,1)S(1)} %collective-permute-done.4, pred[]{:T(512)S(6)} %eq.3), kind=kLoop, calls=%fused_computation.8 | loop fusion | flops 24575 | bytes 196609
  13.8 1.6 %collective-permute-start.5 = (bf16[2,192,128]{2,1,0:T(8,128)(2,1)S(1)}, bf16[2,192,128]{2,1,0:T(8,128)(2,1)S(1)}, u32[]{:S(2)}, u32[]{:S(2)}) collective-permute-start(bf16[2,192,128]{2,1,0:T(8,128)(2,1)S(1)} %pad_maximum_fusion), channel_id=1, source_target_pairs={{0,4},{1,5},{2,6},{3,7},{4,0},{5,1},{6,2},{7,3},{8,12},{9,13},{10,... | collective-permute-start | bytes 294920 | tf_op jit(solution)/shard_map/ppermute | solution.py:377
  15.4 0.0 copy-done.7
  15.4 0.1 copy.16.refs_6_
  15.5 0.1 copy.17
  15.7 0.0 copy-done
  15.7 0.0 copy-done.1
  15.7 0.0 copy-done.2
  15.7 1.7 %project_own.1 = (bf16[24,192,128]{2,1,0:T(8,128)(2,1)S(1)}, bf16[24,128,192]{2,1,0:T(8,128)(2,1)S(1)}, bf16[24,128,256]{2,1,0:T(8,128)(2,1)S(1)}, f32[24,128,256]{2,1,0:T(8,128)S(1)}) custom-call(bf16[8,192,128]{2,1,0:T(8,128)(2,1)S(1)} %copy-done.2, bf16[8,192,128]{2,1,0:T(8,128)(2,1)S(1)} %copy-done.1, bf16[8,192,128]{2,1,0:T(8,128)(2,1)S(1)} %copy-done, ...), custom_call_target="tpu_custom_call" | custom-call | flops 1 | bytes 10 | tf_op jit(solution)/shard_map/project_own/pallas_call | solution.py:176
  17.4 1.6 %collective-permute-start.7 = (bf16[2,192,128]{2,1,0:T(8,128)(2,1)S(1)}, bf16[2,192,128]{2,1,0:T(8,128)(2,1)S(1)}, u32[]{:S(2)}, u32[]{:S(2)}) collective-permute-start(bf16[2,192,128]{2,1,0:T(8,128)(2,1)S(1)} %pad_maximum_fusion), channel_id=1, source_target_pairs={{0,12},{1,13},{2,14},{3,15},{4,8},{5,9},{6,10},{7,11},{8,4},{9,5},... | collective-permute-start | bytes 294920 | tf_op jit(solution)/shard_map/ppermute | solution.py:377
  19.0 0.4 %collective-permute-start.6 = (bf16[2,192,128]{2,1,0:T(8,128)(2,1)S(1)}, bf16[2,192,128]{2,1,0:T(8,128)(2,1)S(1)}, u32[]{:S(2)}, u32[]{:S(2)}) collective-permute-start(bf16[2,192,128]{2,1,0:T(8,128)(2,1)S(1)} %pad_maximum_fusion), channel_id=1, source_target_pairs={{0,8},{1,9},{2,10},{3,11},{4,12},{5,13},{6,14},{7,15},{8,0},{9,1},... | collective-permute-start | bytes 294920 | tf_op jit(solution)/shard_map/ppermute | solution.py:377
  19.5 1.7 %collective-permute-start.3 = (bf16[8,192,128]{2,1,0:T(8,128)(2,1)S(1)}, bf16[8,192,128]{2,1,0:T(8,128)(2,1)S(1)}, u32[]{:S(2)}, u32[]{:S(2)}) collective-permute-start(bf16[8,192,128]{2,1,0:T(8,128)(2,1)S(1)} %copy-done.1), channel_id=1, source_target_pairs={{0,1},{1,0},{2,3},{3,2},{4,5},{5,4},{6,7},{7,6},{8,9},{9,8},{10,11... | collective-permute-start | bytes 1179656 | tf_op jit(solution)/shard_map/ppermute | solution.py:505
  21.2 0.0 collective-permute-done.5
  21.2 2.4 %collective-permute-done.6 = bf16[2,192,128]{2,1,0:T(8,128)(2,1)S(1)} collective-permute-done((bf16[2,192,128]{2,1,0:T(8,128)(2,1)S(1)}, bf16[2,192,128]{2,1,0:T(8,128)(2,1)S(1)}, u32[]{:S(2)}, u32[]{:S(2)}) %collective-permute-start.6) | collective-permute-done | bytes 98336 | tf_op jit(solution)/shard_map/ppermute | solution.py:377
  23.6 0.0 collective-permute-done.7
  23.7 0.0 copy-start.5
  23.7 0.1 collective-permute-start.8
  23.8 0.0 collective-permute-done.other_ref
  23.8 0.5 %widen_rows.1 = (bf16[8,192,128]{2,1,0:T(8,128)(2,1)S(1)}, bf16[8,128,192]{2,1,0:T(8,128)(2,1)S(1)}) custom-call(bf16[8,192,128]{2,1,0:T(8,128)(2,1)S(1)} %collective-permute-done.other_ref, bf16[128,128]{1,0:T(8,128)(2,1)S(1)} %get-tuple-element.57.wk_ref.refs_3_.refs_2_, bf16[128,128]{1,0:T(8,128)(2,1)S(1)} %bitcast.16), custom_call_target="tpu_custom_call" | custom-call | flops 10000000000 | bytes 10 | tf_op jit(solution)/shard_map/widen_rows/pallas_call | solution.py:198
  24.3 0.0 copy-start.3
  24.3 0.0 copy-start.4
  24.3 1.5 %collective-permute-start.1 = (bf16[8,192,128]{2,1,0:T(8,128)(2,1)S(1)}, bf16[8,192,128]{2,1,0:T(8,128)(2,1)S(1)}, u32[]{:S(2)}, u32[]{:S(2)}) collective-permute-start(bf16[8,192,128]{2,1,0:T(8,128)(2,1)S(1)} %copy-done), channel_id=1, source_target_pairs={{0,1},{1,0},{2,3},{3,2},{4,5},{5,4},{6,7},{7,6},{8,9},{9,8},{10,11... | collective-permute-start | bytes 1179656 | tf_op jit(solution)/shard_map/ppermute | solution.py:508
  25.8 0.0 collective-permute-done.8.far_ref
  25.8 0.0 copy-done.5
  25.8 1.4 %assemble_bias.1.refs_6_.refs_8_ = f32[392,768]{1,0:T(8,128)S(1)} custom-call(s32[16]{0:T(128)S(1)} %shift-right-arithmetic_add_fusion.index_ref, bf16[8,192,128]{2,1,0:T(8,128)(2,1)S(1)} %constant_dynamic-update-slice_fusion.near_ref, bf16[8,192,128]{2,1,0:T(8,128)(2,1)S(1)} %collective-permute-done.8.far_ref, bf16[1024,768]{1,0:T(8,128)(2,1)S(1)} %copy-done.5), custom_call_target="tpu_custom_call" | custom-call | flops 1000000000 | bytes 4000000 | tf_op jit(solution)/shard_map/assemble_bias/pallas_call | solution.py:138
  27.1 0.0 copy-done.3
  27.1 0.0 copy-done.4
  27.2 5.0 %attend_rows.3.refs_0_ = bf16[24,192,128]{2,1,0:T(8,128)(2,1)} custom-call(bf16[8,192,128]{2,1,0:T(8,128)(2,1)S(1)} %get-tuple-element.35.refs_0_, bf16[8,128,192]{2,1,0:T(8,128)(2,1)S(1)} %get-tuple-element.36.refs_1_, bf16[24,192,128]{2,1,0:T(8,128)(2,1)S(1)} %get-tuple-element.42.refs_2_.refs_4_, ...), custom_call_target="tpu_custom_call" | custom-call | flops 10000000000 | bytes 10 | tf_op jit(solution)/shard_map/attend_rows/pallas_call | solution.py:348
  32.2 0.0 collective-permute-done.3.refs_1_
  32.2 5.5 %attend_rows.4.refs_0_ = bf16[24,192,128]{2,1,0:T(8,128)(2,1)} custom-call(bf16[24,192,128]{2,1,0:T(8,128)(2,1)} %attend_rows.3.refs_0_, bf16[8,192,128]{2,1,0:T(8,128)(2,1)S(1)} %collective-permute-done.3.refs_1_, bf16[128,128]{1,0:T(8,128)(2,1)S(1)} %get-tuple-element.57.wk_ref.refs_3_.refs_2_, ...), custom_call_target="tpu_custom_call", output_to_operand_aliasing={{}: (0, {})} | custom-call | flops 10000000000 | bytes 10 | tf_op jit(solution)/shard_map/attend_rows/pallas_call | solution.py:348
  37.7 0.5 %collective-permute-done.1.refs_1_ = bf16[8,192,128]{2,1,0:T(8,128)(2,1)S(1)} collective-permute-done((bf16[8,192,128]{2,1,0:T(8,128)(2,1)S(1)}, bf16[8,192,128]{2,1,0:T(8,128)(2,1)S(1)}, u32[]{:S(2)}, u32[]{:S(2)}) %collective-permute-start.1) | collective-permute-done | bytes 393248 | tf_op jit(solution)/shard_map/ppermute | solution.py:508
  38.3 5.3 %attend_rows.5 = bf16[24,192,128]{2,1,0:T(8,128)(2,1)} custom-call(bf16[24,192,128]{2,1,0:T(8,128)(2,1)} %attend_rows.4.refs_0_, bf16[8,192,128]{2,1,0:T(8,128)(2,1)S(1)} %collective-permute-done.1.refs_1_, bf16[128,128]{1,0:T(8,128)(2,1)S(1)} %get-tuple-element.57.wk_ref.refs_3_.refs_2_, ...), custom_call_target="tpu_custom_call", output_to_operand_aliasing={{}: (0, {})} | custom-call | flops 10000000000 | bytes 10 | tf_op jit(solution)/shard_map/attend_rows/pallas_call | solution.py:348
  (8 shorter events, 0.1 us)
Async XLA Ops:
  0.0 12.6 %copy-start.6 = (bf16[128,512]{1,0:T(8,128)(2,1)S(1)}, bf16[128,512]{1,0:T(8,128)(2,1)}, u32[]{:S(2)}) copy-start(bf16[128,512]{1,0:T(8,128)(2,1)} %param.14) | copy-start | bytes 393220
  0.0 15.4 %copy-start.7 = (f32[128]{0:T(128)S(1)}, f32[128]{0:T(128)}, u32[]{:S(2)}) copy-start(f32[128]{0:T(128)} %param.15) | copy-start | bytes 1540
  3.6 12.1 %copy-start = (bf16[8,192,128]{2,1,0:T(8,128)(2,1)S(1)}, bf16[8,192,128]{2,1,0:T(8,128)(2,1)}, u32[]{:S(2)}) copy-start(bf16[8,192,128]{2,1,0:T(8,128)(2,1)} %get-tuple-element.31.refs_2_) | copy-start | bytes 1179652
  3.6 12.1 %copy-start.1 = (bf16[8,192,128]{2,1,0:T(8,128)(2,1)S(1)}, bf16[8,192,128]{2,1,0:T(8,128)(2,1)}, u32[]{:S(2)}) copy-start(bf16[8,192,128]{2,1,0:T(8,128)(2,1)} %get-tuple-element.34.refs_1_) | copy-start | bytes 1179652
  3.6 12.1 %copy-start.2 = (bf16[8,192,128]{2,1,0:T(8,128)(2,1)S(1)}, bf16[8,192,128]{2,1,0:T(8,128)(2,1)}, u32[]{:S(2)}) copy-start(bf16[8,192,128]{2,1,0:T(8,128)(2,1)} %get-tuple-element.29.refs_0_) | copy-start | bytes 1179652
  3.6 9.3 %collective-permute-start.4 = (bf16[192,128]{1,0:T(8,128)(2,1)}, bf16[192,128]{1,0:T(8,128)(2,1)S(1)}, u32[]{:S(2)}, u32[]{:S(2)}) collective-permute-start(bf16[192,128]{1,0:T(8,128)(2,1)} %get-tuple-element.32), channel_id=1, source_target_pairs={{0,16},{1,0},{2,18},{3,2},{4,20},{5,4},{6,22},{7,6},{8,24},{9,8},{... | collective-permute-start | bytes 147464 | tf_op jit(solution)/shard_map/ppermute | solution.py:377
  7.7 5.2 %collective-permute-start.2 = (bf16[192,128]{1,0:T(8,128)(2,1)}, bf16[192,128]{1,0:T(8,128)(2,1)S(1)}, u32[]{:S(2)}, u32[]{:S(2)}) collective-permute-start(bf16[192,128]{1,0:T(8,128)(2,1)} %get-tuple-element.32), channel_id=1, source_target_pairs={{1,16},{3,18},{5,20},{7,22},{9,24},{11,26},{13,28},{15,30},{16,1},... | collective-permute-start | bytes 147464 | tf_op jit(solution)/shard_map/ppermute | solution.py:377
  8.4 15.4 %collective-permute-start = (bf16[8,192,128]{2,1,0:T(8,128)(2,1)}, bf16[8,192,128]{2,1,0:T(8,128)(2,1)S(1)}, u32[]{:S(2)}, u32[]{:S(2)}) collective-permute-start(bf16[8,192,128]{2,1,0:T(8,128)(2,1)} %get-tuple-element.29.refs_0_), channel_id=1, source_target_pairs={{0,1},{1,0},{2,3},{3,2},{4,5},{5,4},{6,7},{7,6},{8,9},{9,8},{10,11... | collective-permute-start | bytes 1179656 | tf_op jit(solution)/shard_map/ppermute | solution.py:505
  13.8 7.3 %collective-permute-start.5 = (bf16[2,192,128]{2,1,0:T(8,128)(2,1)S(1)}, bf16[2,192,128]{2,1,0:T(8,128)(2,1)S(1)}, u32[]{:S(2)}, u32[]{:S(2)}) collective-permute-start(bf16[2,192,128]{2,1,0:T(8,128)(2,1)S(1)} %pad_maximum_fusion), channel_id=1, source_target_pairs={{0,4},{1,5},{2,6},{3,7},{4,0},{5,1},{6,2},{7,3},{8,12},{9,13},{10,... | collective-permute-start | bytes 294920 | tf_op jit(solution)/shard_map/ppermute | solution.py:377
  17.4 6.2 %collective-permute-start.7 = (bf16[2,192,128]{2,1,0:T(8,128)(2,1)S(1)}, bf16[2,192,128]{2,1,0:T(8,128)(2,1)S(1)}, u32[]{:S(2)}, u32[]{:S(2)}) collective-permute-start(bf16[2,192,128]{2,1,0:T(8,128)(2,1)S(1)} %pad_maximum_fusion), channel_id=1, source_target_pairs={{0,12},{1,13},{2,14},{3,15},{4,8},{5,9},{6,10},{7,11},{8,4},{9,5},... | collective-permute-start | bytes 294920 | tf_op jit(solution)/shard_map/ppermute | solution.py:377
  19.0 4.6 %collective-permute-start.6 = (bf16[2,192,128]{2,1,0:T(8,128)(2,1)S(1)}, bf16[2,192,128]{2,1,0:T(8,128)(2,1)S(1)}, u32[]{:S(2)}, u32[]{:S(2)}) collective-permute-start(bf16[2,192,128]{2,1,0:T(8,128)(2,1)S(1)} %pad_maximum_fusion), channel_id=1, source_target_pairs={{0,8},{1,9},{2,10},{3,11},{4,12},{5,13},{6,14},{7,15},{8,0},{9,1},... | collective-permute-start | bytes 294920 | tf_op jit(solution)/shard_map/ppermute | solution.py:377
  19.5 12.8 %collective-permute-start.3 = (bf16[8,192,128]{2,1,0:T(8,128)(2,1)S(1)}, bf16[8,192,128]{2,1,0:T(8,128)(2,1)S(1)}, u32[]{:S(2)}, u32[]{:S(2)}) collective-permute-start(bf16[8,192,128]{2,1,0:T(8,128)(2,1)S(1)} %copy-done.1), channel_id=1, source_target_pairs={{0,1},{1,0},{2,3},{3,2},{4,5},{5,4},{6,7},{7,6},{8,9},{9,8},{10,11... | collective-permute-start | bytes 1179656 | tf_op jit(solution)/shard_map/ppermute | solution.py:505
  23.7 2.1 %copy-start.5 = (bf16[1024,768]{1,0:T(8,128)(2,1)S(1)}, bf16[1024,768]{1,0:T(8,128)(2,1)}, u32[]{:S(2)}) copy-start(bf16[1024,768]{1,0:T(8,128)(2,1)} %constant.7.clone.order_ref) | copy-start | bytes 4718596
  23.7 2.1 %collective-permute-start.8 = (bf16[8,192,128]{2,1,0:T(8,128)(2,1)S(1)}, bf16[8,192,128]{2,1,0:T(8,128)(2,1)S(1)}, u32[]{:S(2)}, u32[]{:S(2)}) collective-permute-start(bf16[8,192,128]{2,1,0:T(8,128)(2,1)S(1)} %constant_dynamic-update-slice_fusion.near_ref), channel_id=1, source_target_pairs={{0,2},{1,3},{2,0},{3,1},{4,6},{5,7},{6,4},{7,5},{8,10},{9,11},{10,... | collective-permute-start | bytes 1179656 | tf_op jit(solution)/shard_map/ppermute | solution.py:377
  24.3 2.9 %copy-start.3 = (bf16[128,128]{1,0:T(8,128)(2,1)S(1)}, bf16[128,128]{1,0:T(8,128)(2,1)}, u32[]{:S(2)}) copy-start(bf16[128,128]{1,0:T(8,128)(2,1)} %refs_9_.3) | copy-start | bytes 98308
  24.3 2.9 %copy-start.4 = (f32[128]{0:T(128)S(1)}, f32[128]{0:T(128)}, u32[]{:S(2)}) copy-start(f32[128]{0:T(128)} %param.18) | copy-start | bytes 1540
  24.3 14.0 %collective-permute-start.1 = (bf16[8,192,128]{2,1,0:T(8,128)(2,1)S(1)}, bf16[8,192,128]{2,1,0:T(8,128)(2,1)S(1)}, u32[]{:S(2)}, u32[]{:S(2)}) collective-permute-start(bf16[8,192,128]{2,1,0:T(8,128)(2,1)S(1)} %copy-done), channel_id=1, source_target_pairs={{0,1},{1,0},{2,3},{3,2},{4,5},{5,4},{6,7},{7,6},{8,9},{9,8},{10,11... | collective-permute-start | bytes 1179656 | tf_op jit(solution)/shard_map/ppermute | solution.py:508
